TPU v7x, 256 devices: a whole 4x4x8 slice. The times are simulated.
256 devices in a mesh: inst: 32 (over y, x, core), space: 8 (over z).
Axes of the slice: x: 4, y: 4, z: 8, core: 2. Of those that a mesh axis runs over, the one named last changes fastest.
Arguments:
- harmonic_state: bfloat16 [32, 122880], P('inst', 'space'), may hold values from -6 to 6
- direction: bfloat16 [32, 122880], P('inst', 'space'), may hold values from -6 to 6
- source: float32 [32, 122880], P('inst', 'space'), may hold values from -6 to 6
- jacobian: bfloat16 [32, 384, 102400], P('inst', 'space'), may hold values from -0.3125 to 0.3125
- frequency: float32 [1], replicated, may hold values from 0.05 to 0.2
- viscosity: float32 [1], replicated, may hold values from 0.01 to 0.03
- quad_weight: float32 [16], replicated, may hold values from 0.3 to 3
- partner_device: int32 [32, 1536, 1], P('inst', 'space'), may hold values from 0 to 7; in each aligned block of 192 rows (0 to 191, 192 to 383, ..., all dimensions but the last counted through in order) at most 96 rows name the same one
- partner_face: int32 [32, 1536], P('inst', 'space'), may hold values from 0 to 287
- local_face: int32 [32, 1536], P('inst', 'space'), may hold values from 0 to 287
- weight_index: int32 [32, 1536], P('inst', 'space'), may hold values from 0 to 15
Outputs:
- residual: float32 [32, 122880], P('inst', 'space')
- product: float32 [32, 122880], P('inst', 'space')
Inputs may be any that keep to these rules, and one draw needn't show every extreme that they name: `partner_device`: within the 192 slots of one device, each partner device is named at most 96 times, and some device is named exactly 96 times in every draw.
All inputs are finite; a program needn't handle non-finite values.
Results may differ from a plain program's by a relative error of at most 0.00035.
Values may be sent and summed in bfloat16 or wider, within the bound.
No kernel may reach another device: no remote copies, remote signals or barrier semaphores. Data moves between devices by JAX's collectives and lax.ppermute only.
A program may use at most 64 MiB of HBM per device.

v0:
```python
import jax
import jax.numpy as jnp
import numpy as np
from jax import lax
from jax.sharding import PartitionSpec as P

VARS = 5
PNODE = 4
E_DEV = 48
DOF = 320
FACES_DEV = 288


def spectral_matrix(frequency, viscosity, length):
    indices = jnp.arange(length, dtype=jnp.int32)
    offsets = indices[:, None] - indices[None, :]
    on_diag = offsets == 0
    angles = jnp.where(on_diag, 0.5 * jnp.pi, jnp.pi * offsets.astype(jnp.float32) / length)
    parity = 1.0 - 2.0 * (jnp.abs(offsets) % 2).astype(jnp.float32)
    sine_values = jnp.sin(angles)
    first_order = jnp.where(on_diag, 0.0, 0.5 * parity * jnp.cos(angles) / sine_values)
    second = jnp.where(
        on_diag, -(length * length + 2) / 12.0, -parity / (2.0 * sine_values * sine_values)
    )
    return frequency[0] * first_order + viscosity[0] * second


def face_selector(variables, nodes):
    per_face = variables * nodes * nodes
    table = np.zeros((variables * nodes**3, 6 * per_face), np.float32)
    last_node = nodes - 1
    for face in range(6):
        fixed_value = 0 if face % 2 == 0 else last_node
        for comp in range(variables):
            for first in range(nodes):
                for second in range(nodes):
                    if face < 2:
                        node_i, node_j, node_k = (fixed_value, first, second)
                    elif face < 4:
                        node_i, node_j, node_k = (first, fixed_value, second)
                    else:
                        node_i, node_j, node_k = (first, second, fixed_value)
                    row_index = comp * nodes**3 + node_i * nodes * nodes + node_j * nodes + node_k
                    col_index = face * per_face + comp * nodes * nodes + first * nodes + second
                    table[row_index, col_index] = 1.0
    return table


def slot_weights(quad_weight, weight_index):
    classes = jnp.arange(quad_weight.shape[0], dtype=jnp.int32)
    return jnp.sum(
        jnp.where(weight_index[:, None] == classes[None, :], quad_weight[None, :], 0.0), axis=1
    )


def per_device(
    harmonic_state,
    direction,
    source,
    jacobian,
    frequency,
    viscosity,
    quad_weight,
    partner_device,
    partner_face,
    local_face,
    weight_index,
):
    length = lax.axis_size("inst")
    spectral = spectral_matrix(frequency, viscosity, length)
    state_flat = harmonic_state.reshape(E_DEV, DOF)
    direction_flat = direction.reshape(E_DEV, DOF)
    stacked_rows = jnp.stack([harmonic_state, direction], axis=1)
    row_weights = lax.dynamic_index_in_dim(spectral, lax.axis_index("inst"), 0, keepdims=False)
    time_terms = jnp.einsum(
        "s,skm->km",
        row_weights,
        lax.all_gather(stacked_rows, "inst", axis=0, tiled=True).astype(jnp.float32),
        precision=lax.Precision.HIGHEST,
    )
    matrices = jacobian.reshape(E_DEV, DOF, DOF)
    flat_fields = jnp.stack([state_flat, direction_flat], axis=1)
    element_terms = jnp.einsum(
        "eab,ekb->eka", matrices, flat_fields, preferred_element_type=jnp.float32
    )
    selector_f32 = jnp.asarray(face_selector(VARS, PNODE))
    selector = selector_f32.astype(jnp.bfloat16)
    per_face = VARS * PNODE * PNODE
    state_faces = (
        jnp.dot(state_flat, selector, preferred_element_type=jnp.float32)
        .astype(jnp.bfloat16)
        .reshape(FACES_DEV, per_face)
    )
    direction_faces = (
        jnp.dot(direction_flat, selector, preferred_element_type=jnp.float32)
        .astype(jnp.bfloat16)
        .reshape(FACES_DEV, per_face)
    )
    trace_table = jnp.concatenate([state_faces, direction_faces], axis=1)
    devices = partner_device.reshape(-1)
    far_faces = partner_face.reshape(-1)
    near_faces = local_face.reshape(-1)
    classes = weight_index.reshape(-1)
    targets = devices * FACES_DEV + far_faces
    shard_rows = lax.all_gather(trace_table, "space", axis=0, tiled=True)
    columns = jnp.arange(shard_rows.shape[0], dtype=jnp.int32)
    select = (targets[:, None] == columns[None, :]).astype(jnp.bfloat16)
    far_traces = jnp.dot(select, shard_rows, preferred_element_type=jnp.float32)
    near_select = near_faces[:, None] == jnp.arange(FACES_DEV, dtype=jnp.int32)[None, :]
    near_rows = jnp.dot(
        near_select.astype(jnp.bfloat16), trace_table, preferred_element_type=jnp.float32
    )
    weights = slot_weights(quad_weight, classes)
    slot_terms = weights[:, None] * (near_rows - far_traces)
    face_flux = lax.dot_general(
        near_select.astype(jnp.float32),
        slot_terms,
        (((0,), (0,)), ((), ())),
        precision=lax.Precision.HIGHEST,
    )
    state_flux = face_flux[:, :per_face].reshape(E_DEV, 6 * per_face)
    direction_flux = face_flux[:, per_face:].reshape(E_DEV, 6 * per_face)
    lifted_state = lax.dot_general(
        state_flux, selector_f32, (((1,), (1,)), ((), ())), precision=lax.Precision.HIGHEST
    )
    lifted_direction = lax.dot_general(
        direction_flux, selector_f32, (((1,), (1,)), ((), ())), precision=lax.Precision.HIGHEST
    )
    state_sum = element_terms[:, 0] + lifted_state
    direction_sum = element_terms[:, 1] + lifted_direction
    residual = source - (time_terms[0] + state_sum.reshape(-1)).reshape(1, -1)
    product = (time_terms[1] + direction_sum.reshape(-1)).reshape(1, -1)
    return (residual, product)


def solution(mesh):
    in_specs = (
        P("inst", "space"),
        P("inst", "space"),
        P("inst", "space"),
        P("inst", "space", None),
        P(),
        P(),
        P(),
        P("inst", "space", None),
        P("inst", "space"),
        P("inst", "space"),
        P("inst", "space"),
    )
    out_specs = (P("inst", "space"), P("inst", "space"))
    return jax.shard_map(
        per_device, mesh=mesh, in_specs=in_specs, out_specs=out_specs, check_vma=False
    )
```

profile of v0, /device:TPU:18, one launch (start us, length us, event | category | flops | bytes accessed | tf_op | source)
XLA Modules:
  0.0 85.5 jit_solution(8816876921594021440)
XLA Ops:
  7.2 0.0 all-gather.3.cloned.1.call-start
  7.2 1.6 %pad_maximum_fusion.2 = bf16[1,2,15360]{2,1,0:T(2,128)(2,1)} fusion(bf16[1,1,15360]{2,1,0:T(2,128)(2,1)} %bitcast.43, bf16[1,1,15360]{2,1,0:T(2,128)(2,1)} %bitcast.42), kind=kLoop, calls=%fused_computation.28 | loop fusion | flops 122880 | bytes 122880 | tf_op jit(solution)/shard_map/stack | solution.py:73
  8.8 0.0 all-gather.3.cloned.1.call-update
  8.9 1.0 %reduce = bf16[15360]{0:T(1024)(128)(2,1)S(1)} reduce(bf16[1,15360]{1,0:T(2,128)(2,1)} %param.12, bf16[]{:T(256)} %constant.58), dimensions={0}, to_apply=%param.12.reduce_sub_computation | reduce | bytes 61442 | tf_op args[0]
  9.9 0.1 reshape.56
  10.0 1.1 %fusion.5 = bf16[48,480]{1,0:T(8,128)(2,1)S(1)} fusion(bf16[48,320]{1,0:T(8,128)(2,1)S(1)} %reshape.56, bf16[320,480]{1,0:T(8,128)(2,1)} %constant.57), kind=kOutput, calls=%fused_computation.10 | convolution fusion | flops 14768640 | bytes 384000 | tf_op jit(solution)/shard_map/dot_general | solution.py:90
  11.1 1.0 %reduce.1 = bf16[15360]{0:T(1024)(128)(2,1)S(1)} reduce(bf16[1,15360]{1,0:T(2,128)(2,1)} %param.13, bf16[]{:T(256)} %constant.58), dimensions={0}, to_apply=%param.13.reduce_sub_computation | reduce | bytes 61442 | tf_op args[1]
  12.1 0.1 stack_reshape.8
  12.2 0.1 reshape.58
  12.3 0.1 stack_reshape.9
  12.4 0.1 reshape.57
  12.6 1.1 %fusion.6 = bf16[48,480]{1,0:T(8,128)(2,1)S(1)} fusion(bf16[48,320]{1,0:T(8,128)(2,1)S(1)} %reshape.58, bf16[320,480]{1,0:T(8,128)(2,1)} %constant.57), kind=kOutput, calls=%fused_computation.11 | convolution fusion | flops 14768640 | bytes 384000 | tf_op jit(solution)/shard_map/dot_general | solution.py:95
  13.7 0.1 reshape.59
  13.9 0.1 fusion.12
  14.0 0.1 copy.31
  14.1 30.4 %all-gather = bf16[8,288,160]{1,2,0:T(8,128)(2,1)S(1)} all-gather(bf16[1,288,160]{1,2,0:T(8,128)(2,1)S(1)} %copy.31), channel_id=1, replica_groups=mesh['inst'=32,'space'=8] {'space'}, dimensions={0}, use_global_device_ids=true | all-gather | bytes 829440 | tf_op jit(solution)/shard_map/all_gather | solution.py:105
  44.5 0.0 copy-start.4
  44.5 0.0 copy-start.3
  44.5 0.0 copy-start.5
  44.5 0.0 copy-start.6
  44.5 0.0 copy-start.2
  44.5 0.3 copy.32
  44.9 0.7 reshape.66
  45.6 0.0 copy-done.4
  45.6 0.0 copy-done.3
  45.7 0.0 copy-done.5
  45.7 0.0 copy-done.6
  45.7 0.1 select_reduce_fusion
  45.8 0.0 copy-done.2
  45.8 0.4 fusion.9
  46.2 0.6 fusion.4
  46.7 0.4 fusion.8
  47.1 0.1 copy.33
  47.2 0.1 reshape.61
  47.3 16.4 %reshape.55 = bf16[48,320,320]{2,1,0:T(8,128)(2,1)} reshape(bf16[1,48,102400]{2,1,0:T(8,128)(2,1)} %param.15) | data formatting | bytes 19660800 | tf_op jit(solution)/shard_map/reshape | solution.py:81
  63.7 0.0 copy-start
  63.7 7.8 %fusion.13 = f32[48,2,320]{2,1,0:T(2,128)S(1)} fusion(bf16[48,320,320]{2,1,0:T(8,128)(2,1)} %reshape.55, bf16[48,1,320]{2,1,0:T(2,128)(2,1)S(1)} %stack_reshape.9, bf16[48,1,320]{2,1,0:T(2,128)(2,1)S(1)} %stack_reshape.8), kind=kOutput, calls=%fused_computation.21 | convolution fusion | flops 19783680 | bytes 10014720 | tf_op jit(solution)/shard_map/eab,ekb->eka/dot_general | solution.py:83
  71.5 0.1 fusion.49
  71.6 0.0 copy-done
  71.6 0.7 convolution_add_fusion.1
  72.3 0.1 reshape.62
  72.4 0.0 copy-start.1
  72.4 0.1 copy.34
  72.5 0.1 reshape.63
  72.6 0.7 convolution_add_fusion
  73.3 0.1 reshape.64
  74.8 0.1 fusion.23
  74.9 0.0 all-gather.3.cloned.1.call-done
  74.9 2.8 %fusion = f32[1,2,15360]{2,0,1:T(1,128)S(1)} fusion(bf16[32,2,15360]{2,1,0:T(2,128)(2,1)} %all-gather.3.cloned.1.call-done, pred[32,32]{1,0:T(8,128)(4,1)S(1)} %fusion.22, s32[]{:T(128)S(6)} %select_n.33, f32[32,32]{1,0:T(8,128)S(1)} %get-tuple-element.9, f32[32,32]{1,0:T(8,128)S(1)} %get-tuple-element.8, f32[32,32]{1,0:T(8,128)S(1)} %fusion.23, f32[]{:T(128)} %bitcast.40, ...), kind=kOutput, calls=%fused_computation | convolution fusion | flops 11796864 | bytes 2091020 | tf_op jit(solution)/shard_map/s,skm->km/dot_general | solution.py:75
  77.7 0.1 copy.44
  77.8 0.0 copy-done.1
  77.8 0.8 slice_add_fusion
  (5 shorter events, 0.1 us)
Async XLA Ops:
  7.2 67.7 %all-gather.3.cloned.1.call-start = ((), (), s32[]{:S(2)}) async-start(), calls=%async_computation | async-start | bytes 2027520 | tf_op jit(solution)/shard_map/all_gather | solution.py:78
  44.5 1.1 %copy-start.4 = (s32[1,192,1]{1,2,0:T(1,128)S(1)}, s32[1,192,1]{1,2,0:T(1,128)}, u32[]{:S(2)}) copy-start(s32[1,192,1]{1,2,0:T(1,128)} %param.19) | copy-start | bytes 2308
  44.5 1.1 %copy-start.3 = (s32[1,192]{1,0:T(1,128)S(1)}, s32[1,192]{1,0:T(1,128)}, u32[]{:S(2)}) copy-start(s32[1,192]{1,0:T(1,128)} %param.20) | copy-start | bytes 2308
  44.5 1.1 %copy-start.5 = (s32[1,192]{1,0:T(1,128)S(1)}, s32[1,192]{1,0:T(1,128)}, u32[]{:S(2)}) copy-start(s32[1,192]{1,0:T(1,128)} %param.22) | copy-start | bytes 2308
  44.5 1.2 %copy-start.6 = (f32[16]{0:T(128)S(1)}, f32[16]{0:T(128)}, u32[]{:S(2)}) copy-start(f32[16]{0:T(128)} %param.18) | copy-start | bytes 196
  44.5 1.2 %copy-start.2 = (s32[1,192]{1,0:T(1,128)S(1)}, s32[1,192]{1,0:T(1,128)}, u32[]{:S(2)}) copy-start(s32[1,192]{1,0:T(1,128)} %param.21) | copy-start | bytes 2308
  63.7 7.9 %copy-start = (f32[320,480]{1,0:T(8,128)S(1)}, f32[320,480]{1,0:T(8,128)}, u32[]{:S(2)}) copy-start(f32[320,480]{1,0:T(8,128)} %constant.48.clone) | copy-start | bytes 1843204
  72.4 5.4 %copy-start.1 = (f32[1,15360]{1,0:T(1,128)S(1)}, f32[1,15360]{1,0:T(1,128)}, u32[]{:S(2)}) copy-start(f32[1,15360]{1,0:T(1,128)} %param.14) | copy-start | bytes 184324
Sparse Core Ops, SparseCore 0:
  11.2 49.5 all-gather.2
where the time goes:
time: 85.9 us; the launch traced here: 85.5 us
  blocking collectives  30.4 us (35%)
  local copies, waits for them, and re-layouts  19.1 us (22%)
  between operations  15.6 us (18%)
  matrix products  15.5 us (18%)
  other arithmetic  4.75 us (6%)
    all_gather x1, blocking collectives, per_device(): shard_rows = lax.all_gather(trace_table, 'space', axis=0, tiled=True)  30.4 us
    reshape x1, local copies, waits for them, and re-layouts, per_device(): matrices = jacobian.reshape(E_DEV, DOF, DOF)  16.4 us
    dot_general x1, matrix products, per_device(): jnp.einsum('eab,ekb->eka', matrices, flat_fields, preferred_element_type=...  7.75 us
    dot_general x1, matrix products, per_device(): jnp.einsum('s,skm->km', row_weights, lax.all_gather(stacked_rows, 'inst',...  2.82 us
    unnamed x3, other arithmetic  2.11 us
  transfers between devices with their start and end apart: 1, of which 0 were waited for; matrix products, arithmetic and copies ran while one was open for 40% of the time, Pallas kernels for 0%

commit v1 on v0

v1 whole, which is shorter than its diff:
```python
import jax
import jax.numpy as jnp
import numpy as np
from jax import lax
from jax.experimental import pallas as pl
from jax.experimental.pallas import tpu as pltpu
from jax.sharding import PartitionSpec as P

VARS = 5
PNODE = 4
E_DEV = 48
DOF = 320
SLOTS_DEV = 192
N_SPACE = 8
NT = 32
FLAT = E_DEV * DOF
ROWS = FLAT // 128
CHUNKS = 10
GROUPS = 8
PIECE = GROUPS * 4 * DOF
GROUP = 8
TURNS = NT // GROUP
MIB = 1024 * 1024
F32 = jnp.float32
BF16 = jnp.bfloat16


def face_selector():
    table = np.zeros((DOF, 6 * 128), np.float32)
    for face in range(6):
        fixed = 0 if face % 2 == 0 else PNODE - 1
        for comp in range(VARS):
            for first in range(PNODE):
                for second in range(PNODE):
                    if face < 2:
                        i, j, k = fixed, first, second
                    elif face < 4:
                        i, j, k = first, fixed, second
                    else:
                        i, j, k = first, second, fixed
                    table[comp * 64 + i * 16 + j * 4 + k, face * 128 + comp * 16 + first * 4 + second] = 1.0
    return table


def face_incidence():
    rows = np.zeros((8, 384), np.float32)
    for face in range(6):
        rows[face, :DOF] = face_selector()[:, face * 128 : (face + 1) * 128].sum(axis=1)
    return rows


def lane_half(rows):
    return lax.broadcasted_iota(jnp.int32, (rows, 128), 1) < 64


def swap(x):
    return pltpu.roll(x, 64, 1)


def join(low, high):
    return jnp.where(lane_half(low.shape[0]), swap(low), swap(high))


def prep_kernel(s_ref, d_ref, copies_ref, elem_ref, flat, wide):
    for k, ref in enumerate((s_ref, d_ref)):
        for r in range(ROWS):
            flat[k * ROWS + r : k * ROWS + r + 1, :] = ref[0:1, r * 128 : (r + 1) * 128].astype(F32)
    half = E_DEV // 2
    low = lane_half(half)
    s = [flat[pl.ds(q, half, stride=5), :] for q in range(5)]
    d = [flat[pl.ds(ROWS + q, half, stride=5), :] for q in range(5)]
    even = [s[0], s[1], jnp.where(low, s[2], swap(d[0])), join(d[0], d[1]), join(d[1], d[2])]
    odd = [join(s[2], s[3]), join(s[3], s[4]), jnp.where(low, swap(s[4]), d[2]), d[3], d[4]]
    for q in range(5):
        wide[q, pl.ds(0, half, stride=2), :] = even[q]
        wide[q, pl.ds(1, half, stride=2), :] = odd[q]
    for q in range(5):
        tile = wide[q].astype(BF16)
        elem_ref[:, q * 128 : (q + 1) * 128] = tile
        for to in range(GROUP):
            copies_ref[to, :, q * 128 : (q + 1) * 128] = tile


def prep(state, direction):
    return pl.pallas_call(
        prep_kernel,
        out_shape=(
            jax.ShapeDtypeStruct((GROUP, E_DEV, 2 * DOF), BF16),
            jax.ShapeDtypeStruct((E_DEV, 2 * DOF), BF16),
        ),
        in_specs=[pl.BlockSpec(memory_space=pltpu.VMEM)] * 2,
        out_specs=(pl.BlockSpec(memory_space=pltpu.VMEM),) * 2,
        scratch_shapes=[pltpu.VMEM((2 * ROWS, 128), F32), pltpu.VMEM((5, E_DEV, 128), F32)],
        compiler_params=pltpu.CompilerParams(vmem_limit_bytes=4 * MIB),
        name="prep",
    )(state, direction)


def circulant_parts():
    j = np.arange(1, NT)
    sign = 1.0 - 2.0 * (j % 2)
    angle = np.pi * j / NT
    first = np.concatenate([[0.0], 0.5 * sign * np.cos(angle) / np.sin(angle)])
    second = np.concatenate([[-(NT * NT + 2) / 12.0], -sign / (2.0 * np.sin(angle) ** 2)])
    return first, second


def partial_kernel(place_ref, table_ref, freq_ref, visc_ref, x_ref, y_ref):
    place = place_ref[0]
    row, col = place // GROUP, place % GROUP
    freq, visc = freq_ref[0], visc_ref[0]
    coef = []
    for y in range(TURNS):
        for a in range(GROUP):
            j = ((y - row) * GROUP + col - a) & (NT - 1)
            coef.append(jnp.full((8, 128), freq * table_ref[0, j] + visc * table_ref[1, j], F32))
    for r in range(E_DEV // 16):
        for q in range(5):
            x = [
                x_ref[a, r * 16 : (r + 1) * 16, q * 128 : (q + 1) * 128].astype(F32)
                for a in range(GROUP)
            ]
            for h in range(2):
                part = [v[h * 8 : (h + 1) * 8] for v in x]
                for y in range(TURNS):
                    acc = coef[y * GROUP] * part[0]
                    for a in range(1, GROUP):
                        acc = acc + coef[y * GROUP + a] * part[a]
                    y_ref[y, r * 16 + h * 8 : r * 16 + (h + 1) * 8, q * 128 : (q + 1) * 128] = acc


def partial_sums(place, frequency, viscosity, gathered):
    smem = pl.BlockSpec(memory_space=pltpu.SMEM)
    vmem = pl.BlockSpec(memory_space=pltpu.VMEM)
    table = jnp.asarray(np.stack(circulant_parts()), F32)
    return pl.pallas_call(
        partial_kernel,
        out_shape=jax.ShapeDtypeStruct((TURNS, E_DEV, 2 * DOF), F32),
        in_specs=[smem, smem, smem, smem, vmem],
        out_specs=vmem,
        compiler_params=pltpu.CompilerParams(vmem_limit_bytes=4 * MIB),
        name="partial_sums",
    )(place, table, frequency, viscosity, gathered)


def vector_tiles(elem):
    p = [elem[:, q * 128 : (q + 1) * 128] for q in range(5)]
    low = lane_half(E_DEV)
    zero = jnp.zeros((E_DEV, 128), F32)
    s = [p[0], p[1], jnp.where(low, p[2], zero), jnp.where(low, zero, swap(p[0])), join(p[0], p[1]), join(p[1], p[2])]
    d = [join(p[2], p[3]), join(p[3], p[4]), jnp.where(low, swap(p[4]), zero), jnp.where(low, zero, p[2]), p[3], p[4]]
    return s, d


def jacobian_kernel(jac_ref, elem_ref, out_ref, held, weights, acc, rows, sems):
    copies = [
        pltpu.make_async_copy(jac_ref.at[0, :, pl.ds(c * PIECE, PIECE)], held.at[c], sems.at[c])
        for c in range(CHUNKS)
    ]
    for copy in copies:
        copy.start()
    s, d = vector_tiles(elem_ref[...].astype(F32))
    pad = jnp.zeros((128 - 2 * E_DEV, 128), F32)
    x0, x1, x2, y0, y1, y2 = [
        jnp.concatenate([a, b, pad], axis=0).T.astype(BF16) for a, b in zip(s, d)
    ]
    zero = jnp.zeros((128, 128), BF16)
    layout = (
        ((x0, zero), (x1, zero)),
        ((x2, y0), (zero, y1)),
        ((y2, zero), (zero, x0)),
        ((x1, zero), (x2, y0)),
        ((y1, zero), (y2, zero)),
    )
    for t in range(5):
        for i in range(2):
            for j in range(2):
                weights[t, i * 128 : (i + 1) * 128, j * 128 : (j + 1) * 128] = layout[t][i][j]
    e = lax.broadcasted_iota(jnp.int32, (E_DEV, 128), 0)
    lane = lax.broadcasted_iota(jnp.int32, (E_DEV, 128), 1)
    keep = (lane == e) | (lane == e + E_DEV)

    def step(c, carry):
        start = pl.multiple_of(c * PIECE, PIECE)
        pltpu.make_async_copy(jac_ref.at[0, :, pl.ds(start, PIECE)], held.at[c], sems.at[c]).wait()
        res = []
        for t in range(5):
            lhs = jnp.concatenate(
                [held[c, :, (g * 5 + t) * 256 : (g * 5 + t + 1) * 256] for g in range(GROUPS)], axis=0
            )
            w = weights[t] if t in (1, 2, 3) else weights[t][:, :128]
            res.append(jnp.dot(lhs, w, preferred_element_type=F32))
        pairs = (
            res[0] + res[1][:, :128],
            res[1][:, 128:] + res[2][:, :128],
            res[2][:, 128:] + res[3][:, :128],
            res[3][:, 128:] + res[4],
        )
        for i in range(4):
            r = jnp.where(keep[None], pairs[i].reshape(GROUPS, E_DEV, 128), 0.0)
            acc[i, pl.ds(pl.multiple_of(c * GROUPS, GROUPS), GROUPS), :] = jnp.sum(r, axis=1)
        return carry

    lax.fori_loop(0, CHUNKS, step, 0)
    for i in range(4):
        rows[pl.ds(i, CHUNKS * GROUPS, stride=4), :] = acc[i]
    rows[DOF:, :] = jnp.zeros((384 - DOF, 128), F32)
    for q in range(3):
        out_ref[:, q * 128 : (q + 1) * 128] = rows[q * 128 : (q + 1) * 128, :].T


def jacobian_product(jacobian, elem):
    return pl.pallas_call(
        jacobian_kernel,
        out_shape=jax.ShapeDtypeStruct((128, 384), F32),
        in_specs=[pl.BlockSpec(memory_space=pl.ANY), pl.BlockSpec(memory_space=pltpu.VMEM)],
        out_specs=pl.BlockSpec(memory_space=pltpu.VMEM),
        scratch_shapes=[
            pltpu.VMEM((CHUNKS, E_DEV, PIECE), BF16),
            pltpu.VMEM((5, 256, 256), BF16),
            pltpu.VMEM((4, CHUNKS * GROUPS, 128), F32),
            pltpu.VMEM((384, 128), F32),
            pltpu.SemaphoreType.DMA((CHUNKS,)),
        ],
        compiler_params=pltpu.CompilerParams(vmem_limit_bytes=49 * MIB),
        cost_estimate=pl.CostEstimate(
            flops=2 * 2 * E_DEV * DOF * DOF * 48, bytes_accessed=2 * E_DEV * DOF * DOF, transcendentals=0
        ),
        name="jacobian",
    )(jacobian, elem)


def split(x):
    high = x.astype(BF16)
    return high, (x - high.astype(F32)).astype(BF16)


def flux_kernel(quad_ref, dev_ref, far_ref, near_ref, cls_ref, elem_ref, jac_ref, sel_ref, inc_ref, table_ref, out_ref):
    far = far_ref[...]
    near = near_ref[...]
    cls = cls_ref[...]
    far_e = (far * 10923) >> 16
    far_l = far - far_e * 6
    near_e = (near * 10923) >> 16
    near_row = (near - near_e * 6) * E_DEV + near_e
    column = dev_ref[...] * E_DEV + far_e
    w = jnp.zeros((1, SLOTS_DEV), F32)
    for c in range(16):
        w = jnp.where(cls == c, quad_ref[c], w)
    r = lax.broadcasted_iota(jnp.int32, (SLOTS_DEV, SLOTS_DEV), 0)
    c = lax.broadcasted_iota(jnp.int32, (SLOTS_DEV, SLOTS_DEV), 1)
    both = (far_l * 512 + column).astype(F32)
    code = jnp.sum(jnp.where(r == c, both, 0.0), axis=1, keepdims=True).astype(jnp.int32)
    column_s = code & 511
    far_ls = code >> 9
    total = N_SPACE * E_DEV
    pick = (lax.broadcasted_iota(jnp.int32, (SLOTS_DEV, total), 1) == column_s).astype(F32).astype(BF16)
    table = table_ref[...].reshape(total, 2 * DOF)
    got = jnp.dot(pick, table, preferred_element_type=F32)
    p = [got[:, q * 128 : (q + 1) * 128] for q in range(5)]
    low = lane_half(SLOTS_DEV)
    zero = jnp.zeros((SLOTS_DEV, 128), F32)
    fields = jnp.concatenate(
        [
            jnp.concatenate([p[0], p[1], jnp.where(low, p[2], zero)], axis=1),
            jnp.concatenate([join(p[2], p[3]), join(p[3], p[4]), jnp.where(low, swap(p[4]), zero)], axis=1),
        ],
        axis=0,
    ).astype(BF16)
    sel = sel_ref[...]
    faces = jnp.dot(fields, sel, preferred_element_type=F32)
    which = jnp.concatenate([far_ls, far_ls], axis=0)
    trace = jnp.zeros((2 * SLOTS_DEV, 128), F32)
    for face in range(6):
        trace = jnp.where(which == face, faces[:, face * 128 : (face + 1) * 128], trace)
    trace = jnp.concatenate([trace[:SLOTS_DEV], trace[SLOTS_DEV:]], axis=1).astype(BF16)
    rows = lax.broadcasted_iota(jnp.int32, (6 * E_DEV, SLOTS_DEV), 0)
    spread = jnp.where(rows == near_row, w, 0.0)
    high, rest_w = split(spread)
    flux = jnp.dot(high, trace, preferred_element_type=F32) + jnp.dot(rest_w, trace, preferred_element_type=F32)
    weight_sum = jnp.sum(spread, axis=1, keepdims=True)
    lhs = jnp.concatenate(
        [
            jnp.concatenate(
                [flux[f * E_DEV : (f + 1) * E_DEV, :128], flux[f * E_DEV : (f + 1) * E_DEV, 128:]], axis=0
            )
            for f in range(6)
        ],
        axis=1,
    )
    high, rest_f = split(lhs)
    dims = (((1,), (1,)), ((), ()))
    lifted = lax.dot_general(high, sel, dims, preferred_element_type=F32) + lax.dot_general(
        rest_f, sel, dims, preferred_element_type=F32
    )
    coef = jnp.zeros((E_DEV, 384), F32)
    for f in range(6):
        coef = coef + weight_sum[f * E_DEV : (f + 1) * E_DEV] * inc_ref[f : f + 1, :]
    fields_own = vector_tiles(elem_ref[...].astype(F32))
    for k in range(2):
        own = jnp.concatenate(fields_own[k][:3], axis=1)
        rows_k = slice(k * E_DEV, (k + 1) * E_DEV)
        out_ref[rows_k, :] = jac_ref[rows_k, :] + coef * own - lifted[rows_k]


def space_terms(quad, dev, far, near, cls, elem, jac_terms, table):
    sel = np.zeros((384, 768), np.float32)
    sel[:DOF] = face_selector()
    vmem = pl.BlockSpec(memory_space=pltpu.VMEM)
    return pl.pallas_call(
        flux_kernel,
        out_shape=jax.ShapeDtypeStruct((2 * E_DEV, 384), F32),
        in_specs=[pl.BlockSpec(memory_space=pltpu.SMEM)] + [vmem] * 9,
        out_specs=vmem,
        compiler_params=pltpu.CompilerParams(vmem_limit_bytes=12 * MIB),
        name="space_terms",
    )(
        quad, dev, far, near, cls, elem, jac_terms,
        jnp.asarray(sel, BF16), jnp.asarray(face_incidence()), table,
    )


def final_kernel(src_ref, time_ref, space_ref, res_ref, prod_ref, scratch):
    total = time_ref[0]
    for y in range(1, TURNS):
        total = total + time_ref[y]
    times = vector_tiles(total)
    half = E_DEV // 2
    low = lane_half(half)
    for k, out_ref in enumerate((res_ref, prod_ref)):
        for q in range(3):
            scratch[q] = space_ref[k * E_DEV : (k + 1) * E_DEV, q * 128 : (q + 1) * 128] + times[k][q]
        even = [scratch[q, pl.ds(0, half, stride=2), :] for q in range(3)]
        odd = [scratch[q, pl.ds(1, half, stride=2), :] for q in range(3)]
        tiles = [
            even[0],
            even[1],
            jnp.where(low, even[2], swap(odd[0])),
            join(odd[0], odd[1]),
            join(odd[1], odd[2]),
        ]
        for q in range(5):
            at = tiles[q]
            if k == 0:
                at = src_ref[pl.ds(q, half, stride=5), :] - at
            out_ref[pl.ds(q, half, stride=5), :] = at


def finish(source, time_parts, space):
    vmem = pl.BlockSpec(memory_space=pltpu.VMEM)
    return pl.pallas_call(
        final_kernel,
        out_shape=(jax.ShapeDtypeStruct((ROWS, 128), F32),) * 2,
        in_specs=[vmem] * 3,
        out_specs=(vmem, vmem),
        scratch_shapes=[pltpu.VMEM((3, E_DEV, 128), F32)],
        compiler_params=pltpu.CompilerParams(vmem_limit_bytes=4 * MIB),
        name="finish",
    )(source, time_parts, space)


def per_device(
    harmonic_state,
    direction,
    source,
    jacobian,
    frequency,
    viscosity,
    quad_weight,
    partner_device,
    partner_face,
    local_face,
    weight_index,
):
    copies, elem = prep(harmonic_state, direction)
    place = lax.axis_index("inst").reshape(1)
    table = lax.all_to_all(copies, "space", 0, 0, tiled=True)
    rows = [[y * GROUP + a for a in range(GROUP)] for y in range(TURNS)]
    columns = [[y * GROUP + a for y in range(TURNS)] for a in range(GROUP)]
    gathered = lax.all_to_all(copies, "inst", 0, 0, axis_index_groups=rows, tiled=True)
    parts = partial_sums(place, frequency, viscosity, gathered)
    time_parts = lax.all_to_all(parts, "inst", 0, 0, axis_index_groups=columns, tiled=True)
    jac_terms = jacobian_product(jacobian, elem)
    space = space_terms(
        quad_weight,
        partner_device.reshape(1, SLOTS_DEV),
        partner_face,
        local_face,
        weight_index,
        elem,
        jac_terms,
        table,
    )
    residual, product = finish(source.reshape(ROWS, 128), time_parts, space)
    return residual.reshape(1, FLAT), product.reshape(1, FLAT)


def solution(mesh):
    in_specs = (
        P("inst", "space"),
        P("inst", "space"),
        P("inst", "space"),
        P("inst", "space", None),
        P(),
        P(),
        P(),
        P("inst", "space", None),
        P("inst", "space"),
        P("inst", "space"),
        P("inst", "space"),
    )
    out_specs = (P("inst", "space"), P("inst", "space"))
    return jax.shard_map(
        per_device, mesh=mesh, in_specs=in_specs, out_specs=out_specs, check_vma=False
    )
```

time: 85.9 us -> 57 us (0.66)
  the two profiles are of different devices: /device:TPU:18 before, /device:TPU:8 now
where the time goes in v1:
time: 57 us; the launch traced here: 56.6 us
  blocking collectives  14.3 us (25%)
  starting transfers between devices  13.4 us (24%)
  waiting for transfers between devices  12.8 us (22%)
  Pallas kernels  11.5 us (20%)
  local copies, waits for them, and re-layouts  2.42 us (4%)
  between operations  2.07 us (4%)
    all_to_all x1, blocking collectives, per_device(): lax.all_to_all(copies, 'inst', 0, 0, axis_index_groups=rows, tiled=True)  14.3 us
    all_to_all x1, waiting for transfers between devices, per_device(): table = lax.all_to_all(copies, 'space', 0, 0, tiled=True)  12.8 us
    all_to_all x1, starting transfers between devices, per_device(): table = lax.all_to_all(copies, 'space', 0, 0, tiled=True)  8.47 us
    pallas_call x1, Pallas kernels, jacobian_product(): pl.pallas_call(jacobian_kernel, out_shape=jax.ShapeDtypeStruct((128, 384)...  5.84 us
    all_to_all x1, starting transfers between devices, per_device(): lax.all_to_all(parts, 'inst', 0, 0, axis_index_groups=columns, tiled=True)  4.91 us
    unnamed x22, local copies, waits for them, and re-layouts  2.42 us
    pallas_call x1, Pallas kernels, space_terms(): pl.pallas_call(flux_kernel, out_shape=jax.ShapeDtypeStruct((2 * E_DEV, 38...  2.28 us
    pallas_call x1, Pallas kernels, partial_sums(): pl.pallas_call(partial_kernel, out_shape=jax.ShapeDtypeStruct((TURNS, E_D...  1.65 us
  transfers between devices with their start and end apart: 2, of which 1 were waited for; matrix products, arithmetic and copies ran while one was open for 0% of the time, Pallas kernels for 17%

profile of v1, /device:TPU:8, one launch (start us, length us, event | category | flops | bytes accessed | tf_op | source)
XLA Modules:
  0.0 56.6 jit_solution(4626174082325044331)
XLA Ops:
  0.6 0.0 copy-start
  0.6 0.0 copy-start.1
  0.7 0.9 %copy-done.1 = bf16[1,15360]{1,0:T(2,128)(2,1)S(1)} copy-done((bf16[1,15360]{1,0:T(2,128)(2,1)S(1)}, bf16[1,15360]{1,0:T(2,128)(2,1)}, u32[]{:S(2)}) %copy-start.1) | copy-done | bytes 30744
  1.5 0.0 copy-start.2
  1.5 0.8 %copy-done.2 = bf16[1,15360]{1,0:T(2,128)(2,1)S(1)} copy-done((bf16[1,15360]{1,0:T(2,128)(2,1)S(1)}, bf16[1,15360]{1,0:T(2,128)(2,1)}, u32[]{:S(2)}) %copy-start.2) | copy-done | bytes 30744
  2.4 0.0 copy-start.4
  2.4 0.0 copy-start.6
  2.4 0.0 copy-start.7
  2.4 0.0 copy-start.8
  2.4 0.0 copy-start.9
  2.4 0.0 copy-start.10
  2.4 0.0 copy-start.3
  2.4 1.0 %prep.1 = (bf16[8,48,640]{2,1,0:T(8,128)(2,1)}, bf16[48,640]{1,0:T(8,128)(2,1)S(1)}) custom-call(bf16[1,15360]{1,0:T(2,128)(2,1)S(1)} %copy-done.1, bf16[1,15360]{1,0:T(2,128)(2,1)S(1)} %copy-done.2), custom_call_target="tpu_custom_call" | custom-call | tf_op jit(solution)/shard_map/prep/pallas_call | solution.py:85
  3.4 14.3 %all_to_all.15.x_ref = bf16[8,48,640]{2,1,0:T(8,128)(2,1)S(1)} all-to-all(bf16[8,48,640]{2,1,0:T(8,128)(2,1)} %get-tuple-element.6), channel_id=1, replica_groups={{0,8,16,24,32,40,48,56},{64,72,80,88,96,104,112,120},{128,136,144,152,1..., dimensions={0} | all-to-all | bytes 983040 | tf_op jit(solution)/shard_map/all_to_all | solution.py:380
  17.7 8.5 %all-to-all-start.2 = ((bf16[8,48,640]{2,1,0:T(8,128)(2,1)}), bf16[8,48,640]{2,1,0:T(8,128)(2,1)S(1)}, u32[]{:S(2)}, u32[]{:S(2)}) async-start(bf16[8,48,640]{2,1,0:T(8,128)(2,1)} %get-tuple-element.6), calls=%async_computation.2 | async-start | bytes 983040 | tf_op jit(solution)/shard_map/all_to_all | solution.py:377
  27.5 0.0 copy-start.5
  27.5 0.7 %copy-done.5 = f32[2,32]{1,0:T(2,128)S(1)} copy-done((f32[2,32]{1,0:T(2,128)S(1)}, f32[2,32]{1,0:T(2,128)}, u32[]{:S(2)}) %copy-start.5) | copy-done | bytes 280
  28.2 1.6 %partial_sums.1 = f32[4,48,640]{2,1,0:T(8,128)} custom-call(s32[1]{0:T(128)} %bitcast.1.place_ref, f32[2,32]{1,0:T(2,128)S(1)} %copy-done.5, f32[1]{0:T(128)S(6)} %copy.16.freq_ref, f32[1]{0:T(128)S(6)} %copy.17.visc_ref, bf16[8,48,640]{2,1,0:T(8,128)(2,1)S(1)} %all_to_all.15.x_ref), custom_call_target="tpu_custom_call" | custom-call | tf_op jit(solution)/shard_map/partial_sums/pallas_call | solution.py:136
  29.8 12.8 %all-to-all-done.2.table_ref = bf16[8,48,640]{2,1,0:T(8,128)(2,1)S(1)} async-done(((bf16[8,48,640]{2,1,0:T(8,128)(2,1)}), bf16[8,48,640]{2,1,0:T(8,128)(2,1)S(1)}, u32[]{:S(2)}, u32[]{:S(2)}) %all-to-all-start.2) | async-done | bytes 491552 | tf_op jit(solution)/shard_map/all_to_all | solution.py:377
  42.7 4.9 %all-to-all-start.1 = ((f32[4,48,640]{2,1,0:T(8,128)}), f32[4,48,640]{2,1,0:T(8,128)S(1)}, u32[]{:S(2)}, u32[]{:S(2)}) async-start(f32[4,48,640]{2,1,0:T(8,128)} %partial_sums.1), calls=%async_computation.1 | async-start | bytes 983040 | tf_op jit(solution)/shard_map/all_to_all | solution.py:382
  47.6 5.8 %jacobian.1.jac_ref = f32[128,384]{1,0:T(8,128)S(1)} custom-call(bf16[1,48,102400]{2,1,0:T(8,128)(2,1)} %jac_ref.1, bf16[48,640]{1,0:T(8,128)(2,1)S(1)} %get-tuple-element.7.elem_ref), custom_call_target="tpu_custom_call" | custom-call | flops 943718400 | bytes 9830400 | tf_op jit(solution)/shard_map/jacobian/pallas_call | solution.py:213
  53.4 0.0 copy-done
  53.4 0.0 copy-done.4
  53.4 0.0 copy-done.6
  53.4 0.0 copy-done.7
  53.5 0.0 copy-done.8
  53.5 0.0 copy-done.9
  53.5 0.0 copy-done.10
  53.5 2.3 %space_terms.1.space_ref = f32[96,384]{1,0:T(8,128)S(1)} custom-call(f32[16]{0:T(128)S(1)} %copy-done.10, s32[1,192]{1,0:T(1,128)S(1)} %bitcast.6, s32[1,192]{1,0:T(1,128)S(1)} %copy-done.7, s32[1,192]{1,0:T(1,128)S(1)} %copy-done.8, s32[1,192]{1,0:T(1,128)S(1)} %copy-done.9, bf16[48,640]{1,0:T(8,128)(2,1)S(1)} %get-tuple-element.7.elem_ref, ...), custom_call_target="tpu_custom_call" | custom-call | tf_op jit(solution)/shard_map/space_terms/pallas_call | solution.py:310
  55.8 0.0 all-to-all-done.1.time_ref
  55.8 0.0 copy-done.3
  55.8 0.8 %finish.1 = (f32[120,128]{1,0:T(8,128)}, f32[120,128]{1,0:T(8,128)}) custom-call(f32[120,128]{1,0:T(8,128)S(1)} %bitcast.5, f32[4,48,640]{2,1,0:T(8,128)S(1)} %all-to-all-done.1.time_ref, f32[96,384]{1,0:T(8,128)S(1)} %space_terms.1.space_ref), custom_call_target="tpu_custom_call" | custom-call | tf_op jit(solution)/shard_map/finish/pallas_call | solution.py:351
Async XLA Ops:
  0.6 52.8 %copy-start = (bf16[384,768]{1,0:T(8,128)(2,1)S(1)}, bf16[384,768]{1,0:T(8,128)(2,1)}, u32[]{:S(2)}) copy-start(bf16[384,768]{1,0:T(8,128)(2,1)} %constant.13.clone.sel_ref) | copy-start | bytes 1769476
  0.6 0.9 %copy-start.1 = (bf16[1,15360]{1,0:T(2,128)(2,1)S(1)}, bf16[1,15360]{1,0:T(2,128)(2,1)}, u32[]{:S(2)}) copy-start(bf16[1,15360]{1,0:T(2,128)(2,1)} %s_ref.1) | copy-start | bytes 92164
  1.5 0.8 %copy-start.2 = (bf16[1,15360]{1,0:T(2,128)(2,1)S(1)}, bf16[1,15360]{1,0:T(2,128)(2,1)}, u32[]{:S(2)}) copy-start(bf16[1,15360]{1,0:T(2,128)(2,1)} %d_ref.1) | copy-start | bytes 92164
  2.4 51.1 %copy-start.4 = (f32[8,384]{1,0:T(8,128)S(1)}, f32[8,384]{1,0:T(8,128)}, u32[]{:S(2)}) copy-start(f32[8,384]{1,0:T(8,128)} %constant.14.clone.inc_ref) | copy-start | bytes 36868
  2.4 51.1 %copy-start.6 = (s32[1,192,1]{1,2,0:T(1,128)S(1)}, s32[1,192,1]{1,2,0:T(1,128)}, u32[]{:S(2)}) copy-start(s32[1,192,1]{1,2,0:T(1,128)} %param.21) | copy-start | bytes 2308
  2.4 51.1 %copy-start.7 = (s32[1,192]{1,0:T(1,128)S(1)}, s32[1,192]{1,0:T(1,128)}, u32[]{:S(2)}) copy-start(s32[1,192]{1,0:T(1,128)} %far_ref.1) | copy-start | bytes 2308
  2.4 51.1 %copy-start.8 = (s32[1,192]{1,0:T(1,128)S(1)}, s32[1,192]{1,0:T(1,128)}, u32[]{:S(2)}) copy-start(s32[1,192]{1,0:T(1,128)} %near_ref.1) | copy-start | bytes 2308
  2.4 51.1 %copy-start.9 = (s32[1,192]{1,0:T(1,128)S(1)}, s32[1,192]{1,0:T(1,128)}, u32[]{:S(2)}) copy-start(s32[1,192]{1,0:T(1,128)} %cls_ref.1) | copy-start | bytes 2308
  2.4 51.1 %copy-start.10 = (f32[16]{0:T(128)S(1)}, f32[16]{0:T(128)}, u32[]{:S(2)}) copy-start(f32[16]{0:T(128)} %quad_ref.1) | copy-start | bytes 196
  2.4 53.4 %copy-start.3 = (f32[1,15360]{1,0:T(1,128)S(1)}, f32[1,15360]{1,0:T(1,128)}, u32[]{:S(2)}) copy-start(f32[1,15360]{1,0:T(1,128)} %param.16) | copy-start | bytes 184324
  17.7 24.9 %all-to-all-start.2 = ((bf16[8,48,640]{2,1,0:T(8,128)(2,1)}), bf16[8,48,640]{2,1,0:T(8,128)(2,1)S(1)}, u32[]{:S(2)}, u32[]{:S(2)}) async-start(bf16[8,48,640]{2,1,0:T(8,128)(2,1)} %get-tuple-element.6), calls=%async_computation.2 | async-start | bytes 983040 | tf_op jit(solution)/shard_map/all_to_all | solution.py:377
  27.5 0.7 %copy-start.5 = (f32[2,32]{1,0:T(2,128)S(1)}, f32[2,32]{1,0:T(2,128)}, u32[]{:S(2)}) copy-start(f32[2,32]{1,0:T(2,128)} %constant.12.clone.table_ref) | copy-start | bytes 772
  42.7 13.1 %all-to-all-start.1 = ((f32[4,48,640]{2,1,0:T(8,128)}), f32[4,48,640]{2,1,0:T(8,128)S(1)}, u32[]{:S(2)}, u32[]{:S(2)}) async-start(f32[4,48,640]{2,1,0:T(8,128)} %partial_sums.1), calls=%async_computation.1 | async-start | bytes 983040 | tf_op jit(solution)/shard_map/all_to_all | solution.py:382

commit v2 on v1

v2 whole, which is shorter than its diff:
```python
import jax
import jax.numpy as jnp
import numpy as np
from jax import lax
from jax.experimental import pallas as pl
from jax.experimental.pallas import tpu as pltpu
from jax.sharding import PartitionSpec as P

VARS = 5
PNODE = 4
E_DEV = 48
DOF = 320
SLOTS_DEV = 192
N_SPACE = 8
NT = 32
FLAT = E_DEV * DOF
ROWS = FLAT // 128
CHUNKS = 5
GROUPS = 16
BLOCK = 16
PIECE = GROUPS * 4 * DOF
MIB = 1024 * 1024
F32 = jnp.float32
BF16 = jnp.bfloat16


def face_selector():
    table = np.zeros((DOF, 6 * 128), np.float32)
    for face in range(6):
        fixed = 0 if face % 2 == 0 else PNODE - 1
        for comp in range(VARS):
            for first in range(PNODE):
                for second in range(PNODE):
                    if face < 2:
                        i, j, k = fixed, first, second
                    elif face < 4:
                        i, j, k = first, fixed, second
                    else:
                        i, j, k = first, second, fixed
                    table[comp * 64 + i * 16 + j * 4 + k, face * 128 + comp * 16 + first * 4 + second] = 1.0
    return table


def face_incidence():
    rows = np.zeros((8, 384), np.float32)
    for face in range(6):
        rows[face, :DOF] = face_selector()[:, face * 128 : (face + 1) * 128].sum(axis=1)
    return rows


def lane_half(rows):
    return lax.broadcasted_iota(jnp.int32, (rows, 128), 1) < 64


def swap(x):
    return pltpu.roll(x, 64, 1)


def join(low, high):
    return jnp.where(lane_half(low.shape[0]), swap(low), swap(high))


def prep_kernel(s_hbm, d_hbm, send_ref, elem_ref, held, flat, wide, sems):
    copies = [pltpu.make_async_copy(ref, held.at[k], sems.at[k]) for k, ref in enumerate((s_hbm, d_hbm))]
    for copy in copies:
        copy.start()
    for k in range(2):
        copies[k].wait()
        for r in range(ROWS):
            flat[k * ROWS + r : k * ROWS + r + 1, :] = held[k, 0:1, r * 128 : (r + 1) * 128].astype(F32)
    flat[2 * ROWS : 256, :] = jnp.zeros((256 - 2 * ROWS, 128), F32)
    send_ref[...] = flat[...].astype(BF16)
    half = E_DEV // 2
    low = lane_half(half)
    s = [flat[pl.ds(q, half, stride=5), :] for q in range(5)]
    d = [flat[pl.ds(ROWS + q, half, stride=5), :] for q in range(5)]
    even = [s[0], s[1], jnp.where(low, s[2], swap(d[0])), join(d[0], d[1]), join(d[1], d[2])]
    odd = [join(s[2], s[3]), join(s[3], s[4]), jnp.where(low, swap(s[4]), d[2]), d[3], d[4]]
    for q in range(5):
        wide[q, pl.ds(0, half, stride=2), :] = even[q]
        wide[q, pl.ds(1, half, stride=2), :] = odd[q]
    for q in range(5):
        elem_ref[:, q * 128 : (q + 1) * 128] = wide[q].astype(BF16)


def prep(state, direction):
    return pl.pallas_call(
        prep_kernel,
        out_shape=(
            jax.ShapeDtypeStruct((256, 128), BF16),
            jax.ShapeDtypeStruct((E_DEV, 2 * DOF), BF16),
        ),
        in_specs=[pl.BlockSpec(memory_space=pltpu.HBM)] * 2,
        out_specs=(pl.BlockSpec(memory_space=pltpu.VMEM),) * 2,
        scratch_shapes=[
            pltpu.VMEM((2, 1, FLAT), BF16),
            pltpu.VMEM((256, 128), F32),
            pltpu.VMEM((5, E_DEV, 128), F32),
            pltpu.SemaphoreType.DMA((2,)),
        ],
        compiler_params=pltpu.CompilerParams(vmem_limit_bytes=4 * MIB),
        name="prep",
    )(state, direction)


def circulant_parts():
    j = np.arange(1, NT)
    sign = 1.0 - 2.0 * (j % 2)
    angle = np.pi * j / NT
    first = np.concatenate([[0.0], 0.5 * sign * np.cos(angle) / np.sin(angle)])
    second = np.concatenate([[-(NT * NT + 2) / 12.0], -sign / (2.0 * np.sin(angle) ** 2)])
    return first, second


def spectral_kernel(freq_ref, visc_ref, x_ref, own_ref, left_ref, right_ref, far_ref, y_ref, to_right_ref, to_left_ref):
    to_right_ref[:E_DEV, :] = own_ref[...]
    to_right_ref[E_DEV:, :] = left_ref[...]
    to_left_ref[:E_DEV, :] = own_ref[...]
    to_left_ref[E_DEV:, :] = right_ref[...]
    first, second = circulant_parts()
    freq, visc = freq_ref[0], visc_ref[0]
    half = NT // 2
    x = x_ref[...].astype(F32).reshape(NT, 8, 128)

    def coef(a, b):
        return jnp.full((8, 128), freq * float(a) + visc * float(b), F32)

    def part(sgn):
        c = [
            coef(0.5 * (first[j] + sgn * first[j + half]), 0.5 * (second[j] + sgn * second[j + half]))
            for j in range(half)
        ]
        u = [x[s] + sgn * x[s + half] for s in range(half)]
        out = []
        for t in range(half):
            acc = None
            for s in range(half):
                j = t - s
                term = c[j % half] * u[s]
                if acc is None:
                    acc = term
                elif j < 0 and sgn < 0:
                    acc = acc - term
                else:
                    acc = acc + term
            out.append(acc)
        return out

    even = part(1.0)
    for t in range(half):
        y_ref[t * 8 : (t + 1) * 8, :] = even[t]
    odd = part(-1.0)
    for t in range(half):
        e = y_ref[t * 8 : (t + 1) * 8, :]
        y_ref[t * 8 : (t + 1) * 8, :] = e + odd[t]
        y_ref[(t + half) * 8 : (t + half + 1) * 8, :] = e - odd[t]


def spectral_sum(frequency, viscosity, received, own, left, right, far):
    smem = pl.BlockSpec(memory_space=pltpu.SMEM)
    vmem = pl.BlockSpec(memory_space=pltpu.VMEM)
    pair = jax.ShapeDtypeStruct((2 * E_DEV, 2 * DOF), BF16)
    return pl.pallas_call(
        spectral_kernel,
        out_shape=(jax.ShapeDtypeStruct((256, 128), F32), pair, pair),
        in_specs=[smem, smem] + [vmem] * 4 + [pl.BlockSpec(memory_space=pl.ANY)],
        out_specs=(vmem,) * 3,
        compiler_params=pltpu.CompilerParams(vmem_limit_bytes=4 * MIB),
        name="spectral",
    )(frequency, viscosity, received, own, left, right, far)


def vector_tiles(elem):
    p = [elem[:, q * 128 : (q + 1) * 128] for q in range(5)]
    low = lane_half(E_DEV)
    zero = jnp.zeros((E_DEV, 128), F32)
    s = [p[0], p[1], jnp.where(low, p[2], zero), jnp.where(low, zero, swap(p[0])), join(p[0], p[1]), join(p[1], p[2])]
    d = [join(p[2], p[3]), join(p[3], p[4]), jnp.where(low, swap(p[4]), zero), jnp.where(low, zero, p[2]), p[3], p[4]]
    return s, d


def jacobian_kernel(jac_hbm, elem_ref, after_ref, out_ref, held, weights, acc, rows, sems):
    def piece(c, start):
        return pltpu.make_async_copy(jac_hbm.at[0, :, pl.ds(start, PIECE)], held.at[c], sems.at[c])

    for c in range(CHUNKS):
        piece(c, c * PIECE).start()
    s, d = vector_tiles(elem_ref[...].astype(F32))
    pad = jnp.zeros((128 - 2 * E_DEV, 128), F32)
    blocks = E_DEV // BLOCK
    turned = []
    for q in range(3):
        parts = []
        for b in range(blocks):
            parts += [s[q][b * BLOCK : (b + 1) * BLOCK], d[q][b * BLOCK : (b + 1) * BLOCK]]
        turned.append(jnp.concatenate(parts + [pad], axis=0).T)
    turned = jnp.concatenate(turned, axis=0)[:DOF]
    lane = lax.broadcasted_iota(jnp.int32, (DOF, 128), 1)
    for b in range(blocks):
        for i in range(4):
            at = turned if i == b else pltpu.roll(turned, (i - b) * 32 % 128, 1)
            at = jnp.where((lane >= 32 * i) & (lane < 32 * (i + 1)), at, 0.0)
            weights[b, DOF * i : DOF * (i + 1), :] = at.astype(BF16)
    e = lax.broadcasted_iota(jnp.int32, (BLOCK, 128), 0)
    keep = (lax.broadcasted_iota(jnp.int32, (BLOCK, 128), 1) & (BLOCK - 1)) == e

    def step(c, carry):
        piece(c, pl.multiple_of(c * PIECE, PIECE)).wait()
        for b in range(blocks):
            lhs = jnp.concatenate(
                [
                    held[c, b * BLOCK : (b + 1) * BLOCK, g * 4 * DOF : (g + 1) * 4 * DOF]
                    for g in range(GROUPS)
                ],
                axis=0,
            )
            res = jnp.dot(lhs, weights[b], preferred_element_type=F32)
            res = jnp.where(keep[None], res.reshape(GROUPS, BLOCK, 128), 0.0)
            acc[b, pl.ds(pl.multiple_of(c * GROUPS, GROUPS), GROUPS), :] = jnp.sum(res, axis=1)
        return carry

    lax.fori_loop(0, CHUNKS, step, 0)
    groups = CHUNKS * GROUPS
    lane = lax.broadcasted_iota(jnp.int32, (groups, 128), 1)
    for i in range(4):
        at = jnp.zeros((groups, 128), F32)
        for b in range(blocks):
            moved = acc[b] if i == b else pltpu.roll(acc[b], (b - i) * 32 % 128, 1)
            at = jnp.where((lane >= 32 * b) & (lane < 32 * (b + 1)), moved, at)
        rows[pl.ds(i, groups, stride=4), :] = at
    rows[DOF:, :] = jnp.zeros((384 - DOF, 128), F32)
    for q in range(3):
        back = rows[q * 128 : (q + 1) * 128, :].T
        for b in range(blocks):
            for k in range(2):
                out_ref[k * E_DEV + b * BLOCK : k * E_DEV + (b + 1) * BLOCK, q * 128 : (q + 1) * 128] = back[
                    b * 32 + k * BLOCK : b * 32 + (k + 1) * BLOCK
                ]


def jacobian_product(jacobian, elem, after):
    return pl.pallas_call(
        jacobian_kernel,
        out_shape=jax.ShapeDtypeStruct((2 * E_DEV, 384), F32),
        in_specs=[
            pl.BlockSpec(memory_space=pltpu.HBM),
            pl.BlockSpec(memory_space=pltpu.VMEM),
            pl.BlockSpec(memory_space=pl.ANY),
        ],
        out_specs=pl.BlockSpec(memory_space=pltpu.VMEM),
        scratch_shapes=[
            pltpu.VMEM((CHUNKS, E_DEV, PIECE), BF16),
            pltpu.VMEM((E_DEV // BLOCK, 4 * DOF, 128), BF16),
            pltpu.VMEM((E_DEV // BLOCK, CHUNKS * GROUPS, 128), F32),
            pltpu.VMEM((384, 128), F32),
            pltpu.SemaphoreType.DMA((CHUNKS,)),
        ],
        compiler_params=pltpu.CompilerParams(vmem_limit_bytes=49 * MIB),
        cost_estimate=pl.CostEstimate(
            flops=2 * 2 * E_DEV * DOF * DOF * 48, bytes_accessed=2 * E_DEV * DOF * DOF, transcendentals=0
        ),
        name="jacobian",
    )(jacobian, elem, after)


def split(x):
    high = x.astype(BF16)
    return high, (x - high.astype(F32)).astype(BF16)


def flux_kernel(
    me_ref, quad_ref, dev_ref, far_ref, near_ref, cls_ref, jac_ref, sel_ref, inc_ref, elem_ref, *rest
):
    tables, out_ref = rest[:-1], rest[-1]
    me = me_ref[0]
    far = far_ref[...]
    near = near_ref[...]
    cls = cls_ref[...]
    far_e = (far * 10923) >> 16
    far_l = far - far_e * 6
    near_e = (near * 10923) >> 16
    near_row = (near - near_e * 6) * E_DEV + near_e
    turn = (dev_ref[...] - me) & (N_SPACE - 1)
    block = jnp.zeros((1, SLOTS_DEV), jnp.int32)
    for at, which in enumerate((0, 7, 1, 4, 6, 5, 2, 3)):
        block = jnp.where(turn == which, at, block)
    column = block * E_DEV + far_e
    w = jnp.zeros((1, SLOTS_DEV), F32)
    for c in range(16):
        w = jnp.where(cls == c, quad_ref[c], w)
    r = lax.broadcasted_iota(jnp.int32, (SLOTS_DEV, SLOTS_DEV), 0)
    c = lax.broadcasted_iota(jnp.int32, (SLOTS_DEV, SLOTS_DEV), 1)
    both = (far_l * 512 + column).astype(F32)
    code = jnp.sum(jnp.where(r == c, both, 0.0), axis=1, keepdims=True).astype(jnp.int32)
    column_s = code & 511
    far_ls = code >> 9
    total = N_SPACE * E_DEV
    pick = (lax.broadcasted_iota(jnp.int32, (SLOTS_DEV, total), 1) == column_s).astype(F32).astype(BF16)
    table = jnp.concatenate([elem_ref[...]] + [t[...] for t in tables], axis=0)
    got = jnp.dot(pick, table, preferred_element_type=F32)
    p = [got[:, q * 128 : (q + 1) * 128] for q in range(5)]
    low = lane_half(SLOTS_DEV)
    zero = jnp.zeros((SLOTS_DEV, 128), F32)
    fields = jnp.concatenate(
        [
            jnp.concatenate([p[0], p[1], jnp.where(low, p[2], zero)], axis=1),
            jnp.concatenate([join(p[2], p[3]), join(p[3], p[4]), jnp.where(low, swap(p[4]), zero)], axis=1),
        ],
        axis=0,
    ).astype(BF16)
    sel = sel_ref[...]
    faces = jnp.dot(fields, sel, preferred_element_type=F32)
    which = jnp.concatenate([far_ls, far_ls], axis=0)
    trace = jnp.zeros((2 * SLOTS_DEV, 128), F32)
    for face in range(6):
        trace = jnp.where(which == face, faces[:, face * 128 : (face + 1) * 128], trace)
    trace = jnp.concatenate([trace[:SLOTS_DEV], trace[SLOTS_DEV:]], axis=1).astype(BF16)
    rows = lax.broadcasted_iota(jnp.int32, (6 * E_DEV, SLOTS_DEV), 0)
    spread = jnp.where(rows == near_row, w, 0.0)
    high, rest_w = split(spread)
    flux = jnp.dot(high, trace, preferred_element_type=F32) + jnp.dot(rest_w, trace, preferred_element_type=F32)
    weight_sum = jnp.sum(spread, axis=1, keepdims=True)
    lhs = jnp.concatenate(
        [
            jnp.concatenate(
                [flux[f * E_DEV : (f + 1) * E_DEV, :128], flux[f * E_DEV : (f + 1) * E_DEV, 128:]], axis=0
            )
            for f in range(6)
        ],
        axis=1,
    )
    high, rest_f = split(lhs)
    dims = (((1,), (1,)), ((), ()))
    lifted = lax.dot_general(high, sel, dims, preferred_element_type=F32) + lax.dot_general(
        rest_f, sel, dims, preferred_element_type=F32
    )
    coef = jnp.zeros((E_DEV, 384), F32)
    for f in range(6):
        coef = coef + weight_sum[f * E_DEV : (f + 1) * E_DEV] * inc_ref[f : f + 1, :]
    fields_own = vector_tiles(elem_ref[...].astype(F32))
    for k in range(2):
        own = jnp.concatenate(fields_own[k][:3], axis=1)
        rows_k = slice(k * E_DEV, (k + 1) * E_DEV)
        out_ref[rows_k, :] = jac_ref[rows_k, :] + coef * own - lifted[rows_k]


def space_terms(me, quad, dev, far, near, cls, jac_terms, elem, tables):
    sel = np.zeros((384, 768), np.float32)
    sel[:DOF] = face_selector()
    vmem = pl.BlockSpec(memory_space=pltpu.VMEM)
    return pl.pallas_call(
        flux_kernel,
        out_shape=jax.ShapeDtypeStruct((2 * E_DEV, 384), F32),
        in_specs=[pl.BlockSpec(memory_space=pltpu.SMEM)] * 2 + [vmem] * (8 + len(tables)),
        out_specs=vmem,
        compiler_params=pltpu.CompilerParams(vmem_limit_bytes=12 * MIB),
        name="space_terms",
    )(
        me, quad, dev, far, near, cls, jac_terms,
        jnp.asarray(sel, BF16), jnp.asarray(face_incidence()), elem, *tables,
    )


def final_kernel(src_ref, time_ref, space_ref, res_ref, prod_ref, scratch):
    half = E_DEV // 2
    low = lane_half(half)
    for k, out_ref in enumerate((res_ref, prod_ref)):
        for q in range(3):
            scratch[q] = space_ref[k * E_DEV : (k + 1) * E_DEV, q * 128 : (q + 1) * 128]
        even = [scratch[q, pl.ds(0, half, stride=2), :] for q in range(3)]
        odd = [scratch[q, pl.ds(1, half, stride=2), :] for q in range(3)]
        tiles = [
            even[0],
            even[1],
            jnp.where(low, even[2], swap(odd[0])),
            join(odd[0], odd[1]),
            join(odd[1], odd[2]),
        ]
        for q in range(5):
            at = time_ref[pl.ds(k * ROWS + q, half, stride=5), :] + tiles[q]
            if k == 0:
                at = src_ref[pl.ds(q, half, stride=5), :] - at
            out_ref[pl.ds(q, half, stride=5), :] = at


def finish(source, time_parts, space):
    vmem = pl.BlockSpec(memory_space=pltpu.VMEM)
    return pl.pallas_call(
        final_kernel,
        out_shape=(jax.ShapeDtypeStruct((ROWS, 128), F32),) * 2,
        in_specs=[vmem] * 3,
        out_specs=(vmem, vmem),
        scratch_shapes=[pltpu.VMEM((3, E_DEV, 128), F32)],
        compiler_params=pltpu.CompilerParams(vmem_limit_bytes=4 * MIB),
        name="finish",
    )(source, time_parts, space)


def per_device(
    harmonic_state,
    direction,
    source,
    jacobian,
    frequency,
    viscosity,
    quad_weight,
    partner_device,
    partner_face,
    local_face,
    weight_index,
):
    send, elem = prep(harmonic_state, direction)

    def over_space(x, turn):
        return lax.ppermute(x, "space", [(i, (i + turn) % N_SPACE) for i in range(N_SPACE)])

    left, right, across = over_space(elem, 1), over_space(elem, -1), over_space(elem, 4)
    received = lax.all_to_all(send, "inst", 0, 0, tiled=True)
    back, to_right, to_left = spectral_sum(frequency, viscosity, received, elem, left, right, across)
    lefts, rights = over_space(to_right, 2), over_space(to_left, -2)
    time_terms = lax.all_to_all(back, "inst", 0, 0, tiled=True)
    jac_terms = jacobian_product(jacobian, elem, to_right)
    space = space_terms(
        lax.axis_index("space").reshape(1),
        quad_weight,
        partner_device.reshape(1, SLOTS_DEV),
        partner_face,
        local_face,
        weight_index,
        jac_terms,
        elem,
        (left, right, across, lefts, rights),
    )
    residual, product = finish(source.reshape(ROWS, 128), time_terms, space)
    return residual.reshape(1, FLAT), product.reshape(1, FLAT)


def solution(mesh):
    in_specs = (
        P("inst", "space"),
        P("inst", "space"),
        P("inst", "space"),
        P("inst", "space", None),
        P(),
        P(),
        P(),
        P("inst", "space", None),
        P("inst", "space"),
        P("inst", "space"),
        P("inst", "space"),
    )
    out_specs = (P("inst", "space"), P("inst", "space"))
    return jax.shard_map(
        per_device, mesh=mesh, in_specs=in_specs, out_specs=out_specs, check_vma=False
    )
```

time: 57 us -> 48.2 us (0.85)
  the two profiles are of different devices: /device:TPU:8 before, /device:TPU:2 now
where the time goes in v2:
time: 48.2 us; the launch traced here: 47.9 us
  starting transfers between devices  27.7 us (57%)
  Pallas kernels  9.94 us (21%)
  waiting for transfers between devices  6.48 us (13%)
  between operations  2.08 us (4%)
  local copies, waits for them, and re-layouts  1.75 us (4%)
    ppermute x5, starting transfers between devices, over_space(): lax.ppermute(x, 'space', [(i, (i + turn) % N_SPACE) for i in range(N_SPAC...  12.7 us
    all_to_all x1, starting transfers between devices, per_device(): received = lax.all_to_all(send, 'inst', 0, 0, tiled=True)  7.63 us
    all_to_all x1, starting transfers between devices, per_device(): time_terms = lax.all_to_all(back, 'inst', 0, 0, tiled=True)  7.38 us
    ppermute x5, waiting for transfers between devices, over_space(): lax.ppermute(x, 'space', [(i, (i + turn) % N_SPACE) for i in range(N_SPAC...  6.48 us
    pallas_call x1, Pallas kernels, jacobian_product(): pl.pallas_call(jacobian_kernel, out_shape=jax.ShapeDtypeStruct((2 * E_DEV...  5.23 us
    pallas_call x1, Pallas kernels, space_terms(): pl.pallas_call(flux_kernel, out_shape=jax.ShapeDtypeStruct((2 * E_DEV, 38...  2.24 us
    unnamed x20, local copies, waits for them, and re-layouts  1.75 us
  transfers between devices with their start and end apart: 7, of which 3 were waited for; matrix products, arithmetic and copies ran while one was open for 0% of the time, Pallas kernels for 16%

profile of v2, /device:TPU:2, one launch (start us, length us, event | category | flops | bytes accessed | tf_op | source)
XLA Modules:
  0.0 47.9 jit_solution(18446265196885735488)
XLA Ops:
  0.6 0.0 copy-start
  0.6 0.0 copy-start.1
  0.7 0.9 %copy-done.1 = bf16[1,15360]{1,0:T(2,128)(2,1)S(1)} copy-done((bf16[1,15360]{1,0:T(2,128)(2,1)S(1)}, bf16[1,15360]{1,0:T(2,128)(2,1)}, u32[]{:S(2)}) %copy-start.1) | copy-done | bytes 30744
  1.5 0.0 copy-start.2
  1.5 0.8 %copy-done.2 = bf16[1,15360]{1,0:T(2,128)(2,1)S(1)} copy-done((bf16[1,15360]{1,0:T(2,128)(2,1)S(1)}, bf16[1,15360]{1,0:T(2,128)(2,1)}, u32[]{:S(2)}) %copy-start.2) | copy-done | bytes 30744
  2.4 0.0 copy-start.4
  2.4 0.0 copy-start.5
  2.4 0.0 copy-start.6
  2.4 0.0 copy-start.7
  2.4 0.0 copy-start.8
  2.4 0.0 copy-start.9
  2.4 0.0 copy-start.3
  2.4 0.9 %prep.1 = (bf16[256,128]{1,0:T(8,128)(2,1)}, bf16[48,640]{1,0:T(8,128)(2,1)S(1)}) custom-call(bf16[1,15360]{1,0:T(2,128)(2,1)S(1)} %copy-done.1, bf16[1,15360]{1,0:T(2,128)(2,1)S(1)} %copy-done.2), custom_call_target="tpu_custom_call" | custom-call | tf_op jit(solution)/shard_map/prep/pallas_call | solution.py:87
  3.3 7.6 %all-to-all-start = ((bf16[32,8,128]{2,1,0:T(8,128)(2,1)}), bf16[32,8,128]{2,1,0:T(8,128)(2,1)S(1)}, u32[]{:S(2)}, u32[]{:S(2)}) async-start(bf16[32,8,128]{2,1,0:T(8,128)(2,1)} %bitcast.1), calls=%async_computation | async-start | bytes 131072 | tf_op jit(solution)/shard_map/all_to_all | solution.py:418
  11.0 7.3 %collective-permute-start.2 = (bf16[48,640]{1,0:T(8,128)(2,1)S(1)}, bf16[48,640]{1,0:T(8,128)(2,1)S(1)}, u32[]{:S(2)}, u32[]{:S(2)}) collective-permute-start(bf16[48,640]{1,0:T(8,128)(2,1)S(1)} %get-tuple-element.10.own_ref.elem_ref), channel_id=1, source_target_pairs={{0,4},{1,5},{2,6},{3,7},{4,0},{5,1},{6,2},{7,3},{8,12},{9,13},{10,... | collective-permute-start | bytes 184328 | tf_op jit(solution)/shard_map/ppermute | solution.py:415
  18.2 0.1 collective-permute-start.1
  18.3 1.9 %collective-permute-start = (bf16[48,640]{1,0:T(8,128)(2,1)S(1)}, bf16[48,640]{1,0:T(8,128)(2,1)S(1)}, u32[]{:S(2)}, u32[]{:S(2)}) collective-permute-start(bf16[48,640]{1,0:T(8,128)(2,1)S(1)} %get-tuple-element.10.own_ref.elem_ref), channel_id=1, source_target_pairs={{0,1},{1,2},{2,3},{3,4},{4,5},{5,6},{6,7},{7,0},{8,9},{9,10},{10,1... | collective-permute-start | bytes 184328 | tf_op jit(solution)/shard_map/ppermute | solution.py:415
  21.6 0.0 collective-permute-done.2.far_ref.rest_2_
  21.6 2.4 %collective-permute-done.1.right_ref.rest_1_ = bf16[48,640]{1,0:T(8,128)(2,1)S(1)} collective-permute-done((bf16[48,640]{1,0:T(8,128)(2,1)S(1)}, bf16[48,640]{1,0:T(8,128)(2,1)S(1)}, u32[]{:S(2)}, u32[]{:S(2)}) %collective-permute-start.1) | collective-permute-done | bytes 61472 | tf_op jit(solution)/shard_map/ppermute | solution.py:415
  24.0 0.0 collective-permute-done.left_ref.rest_0_
  24.0 0.0 all-to-all-done
  24.0 0.8 %spectral.1 = (f32[256,128]{1,0:T(8,128)}, bf16[96,640]{1,0:T(8,128)(2,1)S(1)}, bf16[96,640]{1,0:T(8,128)(2,1)S(1)}) custom-call(f32[1]{0:T(128)S(6)} %copy.15.freq_ref, f32[1]{0:T(128)S(6)} %copy.16.visc_ref, bf16[256,128]{1,0:T(8,128)(2,1)S(1)} %bitcast.10, bf16[48,640]{1,0:T(8,128)(2,1)S(1)} %get-tuple-element.10.own_ref.elem_ref, ...), custom_call_target="tpu_custom_call" | custom-call | tf_op jit(solution)/shard_map/spectral/pallas_call | solution.py:163
  24.8 7.4 %all-to-all-start.1 = ((f32[32,8,128]{2,1,0:T(8,128)}), f32[32,8,128]{2,1,0:T(8,128)S(1)}, u32[]{:S(2)}, u32[]{:S(2)}) async-start(f32[32,8,128]{2,1,0:T(8,128)} %bitcast.3), calls=%async_computation.1 | async-start | bytes 262144 | tf_op jit(solution)/shard_map/all_to_all | solution.py:421
  32.2 3.4 %collective-permute-start.4 = (bf16[96,640]{1,0:T(8,128)(2,1)S(1)}, bf16[96,640]{1,0:T(8,128)(2,1)S(1)}, u32[]{:S(2)}, u32[]{:S(2)}) collective-permute-start(bf16[96,640]{1,0:T(8,128)(2,1)S(1)} %get-tuple-element.13), channel_id=1, source_target_pairs={{0,6},{1,7},{2,0},{3,1},{4,2},{5,3},{6,4},{7,5},{8,14},{9,15},{10,... | collective-permute-start | bytes 368648 | tf_op jit(solution)/shard_map/ppermute | solution.py:415
  35.6 0.0 collective-permute-start.3
  35.6 5.2 %jacobian.1.jac_ref = f32[96,384]{1,0:T(8,128)S(1)} custom-call(bf16[1,48,102400]{2,1,0:T(8,128)(2,1)} %jac_hbm.1, bf16[48,640]{1,0:T(8,128)(2,1)S(1)} %get-tuple-element.10.own_ref.elem_ref, bf16[96,640]{1,0:T(8,128)(2,1)S(1)} %get-tuple-element.12.after_ref), custom_call_target="tpu_custom_call" | custom-call | flops 943718400 | bytes 9830400 | tf_op jit(solution)/shard_map/jacobian/pallas_call | solution.py:242
  40.8 0.4 collective-permute-done.4.rest_4_
  41.2 3.7 %collective-permute-done.3.rest_3_ = bf16[96,640]{1,0:T(8,128)(2,1)S(1)} collective-permute-done((bf16[96,640]{1,0:T(8,128)(2,1)S(1)}, bf16[96,640]{1,0:T(8,128)(2,1)S(1)}, u32[]{:S(2)}, u32[]{:S(2)}) %collective-permute-start.3) | collective-permute-done | bytes 122912 | tf_op jit(solution)/shard_map/ppermute | solution.py:415
  44.9 0.0 copy-done
  44.9 0.0 copy-done.4
  44.9 0.0 copy-done.5
  44.9 0.0 copy-done.6
  44.9 0.0 copy-done.7
  44.9 0.0 copy-done.8
  44.9 0.0 copy-done.9
  44.9 2.2 %space_terms.1.space_ref = f32[96,384]{1,0:T(8,128)S(1)} custom-call(s32[1]{0:T(128)} %bitcast.5.me_ref, f32[16]{0:T(128)S(1)} %copy-done.9, s32[1,192]{1,0:T(1,128)S(1)} %bitcast.12, s32[1,192]{1,0:T(1,128)S(1)} %copy-done.6, s32[1,192]{1,0:T(1,128)S(1)} %copy-done.7, s32[1,192]{1,0:T(1,128)S(1)} %copy-done.8, f32[96,384]{1,0:T(8,128)S(1)} %jacobian.1.jac_ref, ...), custom_call_target="tpu_custom_call" | custom-call | tf_op jit(solution)/shard_map/space_terms/pallas_call | solution.py:351
  47.2 0.0 all-to-all-done.1
  47.2 0.0 copy-done.3
  47.2 0.7 %finish.1 = (f32[120,128]{1,0:T(8,128)}, f32[120,128]{1,0:T(8,128)}) custom-call(f32[120,128]{1,0:T(8,128)S(1)} %bitcast.11, f32[256,128]{1,0:T(8,128)S(1)} %bitcast.9, f32[96,384]{1,0:T(8,128)S(1)} %space_terms.1.space_ref), custom_call_target="tpu_custom_call" | custom-call | tf_op jit(solution)/shard_map/finish/pallas_call | solution.py:388
Async XLA Ops:
  0.6 44.2 %copy-start = (bf16[384,768]{1,0:T(8,128)(2,1)S(1)}, bf16[384,768]{1,0:T(8,128)(2,1)}, u32[]{:S(2)}) copy-start(bf16[384,768]{1,0:T(8,128)(2,1)} %constant.8.clone.sel_ref) | copy-start | bytes 1769476
  0.6 0.9 %copy-start.1 = (bf16[1,15360]{1,0:T(2,128)(2,1)S(1)}, bf16[1,15360]{1,0:T(2,128)(2,1)}, u32[]{:S(2)}) copy-start(bf16[1,15360]{1,0:T(2,128)(2,1)} %s_hbm.1) | copy-start | bytes 92164
  1.5 0.8 %copy-start.2 = (bf16[1,15360]{1,0:T(2,128)(2,1)S(1)}, bf16[1,15360]{1,0:T(2,128)(2,1)}, u32[]{:S(2)}) copy-start(bf16[1,15360]{1,0:T(2,128)(2,1)} %d_hbm.1) | copy-start | bytes 92164
  2.4 42.5 %copy-start.4 = (f32[8,384]{1,0:T(8,128)S(1)}, f32[8,384]{1,0:T(8,128)}, u32[]{:S(2)}) copy-start(f32[8,384]{1,0:T(8,128)} %constant.9.clone.inc_ref) | copy-start | bytes 36868
  2.4 42.5 %copy-start.5 = (s32[1,192,1]{1,2,0:T(1,128)S(1)}, s32[1,192,1]{1,2,0:T(1,128)}, u32[]{:S(2)}) copy-start(s32[1,192,1]{1,2,0:T(1,128)} %param.20) | copy-start | bytes 2308
  2.4 42.5 %copy-start.6 = (s32[1,192]{1,0:T(1,128)S(1)}, s32[1,192]{1,0:T(1,128)}, u32[]{:S(2)}) copy-start(s32[1,192]{1,0:T(1,128)} %far_ref.1) | copy-start | bytes 2308
  2.4 42.5 %copy-start.7 = (s32[1,192]{1,0:T(1,128)S(1)}, s32[1,192]{1,0:T(1,128)}, u32[]{:S(2)}) copy-start(s32[1,192]{1,0:T(1,128)} %near_ref.1) | copy-start | bytes 2308
  2.4 42.5 %copy-start.8 = (s32[1,192]{1,0:T(1,128)S(1)}, s32[1,192]{1,0:T(1,128)}, u32[]{:S(2)}) copy-start(s32[1,192]{1,0:T(1,128)} %cls_ref.1) | copy-start | bytes 2308
  2.4 42.5 %copy-start.9 = (f32[16]{0:T(128)S(1)}, f32[16]{0:T(128)}, u32[]{:S(2)}) copy-start(f32[16]{0:T(128)} %quad_ref.1) | copy-start | bytes 196
  2.4 44.8 %copy-start.3 = (f32[1,15360]{1,0:T(1,128)S(1)}, f32[1,15360]{1,0:T(1,128)}, u32[]{:S(2)}) copy-start(f32[1,15360]{1,0:T(1,128)} %param.15) | copy-start | bytes 184324
  3.3 20.7 %all-to-all-start = ((bf16[32,8,128]{2,1,0:T(8,128)(2,1)}), bf16[32,8,128]{2,1,0:T(8,128)(2,1)S(1)}, u32[]{:S(2)}, u32[]{:S(2)}) async-start(bf16[32,8,128]{2,1,0:T(8,128)(2,1)} %bitcast.1), calls=%async_computation | async-start | bytes 131072 | tf_op jit(solution)/shard_map/all_to_all | solution.py:418
  11.0 10.6 %collective-permute-start.2 = (bf16[48,640]{1,0:T(8,128)(2,1)S(1)}, bf16[48,640]{1,0:T(8,128)(2,1)S(1)}, u32[]{:S(2)}, u32[]{:S(2)}) collective-permute-start(bf16[48,640]{1,0:T(8,128)(2,1)S(1)} %get-tuple-element.10.own_ref.elem_ref), channel_id=1, source_target_pairs={{0,4},{1,5},{2,6},{3,7},{4,0},{5,1},{6,2},{7,3},{8,12},{9,13},{10,... | collective-permute-start | bytes 184328 | tf_op jit(solution)/shard_map/ppermute | solution.py:415
  18.2 5.8 %collective-permute-start.1 = (bf16[48,640]{1,0:T(8,128)(2,1)S(1)}, bf16[48,640]{1,0:T(8,128)(2,1)S(1)}, u32[]{:S(2)}, u32[]{:S(2)}) collective-permute-start(bf16[48,640]{1,0:T(8,128)(2,1)S(1)} %get-tuple-element.10.own_ref.elem_ref), channel_id=1, source_target_pairs={{0,7},{1,0},{2,1},{3,2},{4,3},{5,4},{6,5},{7,6},{8,15},{9,8},{10,9... | collective-permute-start | bytes 184328 | tf_op jit(solution)/shard_map/ppermute | solution.py:415
  18.3 5.6 %collective-permute-start = (bf16[48,640]{1,0:T(8,128)(2,1)S(1)}, bf16[48,640]{1,0:T(8,128)(2,1)S(1)}, u32[]{:S(2)}, u32[]{:S(2)}) collective-permute-start(bf16[48,640]{1,0:T(8,128)(2,1)S(1)} %get-tuple-element.10.own_ref.elem_ref), channel_id=1, source_target_pairs={{0,1},{1,2},{2,3},{3,4},{4,5},{5,6},{6,7},{7,0},{8,9},{9,10},{10,1... | collective-permute-start | bytes 184328 | tf_op jit(solution)/shard_map/ppermute | solution.py:415
  24.8 22.4 %all-to-all-start.1 = ((f32[32,8,128]{2,1,0:T(8,128)}), f32[32,8,128]{2,1,0:T(8,128)S(1)}, u32[]{:S(2)}, u32[]{:S(2)}) async-start(f32[32,8,128]{2,1,0:T(8,128)} %bitcast.3), calls=%async_computation.1 | async-start | bytes 262144 | tf_op jit(solution)/shard_map/all_to_all | solution.py:421
  32.2 9.0 %collective-permute-start.4 = (bf16[96,640]{1,0:T(8,128)(2,1)S(1)}, bf16[96,640]{1,0:T(8,128)(2,1)S(1)}, u32[]{:S(2)}, u32[]{:S(2)}) collective-permute-start(bf16[96,640]{1,0:T(8,128)(2,1)S(1)} %get-tuple-element.13), channel_id=1, source_target_pairs={{0,6},{1,7},{2,0},{3,1},{4,2},{5,3},{6,4},{7,5},{8,14},{9,15},{10,... | collective-permute-start | bytes 368648 | tf_op jit(solution)/shard_map/ppermute | solution.py:415
  35.6 9.3 %collective-permute-start.3 = (bf16[96,640]{1,0:T(8,128)(2,1)S(1)}, bf16[96,640]{1,0:T(8,128)(2,1)S(1)}, u32[]{:S(2)}, u32[]{:S(2)}) collective-permute-start(bf16[96,640]{1,0:T(8,128)(2,1)S(1)} %get-tuple-element.12.after_ref), channel_id=1, source_target_pairs={{0,2},{1,3},{2,4},{3,5},{4,6},{5,7},{6,0},{7,1},{8,10},{9,11},{10,... | collective-permute-start | bytes 368648 | tf_op jit(solution)/shard_map/ppermute | solution.py:415

commit v3 on v2

--- a/solution.py
+++ b/solution.py
@@ -60,16 +60,27 @@
     return jnp.where(lane_half(low.shape[0]), swap(low), swap(high))
 
 
-def prep_kernel(s_hbm, d_hbm, send_ref, elem_ref, held, flat, wide, sems):
-    copies = [pltpu.make_async_copy(ref, held.at[k], sems.at[k]) for k, ref in enumerate((s_hbm, d_hbm))]
-    for copy in copies:
-        copy.start()
-    for k in range(2):
-        copies[k].wait()
+def first_kernel(mark_ref):
+    mark_ref[...] = jnp.zeros((8, 128), F32)
+
+
+def first():
+    return pl.pallas_call(
+        first_kernel,
+        out_shape=jax.ShapeDtypeStruct((8, 128), F32),
+        out_specs=pl.BlockSpec(memory_space=pltpu.VMEM),
+        compiler_params=pltpu.CompilerParams(vmem_limit_bytes=MIB),
+        cost_estimate=pl.CostEstimate(flops=4 * 10**9, bytes_accessed=0, transcendentals=0),
+        name="first",
+    )()
+
+
+def prep_kernel(mark_ref, s_ref, d_ref, lin_ref, elem_ref, flat, wide):
+    for k, ref in enumerate((s_ref, d_ref)):
         for r in range(ROWS):
-            flat[k * ROWS + r : k * ROWS + r + 1, :] = held[k, 0:1, r * 128 : (r + 1) * 128].astype(F32)
+            flat[k * ROWS + r : k * ROWS + r + 1, :] = ref[0:1, r * 128 : (r + 1) * 128].astype(F32)
     flat[2 * ROWS : 256, :] = jnp.zeros((256 - 2 * ROWS, 128), F32)
-    send_ref[...] = flat[...].astype(BF16)
+    lin_ref[...] = flat[...].astype(BF16)
     half = E_DEV // 2
     low = lane_half(half)
     s = [flat[pl.ds(q, half, stride=5), :] for q in range(5)]
@@ -83,24 +94,54 @@
         elem_ref[:, q * 128 : (q + 1) * 128] = wide[q].astype(BF16)
 
 
-def prep(state, direction):
+def prep(mark, state, direction):
+    vmem = pl.BlockSpec(memory_space=pltpu.VMEM)
     return pl.pallas_call(
         prep_kernel,
         out_shape=(
             jax.ShapeDtypeStruct((256, 128), BF16),
             jax.ShapeDtypeStruct((E_DEV, 2 * DOF), BF16),
         ),
-        in_specs=[pl.BlockSpec(memory_space=pltpu.HBM)] * 2,
-        out_specs=(pl.BlockSpec(memory_space=pltpu.VMEM),) * 2,
-        scratch_shapes=[
-            pltpu.VMEM((2, 1, FLAT), BF16),
-            pltpu.VMEM((256, 128), F32),
-            pltpu.VMEM((5, E_DEV, 128), F32),
-            pltpu.SemaphoreType.DMA((2,)),
-        ],
+        in_specs=[pl.BlockSpec(memory_space=pl.ANY), vmem, vmem],
+        out_specs=(vmem, vmem),
+        scratch_shapes=[pltpu.VMEM((256, 128), F32), pltpu.VMEM((5, E_DEV, 128), F32)],
         compiler_params=pltpu.CompilerParams(vmem_limit_bytes=4 * MIB),
         name="prep",
-    )(state, direction)
+    )(mark, state, direction)
+
+
+def hand_on_kernel(x_ref, y_ref):
+    y_ref[...] = x_ref[...]
+
+
+def hand_on(x):
+    vmem = pl.BlockSpec(memory_space=pltpu.VMEM)
+    return pl.pallas_call(
+        hand_on_kernel,
+        out_shape=jax.ShapeDtypeStruct(x.shape, x.dtype),
+        in_specs=[vmem],
+        out_specs=vmem,
+        compiler_params=pltpu.CompilerParams(vmem_limit_bytes=MIB),
+        cost_estimate=pl.CostEstimate(flops=10**10, bytes_accessed=0, transcendentals=0),
+        name="hand_on",
+    )(x)
+
+
+def pair_kernel(own_ref, across_ref, pair_ref):
+    pair_ref[:E_DEV, :] = own_ref[...]
+    pair_ref[E_DEV:, :] = across_ref[...]
+
+
+def make_pair(own, across):
+    vmem = pl.BlockSpec(memory_space=pltpu.VMEM)
+    return pl.pallas_call(
+        pair_kernel,
+        out_shape=jax.ShapeDtypeStruct((2 * E_DEV, 2 * DOF), BF16),
+        in_specs=[vmem, vmem],
+        out_specs=vmem,
+        compiler_params=pltpu.CompilerParams(vmem_limit_bytes=2 * MIB),
+        name="pair",
+    )(own, across)
 
 
 def circulant_parts():
@@ -112,18 +153,14 @@
     return first, second
 
 
-def spectral_kernel(freq_ref, visc_ref, x_ref, own_ref, left_ref, right_ref, far_ref, y_ref, to_right_ref, to_left_ref):
-    to_right_ref[:E_DEV, :] = own_ref[...]
-    to_right_ref[E_DEV:, :] = left_ref[...]
-    to_left_ref[:E_DEV, :] = own_ref[...]
-    to_left_ref[E_DEV:, :] = right_ref[...]
+def spectral_kernel(freq_ref, visc_ref, x_ref, after_ref, y_ref):
     first, second = circulant_parts()
-    freq, visc = freq_ref[0], visc_ref[0]
+    freq, visc = freq_ref[...], visc_ref[...]
     half = NT // 2
     x = x_ref[...].astype(F32).reshape(NT, 8, 128)
 
     def coef(a, b):
-        return jnp.full((8, 128), freq * float(a) + visc * float(b), F32)
+        return jnp.broadcast_to(freq * float(a) + visc * float(b), (8, 128))
 
     def part(sgn):
         c = [
@@ -156,18 +193,17 @@
         y_ref[(t + half) * 8 : (t + half + 1) * 8, :] = e - odd[t]
 
 
-def spectral_sum(frequency, viscosity, received, own, left, right, far):
-    smem = pl.BlockSpec(memory_space=pltpu.SMEM)
-    vmem = pl.BlockSpec(memory_space=pltpu.VMEM)
-    pair = jax.ShapeDtypeStruct((2 * E_DEV, 2 * DOF), BF16)
+def spectral_sum(frequency, viscosity, received, after):
+    vmem = pl.BlockSpec(memory_space=pltpu.VMEM)
     return pl.pallas_call(
         spectral_kernel,
-        out_shape=(jax.ShapeDtypeStruct((256, 128), F32), pair, pair),
-        in_specs=[smem, smem] + [vmem] * 4 + [pl.BlockSpec(memory_space=pl.ANY)],
-        out_specs=(vmem,) * 3,
+        out_shape=jax.ShapeDtypeStruct((256, 128), F32),
+        in_specs=[vmem] * 3 + [pl.BlockSpec(memory_space=pl.ANY)],
+        out_specs=vmem,
         compiler_params=pltpu.CompilerParams(vmem_limit_bytes=4 * MIB),
+        cost_estimate=pl.CostEstimate(flops=10**10, bytes_accessed=0, transcendentals=0),
         name="spectral",
-    )(frequency, viscosity, received, own, left, right, far)
+    )(frequency.reshape(1, 1), viscosity.reshape(1, 1), received, after)
 
 
 def vector_tiles(elem):
@@ -179,12 +215,7 @@
     return s, d
 
 
-def jacobian_kernel(jac_hbm, elem_ref, after_ref, out_ref, held, weights, acc, rows, sems):
-    def piece(c, start):
-        return pltpu.make_async_copy(jac_hbm.at[0, :, pl.ds(start, PIECE)], held.at[c], sems.at[c])
-
-    for c in range(CHUNKS):
-        piece(c, c * PIECE).start()
+def jacobian_kernel(jac_ref, elem_ref, after_ref, out_ref, weights, acc, rows):
     s, d = vector_tiles(elem_ref[...].astype(F32))
     pad = jnp.zeros((128 - 2 * E_DEV, 128), F32)
     blocks = E_DEV // BLOCK
@@ -205,11 +236,10 @@
     keep = (lax.broadcasted_iota(jnp.int32, (BLOCK, 128), 1) & (BLOCK - 1)) == e
 
     def step(c, carry):
-        piece(c, pl.multiple_of(c * PIECE, PIECE)).wait()
         for b in range(blocks):
             lhs = jnp.concatenate(
                 [
-                    held[c, b * BLOCK : (b + 1) * BLOCK, g * 4 * DOF : (g + 1) * 4 * DOF]
+                    jac_ref[0, b * BLOCK : (b + 1) * BLOCK, pl.ds(pl.multiple_of(c * PIECE, PIECE) + g * 4 * DOF, 4 * DOF)]
                     for g in range(GROUPS)
                 ],
                 axis=0,
@@ -243,19 +273,17 @@
         jacobian_kernel,
         out_shape=jax.ShapeDtypeStruct((2 * E_DEV, 384), F32),
         in_specs=[
-            pl.BlockSpec(memory_space=pltpu.HBM),
+            pl.BlockSpec(memory_space=pltpu.VMEM),
             pl.BlockSpec(memory_space=pltpu.VMEM),
             pl.BlockSpec(memory_space=pl.ANY),
         ],
         out_specs=pl.BlockSpec(memory_space=pltpu.VMEM),
         scratch_shapes=[
-            pltpu.VMEM((CHUNKS, E_DEV, PIECE), BF16),
             pltpu.VMEM((E_DEV // BLOCK, 4 * DOF, 128), BF16),
             pltpu.VMEM((E_DEV // BLOCK, CHUNKS * GROUPS, 128), F32),
             pltpu.VMEM((384, 128), F32),
-            pltpu.SemaphoreType.DMA((CHUNKS,)),
         ],
-        compiler_params=pltpu.CompilerParams(vmem_limit_bytes=49 * MIB),
+        compiler_params=pltpu.CompilerParams(vmem_limit_bytes=8 * MIB),
         cost_estimate=pl.CostEstimate(
             flops=2 * 2 * E_DEV * DOF * DOF * 48, bytes_accessed=2 * E_DEV * DOF * DOF, transcendentals=0
         ),
@@ -269,10 +297,10 @@
 
 
 def flux_kernel(
-    me_ref, quad_ref, dev_ref, far_ref, near_ref, cls_ref, jac_ref, sel_ref, inc_ref, elem_ref, *rest
+    quad_ref, dev_ref, far_ref, near_ref, cls_ref, jac_ref, sel_ref, inc_ref, elem_ref, *rest
 ):
     tables, out_ref = rest[:-1], rest[-1]
-    me = me_ref[0]
+    me = lax.axis_index("space")
     far = far_ref[...]
     near = near_ref[...]
     cls = cls_ref[...]
@@ -282,12 +310,12 @@
     near_row = (near - near_e * 6) * E_DEV + near_e
     turn = (dev_ref[...] - me) & (N_SPACE - 1)
     block = jnp.zeros((1, SLOTS_DEV), jnp.int32)
-    for at, which in enumerate((0, 7, 1, 4, 6, 5, 2, 3)):
+    for at, which in enumerate((0, 4, 7, 3, 1, 5, 6, 2)):
         block = jnp.where(turn == which, at, block)
     column = block * E_DEV + far_e
     w = jnp.zeros((1, SLOTS_DEV), F32)
     for c in range(16):
-        w = jnp.where(cls == c, quad_ref[c], w)
+        w = jnp.where(cls == c, quad_ref[:, c : c + 1], w)
     r = lax.broadcasted_iota(jnp.int32, (SLOTS_DEV, SLOTS_DEV), 0)
     c = lax.broadcasted_iota(jnp.int32, (SLOTS_DEV, SLOTS_DEV), 1)
     both = (far_l * 512 + column).astype(F32)
@@ -296,7 +324,7 @@
     far_ls = code >> 9
     total = N_SPACE * E_DEV
     pick = (lax.broadcasted_iota(jnp.int32, (SLOTS_DEV, total), 1) == column_s).astype(F32).astype(BF16)
-    table = jnp.concatenate([elem_ref[...]] + [t[...] for t in tables], axis=0)
+    table = jnp.concatenate([t[...] for t in tables], axis=0)
     got = jnp.dot(pick, table, preferred_element_type=F32)
     p = [got[:, q * 128 : (q + 1) * 128] for q in range(5)]
     low = lane_half(SLOTS_DEV)
@@ -344,19 +372,19 @@
         out_ref[rows_k, :] = jac_ref[rows_k, :] + coef * own - lifted[rows_k]
 
 
-def space_terms(me, quad, dev, far, near, cls, jac_terms, elem, tables):
+def space_terms(quad, dev, far, near, cls, jac_terms, elem, tables):
     sel = np.zeros((384, 768), np.float32)
     sel[:DOF] = face_selector()
     vmem = pl.BlockSpec(memory_space=pltpu.VMEM)
     return pl.pallas_call(
         flux_kernel,
         out_shape=jax.ShapeDtypeStruct((2 * E_DEV, 384), F32),
-        in_specs=[pl.BlockSpec(memory_space=pltpu.SMEM)] * 2 + [vmem] * (8 + len(tables)),
+        in_specs=[vmem] * (9 + len(tables)),
         out_specs=vmem,
         compiler_params=pltpu.CompilerParams(vmem_limit_bytes=12 * MIB),
         name="space_terms",
     )(
-        me, quad, dev, far, near, cls, jac_terms,
+        quad.reshape(1, 16), dev, far, near, cls, jac_terms,
         jnp.asarray(sel, BF16), jnp.asarray(face_incidence()), elem, *tables,
     )
 
@@ -409,19 +437,19 @@
     local_face,
     weight_index,
 ):
-    send, elem = prep(harmonic_state, direction)
+    lin, elem = prep(first(), harmonic_state, direction)
 
     def over_space(x, turn):
         return lax.ppermute(x, "space", [(i, (i + turn) % N_SPACE) for i in range(N_SPACE)])
 
-    left, right, across = over_space(elem, 1), over_space(elem, -1), over_space(elem, 4)
-    received = lax.all_to_all(send, "inst", 0, 0, tiled=True)
-    back, to_right, to_left = spectral_sum(frequency, viscosity, received, elem, left, right, across)
-    lefts, rights = over_space(to_right, 2), over_space(to_left, -2)
+    across = over_space(elem, 4)
+    received = lax.all_to_all(hand_on(lin), "inst", 0, 0, tiled=True)
+    pair = make_pair(elem, across)
+    others = [over_space(pair, turn) for turn in (1, -1, 2)]
+    back = spectral_sum(frequency, viscosity, received, pair)
     time_terms = lax.all_to_all(back, "inst", 0, 0, tiled=True)
-    jac_terms = jacobian_product(jacobian, elem, to_right)
+    jac_terms = jacobian_product(jacobian, elem, back)
     space = space_terms(
-        lax.axis_index("space").reshape(1),
         quad_weight,
         partner_device.reshape(1, SLOTS_DEV),
         partner_face,
@@ -429,7 +457,7 @@
         weight_index,
         jac_terms,
         elem,
-        (left, right, across, lefts, rights),
+        [pair] + others,
     )
     residual, product = finish(source.reshape(ROWS, 128), time_terms, space)
     return residual.reshape(1, FLAT), product.reshape(1, FLAT)

time: 48.2 us -> 45.6 us (0.946)
  the two profiles are of different devices: /device:TPU:2 before, /device:TPU:1 now
where the time goes in v3:
time: 45.6 us; the launch traced here: 44.7 us
  starting transfers between devices  27.9 us (61%)
  Pallas kernels  8.15 us (18%)
  local copies, waits for them, and re-layouts  4.67 us (10%)
  between operations  2.1 us (5%)
  waiting for transfers between devices  1.86 us (4%)
    ppermute x4, starting transfers between devices, over_space(): lax.ppermute(x, 'space', [(i, (i + turn) % N_SPACE) for i in range(N_SPAC...  11.3 us
    all_to_all x1, starting transfers between devices, per_device(): received = lax.all_to_all(hand_on(lin), 'inst', 0, 0, tiled=True)  8.59 us
    all_to_all x1, starting transfers between devices, per_device(): time_terms = lax.all_to_all(back, 'inst', 0, 0, tiled=True)  8 us
    unnamed x22, local copies, waits for them, and re-layouts  4.67 us
    pallas_call x1, Pallas kernels, jacobian_product(): pl.pallas_call(jacobian_kernel, out_shape=jax.ShapeDtypeStruct((2 * E_DEV...  3.98 us
    ppermute x4, waiting for transfers between devices, over_space(): lax.ppermute(x, 'space', [(i, (i + turn) % N_SPACE) for i in range(N_SPAC...  1.86 us
    pallas_call x1, Pallas kernels, space_terms(): pl.pallas_call(flux_kernel, out_shape=jax.ShapeDtypeStruct((2 * E_DEV, 38...  1.72 us
  transfers between devices with their start and end apart: 6, of which 2 were waited for; matrix products, arithmetic and copies ran while one was open for 0% of the time, Pallas kernels for 13%

profile of v3, /device:TPU:1, one launch (start us, length us, event | category | flops | bytes accessed | tf_op | source)
XLA Modules:
  0.0 44.7 jit_solution(6433400861580652756)
XLA Ops:
  0.6 0.0 copy-start.3
  0.6 0.0 copy-start.2
  0.7 0.8 %copy-done.3 = bf16[1,15360]{1,0:T(2,128)(2,1)S(1)} copy-done((bf16[1,15360]{1,0:T(2,128)(2,1)S(1)}, bf16[1,15360]{1,0:T(2,128)(2,1)}, u32[]{:S(2)}) %copy-start.3) | copy-done | bytes 30744
  1.5 0.0 copy-done.2
  1.5 0.2 prep.1
  1.7 0.6 %hand_on.1 = bf16[256,128]{1,0:T(8,128)(2,1)} custom-call(bf16[256,128]{1,0:T(8,128)(2,1)S(1)} %get-tuple-element.6.x_ref), custom_call_target="tpu_custom_call" | custom-call | flops 10000000000 | tf_op jit(solution)/shard_map/hand_on/pallas_call | solution.py:119
  2.3 8.6 %all-to-all-start = ((bf16[32,8,128]{2,1,0:T(8,128)(2,1)}), bf16[32,8,128]{2,1,0:T(8,128)(2,1)S(1)}, u32[]{:S(2)}, u32[]{:S(2)}) async-start(bf16[32,8,128]{2,1,0:T(8,128)(2,1)} %bitcast.3), calls=%async_computation | async-start | bytes 131072 | tf_op jit(solution)/shard_map/all_to_all | solution.py:446
  10.9 7.0 %collective-permute-start = (bf16[48,640]{1,0:T(8,128)(2,1)S(1)}, bf16[48,640]{1,0:T(8,128)(2,1)S(1)}, u32[]{:S(2)}, u32[]{:S(2)}) collective-permute-start(bf16[48,640]{1,0:T(8,128)(2,1)S(1)} %get-tuple-element.7.own_ref.elem_ref), channel_id=1, source_target_pairs={{0,4},{1,5},{2,6},{3,7},{4,0},{5,1},{6,2},{7,3},{8,12},{9,13},{10,... | collective-permute-start | bytes 184328 | tf_op jit(solution)/shard_map/ppermute | solution.py:443
  19.2 0.9 %collective-permute-done.across_ref = bf16[48,640]{1,0:T(8,128)(2,1)S(1)} collective-permute-done((bf16[48,640]{1,0:T(8,128)(2,1)S(1)}, bf16[48,640]{1,0:T(8,128)(2,1)S(1)}, u32[]{:S(2)}, u32[]{:S(2)}) %collective-permute-start) | collective-permute-done | bytes 61472 | tf_op jit(solution)/shard_map/ppermute | solution.py:443
  20.1 0.0 all-to-all-done
  20.1 0.0 copy-start.1
  20.2 0.9 %spectral.1.after_ref = f32[256,128]{1,0:T(8,128)} custom-call(f32[1,1]{1,0:T(1,128)} %bitcast.11.freq_ref, f32[1,1]{1,0:T(1,128)} %bitcast.12.visc_ref, bf16[256,128]{1,0:T(8,128)(2,1)S(1)} %bitcast.14, bf16[96,640]{1,0:T(8,128)(2,1)S(1)} %pair.1.after_ref.rest_0_), custom_call_target="tpu_custom_call" | custom-call | flops 10000000000 | tf_op jit(solution)/shard_map/spectral/pallas_call | solution.py:198
  21.0 0.0 copy-start.5
  21.0 0.0 copy-start.6
  21.0 0.0 copy-start.7
  21.1 0.0 copy-start.8
  21.1 0.0 copy-start.9
  21.1 0.0 copy-start.10
  21.1 0.0 copy-start.4
  21.1 8.0 %all-to-all-start.1 = ((f32[32,8,128]{2,1,0:T(8,128)}), f32[32,8,128]{2,1,0:T(8,128)S(1)}, u32[]{:S(2)}, u32[]{:S(2)}) async-start(f32[32,8,128]{2,1,0:T(8,128)} %bitcast.5), calls=%async_computation.1 | async-start | bytes 262144 | tf_op jit(solution)/shard_map/all_to_all | solution.py:450
  29.1 2.8 %collective-permute-start.3 = (bf16[96,640]{1,0:T(8,128)(2,1)S(1)}, bf16[96,640]{1,0:T(8,128)(2,1)S(1)}, u32[]{:S(2)}, u32[]{:S(2)}) collective-permute-start(bf16[96,640]{1,0:T(8,128)(2,1)S(1)} %pair.1.after_ref.rest_0_), channel_id=1, source_target_pairs={{0,2},{1,3},{2,4},{3,5},{4,6},{5,7},{6,0},{7,1},{8,10},{9,11},{10,... | collective-permute-start | bytes 368648 | tf_op jit(solution)/shard_map/ppermute | solution.py:443
  31.9 1.5 %collective-permute-start.2 = (bf16[96,640]{1,0:T(8,128)(2,1)S(1)}, bf16[96,640]{1,0:T(8,128)(2,1)S(1)}, u32[]{:S(2)}, u32[]{:S(2)}) collective-permute-start(bf16[96,640]{1,0:T(8,128)(2,1)S(1)} %pair.1.after_ref.rest_0_), channel_id=1, source_target_pairs={{0,7},{1,0},{2,1},{3,2},{4,3},{5,4},{6,5},{7,6},{8,15},{9,8},{10,9... | collective-permute-start | bytes 368648 | tf_op jit(solution)/shard_map/ppermute | solution.py:443
  33.4 0.0 collective-permute-start.1
  33.4 0.0 copy-start
  33.4 3.8 %copy-done = bf16[1,48,102400]{2,1,0:T(8,128)(2,1)S(1)} copy-done((bf16[1,48,102400]{2,1,0:T(8,128)(2,1)S(1)}, bf16[1,48,102400]{2,1,0:T(8,128)(2,1)}, u32[]{:S(2)}) %copy-start) | copy-done | bytes 9830424
  37.2 4.0 %jacobian.1.jac_ref = f32[96,384]{1,0:T(8,128)S(1)} custom-call(bf16[1,48,102400]{2,1,0:T(8,128)(2,1)S(1)} %copy-done, bf16[48,640]{1,0:T(8,128)(2,1)S(1)} %get-tuple-element.7.own_ref.elem_ref, f32[256,128]{1,0:T(8,128)} %spectral.1.after_ref), custom_call_target="tpu_custom_call" | custom-call | flops 943718400 | bytes 9830400 | tf_op jit(solution)/shard_map/jacobian/pallas_call | solution.py:272
  41.2 0.0 collective-permute-done.3.rest_3_
  41.2 0.0 collective-permute-done.2.rest_2_
  41.2 0.9 %collective-permute-done.1.rest_1_ = bf16[96,640]{1,0:T(8,128)(2,1)S(1)} collective-permute-done((bf16[96,640]{1,0:T(8,128)(2,1)S(1)}, bf16[96,640]{1,0:T(8,128)(2,1)S(1)}, u32[]{:S(2)}, u32[]{:S(2)}) %collective-permute-start.1) | collective-permute-done | bytes 122912 | tf_op jit(solution)/shard_map/ppermute | solution.py:443
  42.1 0.0 copy-done.1
  42.2 0.0 copy-done.5
  42.2 0.0 copy-done.6
  42.2 0.0 copy-done.7
  42.2 0.0 copy-done.8
  42.2 0.0 copy-done.9
  42.2 0.0 copy-done.10
  42.2 1.7 %space_terms.1.space_ref = f32[96,384]{1,0:T(8,128)S(1)} custom-call(f32[1,16]{1,0:T(1,128)S(1)} %bitcast.17, s32[1,192]{1,0:T(1,128)S(1)} %bitcast.16, s32[1,192]{1,0:T(1,128)S(1)} %copy-done.7, s32[1,192]{1,0:T(1,128)S(1)} %copy-done.8, s32[1,192]{1,0:T(1,128)S(1)} %copy-done.9, f32[96,384]{1,0:T(8,128)S(1)} %jacobian.1.jac_ref, ...), custom_call_target="tpu_custom_call" | custom-call | tf_op jit(solution)/shard_map/space_terms/pallas_call | solution.py:379
  43.9 0.0 all-to-all-done.1
  43.9 0.0 copy-done.4
  43.9 0.7 %finish.1 = (f32[120,128]{1,0:T(8,128)}, f32[120,128]{1,0:T(8,128)}) custom-call(f32[120,128]{1,0:T(8,128)S(1)} %bitcast.15, f32[256,128]{1,0:T(8,128)S(1)} %bitcast.13, f32[96,384]{1,0:T(8,128)S(1)} %space_terms.1.space_ref), custom_call_target="tpu_custom_call" | custom-call | tf_op jit(solution)/shard_map/finish/pallas_call | solution.py:416
  (2 shorter events, 0.0 us)
Async XLA Ops:
  0.6 0.8 %copy-start.3 = (bf16[1,15360]{1,0:T(2,128)(2,1)S(1)}, bf16[1,15360]{1,0:T(2,128)(2,1)}, u32[]{:S(2)}) copy-start(bf16[1,15360]{1,0:T(2,128)(2,1)} %d_ref.1) | copy-start | bytes 92164
  0.6 0.9 %copy-start.2 = (bf16[1,15360]{1,0:T(2,128)(2,1)S(1)}, bf16[1,15360]{1,0:T(2,128)(2,1)}, u32[]{:S(2)}) copy-start(bf16[1,15360]{1,0:T(2,128)(2,1)} %s_ref.1) | copy-start | bytes 92164
  2.3 17.8 %all-to-all-start = ((bf16[32,8,128]{2,1,0:T(8,128)(2,1)}), bf16[32,8,128]{2,1,0:T(8,128)(2,1)S(1)}, u32[]{:S(2)}, u32[]{:S(2)}) async-start(bf16[32,8,128]{2,1,0:T(8,128)(2,1)} %bitcast.3), calls=%async_computation | async-start | bytes 131072 | tf_op jit(solution)/shard_map/all_to_all | solution.py:446
  10.9 9.2 %collective-permute-start = (bf16[48,640]{1,0:T(8,128)(2,1)S(1)}, bf16[48,640]{1,0:T(8,128)(2,1)S(1)}, u32[]{:S(2)}, u32[]{:S(2)}) collective-permute-start(bf16[48,640]{1,0:T(8,128)(2,1)S(1)} %get-tuple-element.7.own_ref.elem_ref), channel_id=1, source_target_pairs={{0,4},{1,5},{2,6},{3,7},{4,0},{5,1},{6,2},{7,3},{8,12},{9,13},{10,... | collective-permute-start | bytes 184328 | tf_op jit(solution)/shard_map/ppermute | solution.py:443
  20.1 22.0 %copy-start.1 = (bf16[384,768]{1,0:T(8,128)(2,1)S(1)}, bf16[384,768]{1,0:T(8,128)(2,1)}, u32[]{:S(2)}) copy-start(bf16[384,768]{1,0:T(8,128)(2,1)} %constant.4.clone.sel_ref) | copy-start | bytes 1769476
  21.0 21.1 %copy-start.5 = (f32[8,384]{1,0:T(8,128)S(1)}, f32[8,384]{1,0:T(8,128)}, u32[]{:S(2)}) copy-start(f32[8,384]{1,0:T(8,128)} %constant.5.clone.inc_ref) | copy-start | bytes 36868
  21.0 21.1 %copy-start.6 = (s32[1,192,1]{1,2,0:T(1,128)S(1)}, s32[1,192,1]{1,2,0:T(1,128)}, u32[]{:S(2)}) copy-start(s32[1,192,1]{1,2,0:T(1,128)} %param.20) | copy-start | bytes 2308
  21.0 21.1 %copy-start.7 = (s32[1,192]{1,0:T(1,128)S(1)}, s32[1,192]{1,0:T(1,128)}, u32[]{:S(2)}) copy-start(s32[1,192]{1,0:T(1,128)} %far_ref.1) | copy-start | bytes 2308
  21.1 21.1 %copy-start.8 = (s32[1,192]{1,0:T(1,128)S(1)}, s32[1,192]{1,0:T(1,128)}, u32[]{:S(2)}) copy-start(s32[1,192]{1,0:T(1,128)} %near_ref.1) | copy-start | bytes 2308
  21.1 21.1 %copy-start.9 = (s32[1,192]{1,0:T(1,128)S(1)}, s32[1,192]{1,0:T(1,128)}, u32[]{:S(2)}) copy-start(s32[1,192]{1,0:T(1,128)} %cls_ref.1) | copy-start | bytes 2308
  21.1 21.1 %copy-start.10 = (f32[16]{0:T(128)S(1)}, f32[16]{0:T(128)}, u32[]{:S(2)}) copy-start(f32[16]{0:T(128)} %param.19) | copy-start | bytes 196
  21.1 22.9 %copy-start.4 = (f32[1,15360]{1,0:T(1,128)S(1)}, f32[1,15360]{1,0:T(1,128)}, u32[]{:S(2)}) copy-start(f32[1,15360]{1,0:T(1,128)} %param.15) | copy-start | bytes 184324
  21.1 22.8 %all-to-all-start.1 = ((f32[32,8,128]{2,1,0:T(8,128)}), f32[32,8,128]{2,1,0:T(8,128)S(1)}, u32[]{:S(2)}, u32[]{:S(2)}) async-start(f32[32,8,128]{2,1,0:T(8,128)} %bitcast.5), calls=%async_computation.1 | async-start | bytes 262144 | tf_op jit(solution)/shard_map/all_to_all | solution.py:450
  29.1 12.1 %collective-permute-start.3 = (bf16[96,640]{1,0:T(8,128)(2,1)S(1)}, bf16[96,640]{1,0:T(8,128)(2,1)S(1)}, u32[]{:S(2)}, u32[]{:S(2)}) collective-permute-start(bf16[96,640]{1,0:T(8,128)(2,1)S(1)} %pair.1.after_ref.rest_0_), channel_id=1, source_target_pairs={{0,2},{1,3},{2,4},{3,5},{4,6},{5,7},{6,0},{7,1},{8,10},{9,11},{10,... | collective-permute-start | bytes 368648 | tf_op jit(solution)/shard_map/ppermute | solution.py:443
  31.9 9.3 %collective-permute-start.2 = (bf16[96,640]{1,0:T(8,128)(2,1)S(1)}, bf16[96,640]{1,0:T(8,128)(2,1)S(1)}, u32[]{:S(2)}, u32[]{:S(2)}) collective-permute-start(bf16[96,640]{1,0:T(8,128)(2,1)S(1)} %pair.1.after_ref.rest_0_), channel_id=1, source_target_pairs={{0,7},{1,0},{2,1},{3,2},{4,3},{5,4},{6,5},{7,6},{8,15},{9,8},{10,9... | collective-permute-start | bytes 368648 | tf_op jit(solution)/shard_map/ppermute | solution.py:443
  33.4 8.7 %collective-permute-start.1 = (bf16[96,640]{1,0:T(8,128)(2,1)S(1)}, bf16[96,640]{1,0:T(8,128)(2,1)S(1)}, u32[]{:S(2)}, u32[]{:S(2)}) collective-permute-start(bf16[96,640]{1,0:T(8,128)(2,1)S(1)} %pair.1.after_ref.rest_0_), channel_id=1, source_target_pairs={{0,1},{1,2},{2,3},{3,4},{4,5},{5,6},{6,7},{7,0},{8,9},{9,10},{10,1... | collective-permute-start | bytes 368648 | tf_op jit(solution)/shard_map/ppermute | solution.py:443
  33.4 3.8 %copy-start = (bf16[1,48,102400]{2,1,0:T(8,128)(2,1)S(1)}, bf16[1,48,102400]{2,1,0:T(8,128)(2,1)}, u32[]{:S(2)}) copy-start(bf16[1,48,102400]{2,1,0:T(8,128)(2,1)} %jac_ref.1) | copy-start | bytes 29491204

commit v4 on v3

--- a/solution.py
+++ b/solution.py
@@ -15,10 +15,11 @@
 NT = 32
 FLAT = E_DEV * DOF
 ROWS = FLAT // 128
-CHUNKS = 5
-GROUPS = 16
+CHUNKS = 10
+GROUPS = 8
 BLOCK = 16
 PIECE = GROUPS * 4 * DOF
+SPARE = 16
 MIB = 1024 * 1024
 F32 = jnp.float32
 BF16 = jnp.bfloat16
@@ -91,7 +92,8 @@
         wide[q, pl.ds(0, half, stride=2), :] = even[q]
         wide[q, pl.ds(1, half, stride=2), :] = odd[q]
     for q in range(5):
-        elem_ref[:, q * 128 : (q + 1) * 128] = wide[q].astype(BF16)
+        elem_ref[:E_DEV, q * 128 : (q + 1) * 128] = wide[q].astype(BF16)
+    elem_ref[E_DEV:, :] = jnp.zeros((SPARE, 2 * DOF), BF16)
 
 
 def prep(mark, state, direction):
@@ -100,7 +102,7 @@
         prep_kernel,
         out_shape=(
             jax.ShapeDtypeStruct((256, 128), BF16),
-            jax.ShapeDtypeStruct((E_DEV, 2 * DOF), BF16),
+            jax.ShapeDtypeStruct((E_DEV + SPARE, 2 * DOF), BF16),
         ),
         in_specs=[pl.BlockSpec(memory_space=pl.ANY), vmem, vmem],
         out_specs=(vmem, vmem),
@@ -110,33 +112,17 @@
     )(mark, state, direction)
 
 
-def hand_on_kernel(x_ref, y_ref):
-    y_ref[...] = x_ref[...]
-
-
-def hand_on(x):
-    vmem = pl.BlockSpec(memory_space=pltpu.VMEM)
-    return pl.pallas_call(
-        hand_on_kernel,
-        out_shape=jax.ShapeDtypeStruct(x.shape, x.dtype),
-        in_specs=[vmem],
-        out_specs=vmem,
-        compiler_params=pltpu.CompilerParams(vmem_limit_bytes=MIB),
-        cost_estimate=pl.CostEstimate(flops=10**10, bytes_accessed=0, transcendentals=0),
-        name="hand_on",
-    )(x)
-
-
 def pair_kernel(own_ref, across_ref, pair_ref):
-    pair_ref[:E_DEV, :] = own_ref[...]
-    pair_ref[E_DEV:, :] = across_ref[...]
+    pair_ref[:E_DEV, :] = own_ref[:E_DEV, :]
+    pair_ref[E_DEV : 2 * E_DEV, :] = across_ref[:E_DEV, :]
+    pair_ref[2 * E_DEV :, :] = jnp.zeros((SPARE, 2 * DOF), BF16)
 
 
 def make_pair(own, across):
     vmem = pl.BlockSpec(memory_space=pltpu.VMEM)
     return pl.pallas_call(
         pair_kernel,
-        out_shape=jax.ShapeDtypeStruct((2 * E_DEV, 2 * DOF), BF16),
+        out_shape=jax.ShapeDtypeStruct((2 * E_DEV + SPARE, 2 * DOF), BF16),
         in_specs=[vmem, vmem],
         out_specs=vmem,
         compiler_params=pltpu.CompilerParams(vmem_limit_bytes=2 * MIB),
@@ -215,8 +201,13 @@
     return s, d
 
 
-def jacobian_kernel(jac_ref, elem_ref, after_ref, out_ref, weights, acc, rows):
-    s, d = vector_tiles(elem_ref[...].astype(F32))
+def jacobian_kernel(jac_hbm, elem_ref, after_ref, out_ref, held, weights, acc, rows, sems):
+    def piece(c, start):
+        return pltpu.make_async_copy(jac_hbm.at[0, :, pl.ds(start, PIECE)], held.at[c], sems.at[c])
+
+    for c in range(CHUNKS):
+        piece(c, c * PIECE).start()
+    s, d = vector_tiles(elem_ref[:E_DEV, :].astype(F32))
     pad = jnp.zeros((128 - 2 * E_DEV, 128), F32)
     blocks = E_DEV // BLOCK
     turned = []
@@ -236,10 +227,11 @@
     keep = (lax.broadcasted_iota(jnp.int32, (BLOCK, 128), 1) & (BLOCK - 1)) == e
 
     def step(c, carry):
+        piece(c, pl.multiple_of(c * PIECE, PIECE)).wait()
         for b in range(blocks):
             lhs = jnp.concatenate(
                 [
-                    jac_ref[0, b * BLOCK : (b + 1) * BLOCK, pl.ds(pl.multiple_of(c * PIECE, PIECE) + g * 4 * DOF, 4 * DOF)]
+                    held[c, b * BLOCK : (b + 1) * BLOCK, g * 4 * DOF : (g + 1) * 4 * DOF]
                     for g in range(GROUPS)
                 ],
                 axis=0,
@@ -273,17 +265,19 @@
         jacobian_kernel,
         out_shape=jax.ShapeDtypeStruct((2 * E_DEV, 384), F32),
         in_specs=[
-            pl.BlockSpec(memory_space=pltpu.VMEM),
+            pl.BlockSpec(memory_space=pltpu.HBM),
             pl.BlockSpec(memory_space=pltpu.VMEM),
             pl.BlockSpec(memory_space=pl.ANY),
         ],
         out_specs=pl.BlockSpec(memory_space=pltpu.VMEM),
         scratch_shapes=[
+            pltpu.VMEM((CHUNKS, E_DEV, PIECE), BF16),
             pltpu.VMEM((E_DEV // BLOCK, 4 * DOF, 128), BF16),
             pltpu.VMEM((E_DEV // BLOCK, CHUNKS * GROUPS, 128), F32),
             pltpu.VMEM((384, 128), F32),
+            pltpu.SemaphoreType.DMA((CHUNKS,)),
         ],
-        compiler_params=pltpu.CompilerParams(vmem_limit_bytes=8 * MIB),
+        compiler_params=pltpu.CompilerParams(vmem_limit_bytes=49 * MIB),
         cost_estimate=pl.CostEstimate(
             flops=2 * 2 * E_DEV * DOF * DOF * 48, bytes_accessed=2 * E_DEV * DOF * DOF, transcendentals=0
         ),
@@ -324,7 +318,7 @@
     far_ls = code >> 9
     total = N_SPACE * E_DEV
     pick = (lax.broadcasted_iota(jnp.int32, (SLOTS_DEV, total), 1) == column_s).astype(F32).astype(BF16)
-    table = jnp.concatenate([t[...] for t in tables], axis=0)
+    table = jnp.concatenate([t[: 2 * E_DEV, :] for t in tables], axis=0)
     got = jnp.dot(pick, table, preferred_element_type=F32)
     p = [got[:, q * 128 : (q + 1) * 128] for q in range(5)]
     low = lane_half(SLOTS_DEV)
@@ -365,7 +359,7 @@
     coef = jnp.zeros((E_DEV, 384), F32)
     for f in range(6):
         coef = coef + weight_sum[f * E_DEV : (f + 1) * E_DEV] * inc_ref[f : f + 1, :]
-    fields_own = vector_tiles(elem_ref[...].astype(F32))
+    fields_own = vector_tiles(elem_ref[:E_DEV, :].astype(F32))
     for k in range(2):
         own = jnp.concatenate(fields_own[k][:3], axis=1)
         rows_k = slice(k * E_DEV, (k + 1) * E_DEV)
@@ -443,7 +437,7 @@
         return lax.ppermute(x, "space", [(i, (i + turn) % N_SPACE) for i in range(N_SPACE)])
 
     across = over_space(elem, 4)
-    received = lax.all_to_all(hand_on(lin), "inst", 0, 0, tiled=True)
+    received = lax.all_to_all(lin, "inst", 0, 0, tiled=True)
     pair = make_pair(elem, across)
     others = [over_space(pair, turn) for turn in (1, -1, 2)]
     back = spectral_sum(frequency, viscosity, received, pair)

time: 45.6 us -> 40.3 us (0.88); the launches traced: 44.7 us -> 40 us
  local copies, waits for them, and re-layouts: 4.67 us -> 0.87 us
  starting transfers between devices: 27.9 us -> 24.3 us
  Pallas kernels: 8.15 us -> 9.9 us
  waiting for transfers between devices: 1.86 us -> 2.8 us
    unnamed x22 -> x20, local copies, waits for them, and re-layouts: 4.67 us -> 0.87 us
    all_to_all x1, waiting for transfers between devices: 0.01 us -> 2.78 us  [per_device(): received = lax.all_to_all(lin, 'inst', 0, 0, tiled=True)]
    all_to_all x1, starting transfers between devices: 8 us -> 5.31 us  [per_device(): time_terms = lax.all_to_all(back, 'inst', 0, 0, tiled=True)]
    ppermute x4, waiting for transfers between devices: 1.86 us -> 0.01 us  [over_space(): lax.ppermute(x, 'space', [(i, (i + turn) % N_SPACE) for i in range(N_SPAC...]
    pallas_call x1, Pallas kernels: 3.98 us -> 5.79 us  [jacobian_product(): pl.pallas_call(jacobian_kernel, out_shape=jax.ShapeDtypeStruct((2 * E_DEV...]
    pallas_call x2 -> x1, Pallas kernels: 0.63 us -> 0.01 us  [make_pair(): pl.pallas_call(pair_kernel, out_shape=jax.ShapeDtypeStruct((2 * E_DEV + S...]
    pallas_call x1, Pallas kernels: 0.18 us -> 0.73 us  [prep(): pl.pallas_call(prep_kernel, out_shape=(jax.ShapeDtypeStruct((256, 128), B...]
    all_to_all x1, starting transfers between devices: 8.59 us -> 8.04 us  [per_device(): received = lax.all_to_all(lin, 'inst', 0, 0, tiled=True)]
  transfers between devices with their start and end apart: 6 -> 6, of which waited for: 2 -> 1; matrix products, arithmetic and copies ran while one was open for 0% -> 0% of each run, Pallas kernels for 13% -> 21%
where the time goes in v4:
time: 40.3 us; the launch traced here: 40 us
  starting transfers between devices  24.3 us (60%)
  Pallas kernels  9.9 us (25%)
  waiting for transfers between devices  2.8 us (7%)
  between operations  2.13 us (5%)
  local copies, waits for them, and re-layouts  0.87 us (2%)
    ppermute x4, starting transfers between devices, over_space(): lax.ppermute(x, 'space', [(i, (i + turn) % N_SPACE) for i in range(N_SPAC...  10.9 us
    all_to_all x1, starting transfers between devices, per_device(): received = lax.all_to_all(lin, 'inst', 0, 0, tiled=True)  8.04 us
    pallas_call x1, Pallas kernels, jacobian_product(): pl.pallas_call(jacobian_kernel, out_shape=jax.ShapeDtypeStruct((2 * E_DEV...  5.79 us
    all_to_all x1, starting transfers between devices, per_device(): time_terms = lax.all_to_all(back, 'inst', 0, 0, tiled=True)  5.31 us
    all_to_all x1, waiting for transfers between devices, per_device(): received = lax.all_to_all(lin, 'inst', 0, 0, tiled=True)  2.78 us
    pallas_call x1, Pallas kernels, space_terms(): pl.pallas_call(flux_kernel, out_shape=jax.ShapeDtypeStruct((2 * E_DEV, 38...  1.72 us
    pallas_call x1, Pallas kernels, spectral_sum(): pl.pallas_call(spectral_kernel, out_shape=jax.ShapeDtypeStruct((256, 128)...  0.89 us
    unnamed x20, local copies, waits for them, and re-layouts  0.87 us
  transfers between devices with their start and end apart: 6, of which 1 were waited for; matrix products, arithmetic and copies ran while one was open for 0% of the time, Pallas kernels for 21%

profile of v4, /device:TPU:1, one launch (start us, length us, event | category | flops | bytes accessed | tf_op | source)
XLA Modules:
  0.0 40.0 jit_solution(13068151373816409472)
XLA Ops:
  0.6 0.0 copy-start.2
  0.6 0.0 copy-start.1
  0.7 0.8 %copy-done.2 = bf16[1,15360]{1,0:T(2,128)(2,1)S(1)} copy-done((bf16[1,15360]{1,0:T(2,128)(2,1)S(1)}, bf16[1,15360]{1,0:T(2,128)(2,1)}, u32[]{:S(2)}) %copy-start.2) | copy-done | bytes 30744
  1.5 0.0 copy-done.1
  1.5 0.7 %prep.1 = (bf16[256,128]{1,0:T(8,128)(2,1)}, bf16[64,640]{1,0:T(8,128)(2,1)S(1)}) custom-call(f32[8,128]{1,0:T(8,128)S(1)} %first.1.mark_ref, bf16[1,15360]{1,0:T(2,128)(2,1)S(1)} %copy-done.1, bf16[1,15360]{1,0:T(2,128)(2,1)S(1)} %copy-done.2), custom_call_target="tpu_custom_call" | custom-call | tf_op jit(solution)/shard_map/prep/pallas_call | solution.py:101
  2.2 7.7 %collective-permute-start = (bf16[64,640]{1,0:T(8,128)(2,1)S(1)}, bf16[64,640]{1,0:T(8,128)(2,1)S(1)}, u32[]{:S(2)}, u32[]{:S(2)}) collective-permute-start(bf16[64,640]{1,0:T(8,128)(2,1)S(1)} %get-tuple-element.7.own_ref.elem_ref), channel_id=1, source_target_pairs={{0,4},{1,5},{2,6},{3,7},{4,0},{5,1},{6,2},{7,3},{8,12},{9,13},{10,... | collective-permute-start | bytes 245768 | tf_op jit(solution)/shard_map/ppermute | solution.py:437
  10.0 8.0 %all-to-all-start = ((bf16[32,8,128]{2,1,0:T(8,128)(2,1)}), bf16[32,8,128]{2,1,0:T(8,128)(2,1)S(1)}, u32[]{:S(2)}, u32[]{:S(2)}) async-start(bf16[32,8,128]{2,1,0:T(8,128)(2,1)} %bitcast.3), calls=%async_computation | async-start | bytes 131072 | tf_op jit(solution)/shard_map/all_to_all | solution.py:440
  19.3 0.0 collective-permute-done.across_ref
  19.3 1.3 %collective-permute-start.3 = (bf16[112,640]{1,0:T(8,128)(2,1)S(1)}, bf16[112,640]{1,0:T(8,128)(2,1)S(1)}, u32[]{:S(2)}, u32[]{:S(2)}) collective-permute-start(bf16[112,640]{1,0:T(8,128)(2,1)S(1)} %pair.1.after_ref.rest_0_), channel_id=1, source_target_pairs={{0,2},{1,3},{2,4},{3,5},{4,6},{5,7},{6,0},{7,1},{8,10},{9,11},{10,... | collective-permute-start | bytes 430088 | tf_op jit(solution)/shard_map/ppermute | solution.py:437
  20.6 1.9 %collective-permute-start.2 = (bf16[112,640]{1,0:T(8,128)(2,1)S(1)}, bf16[112,640]{1,0:T(8,128)(2,1)S(1)}, u32[]{:S(2)}, u32[]{:S(2)}) collective-permute-start(bf16[112,640]{1,0:T(8,128)(2,1)S(1)} %pair.1.after_ref.rest_0_), channel_id=1, source_target_pairs={{0,7},{1,0},{2,1},{3,2},{4,3},{5,4},{6,5},{7,6},{8,15},{9,8},{10,9... | collective-permute-start | bytes 430088 | tf_op jit(solution)/shard_map/ppermute | solution.py:437
  22.5 0.0 collective-permute-start.1
  22.5 2.8 %all-to-all-done = bf16[32,8,128]{2,1,0:T(8,128)(2,1)S(1)} async-done(((bf16[32,8,128]{2,1,0:T(8,128)(2,1)}), bf16[32,8,128]{2,1,0:T(8,128)(2,1)S(1)}, u32[]{:S(2)}, u32[]{:S(2)}) %all-to-all-start) | async-done | bytes 65568 | tf_op jit(solution)/shard_map/all_to_all | solution.py:440
  25.3 0.9 %spectral.1.after_ref = f32[256,128]{1,0:T(8,128)} custom-call(f32[1,1]{1,0:T(1,128)} %bitcast.11.freq_ref, f32[1,1]{1,0:T(1,128)} %bitcast.12.visc_ref, bf16[256,128]{1,0:T(8,128)(2,1)S(1)} %bitcast.14, bf16[112,640]{1,0:T(8,128)(2,1)S(1)} %pair.1.after_ref.rest_0_), custom_call_target="tpu_custom_call" | custom-call | flops 10000000000 | tf_op jit(solution)/shard_map/spectral/pallas_call | solution.py:184
  26.2 0.0 copy-start
  26.2 0.0 copy-start.4
  26.2 0.0 copy-start.5
  26.2 0.0 copy-start.6
  26.2 0.0 copy-start.7
  26.2 0.0 copy-start.8
  26.3 0.0 copy-start.9
  26.3 0.0 copy-start.3
  26.3 5.3 %all-to-all-start.1 = ((f32[32,8,128]{2,1,0:T(8,128)}), f32[32,8,128]{2,1,0:T(8,128)S(1)}, u32[]{:S(2)}, u32[]{:S(2)}) async-start(f32[32,8,128]{2,1,0:T(8,128)} %bitcast.5), calls=%async_computation.1 | async-start | bytes 262144 | tf_op jit(solution)/shard_map/all_to_all | solution.py:444
  31.6 5.8 %jacobian.1.jac_ref = f32[96,384]{1,0:T(8,128)S(1)} custom-call(bf16[1,48,102400]{2,1,0:T(8,128)(2,1)} %jac_hbm.1, bf16[64,640]{1,0:T(8,128)(2,1)S(1)} %get-tuple-element.7.own_ref.elem_ref, f32[256,128]{1,0:T(8,128)} %spectral.1.after_ref), custom_call_target="tpu_custom_call" | custom-call | flops 943718400 | bytes 9830400 | tf_op jit(solution)/shard_map/jacobian/pallas_call | solution.py:264
  37.4 0.0 collective-permute-done.3.rest_3_
  37.4 0.0 collective-permute-done.2.rest_2_
  37.4 0.0 collective-permute-done.1.rest_1_
  37.4 0.0 copy-done
  37.4 0.0 copy-done.4
  37.4 0.0 copy-done.5
  37.5 0.0 copy-done.6
  37.5 0.0 copy-done.7
  37.5 0.0 copy-done.8
  37.5 0.0 copy-done.9
  37.5 1.7 %space_terms.1.space_ref = f32[96,384]{1,0:T(8,128)S(1)} custom-call(f32[1,16]{1,0:T(1,128)S(1)} %bitcast.17, s32[1,192]{1,0:T(1,128)S(1)} %bitcast.16, s32[1,192]{1,0:T(1,128)S(1)} %copy-done.6, s32[1,192]{1,0:T(1,128)S(1)} %copy-done.7, s32[1,192]{1,0:T(1,128)S(1)} %copy-done.8, f32[96,384]{1,0:T(8,128)S(1)} %jacobian.1.jac_ref, ...), custom_call_target="tpu_custom_call" | custom-call | tf_op jit(solution)/shard_map/space_terms/pallas_call | solution.py:373
  39.2 0.0 all-to-all-done.1
  39.2 0.0 copy-done.3
  39.2 0.7 %finish.1 = (f32[120,128]{1,0:T(8,128)}, f32[120,128]{1,0:T(8,128)}) custom-call(f32[120,128]{1,0:T(8,128)S(1)} %bitcast.15, f32[256,128]{1,0:T(8,128)S(1)} %bitcast.13, f32[96,384]{1,0:T(8,128)S(1)} %space_terms.1.space_ref), custom_call_target="tpu_custom_call" | custom-call | tf_op jit(solution)/shard_map/finish/pallas_call | solution.py:410
  (2 shorter events, 0.0 us)
Async XLA Ops:
  0.6 0.8 %copy-start.2 = (bf16[1,15360]{1,0:T(2,128)(2,1)S(1)}, bf16[1,15360]{1,0:T(2,128)(2,1)}, u32[]{:S(2)}) copy-start(bf16[1,15360]{1,0:T(2,128)(2,1)} %d_ref.1) | copy-start | bytes 92164
  0.6 0.9 %copy-start.1 = (bf16[1,15360]{1,0:T(2,128)(2,1)S(1)}, bf16[1,15360]{1,0:T(2,128)(2,1)}, u32[]{:S(2)}) copy-start(bf16[1,15360]{1,0:T(2,128)(2,1)} %s_ref.1) | copy-start | bytes 92164
  2.2 17.1 %collective-permute-start = (bf16[64,640]{1,0:T(8,128)(2,1)S(1)}, bf16[64,640]{1,0:T(8,128)(2,1)S(1)}, u32[]{:S(2)}, u32[]{:S(2)}) collective-permute-start(bf16[64,640]{1,0:T(8,128)(2,1)S(1)} %get-tuple-element.7.own_ref.elem_ref), channel_id=1, source_target_pairs={{0,4},{1,5},{2,6},{3,7},{4,0},{5,1},{6,2},{7,3},{8,12},{9,13},{10,... | collective-permute-start | bytes 245768 | tf_op jit(solution)/shard_map/ppermute | solution.py:437
  10.0 15.4 %all-to-all-start = ((bf16[32,8,128]{2,1,0:T(8,128)(2,1)}), bf16[32,8,128]{2,1,0:T(8,128)(2,1)S(1)}, u32[]{:S(2)}, u32[]{:S(2)}) async-start(bf16[32,8,128]{2,1,0:T(8,128)(2,1)} %bitcast.3), calls=%async_computation | async-start | bytes 131072 | tf_op jit(solution)/shard_map/all_to_all | solution.py:440
  19.3 18.1 %collective-permute-start.3 = (bf16[112,640]{1,0:T(8,128)(2,1)S(1)}, bf16[112,640]{1,0:T(8,128)(2,1)S(1)}, u32[]{:S(2)}, u32[]{:S(2)}) collective-permute-start(bf16[112,640]{1,0:T(8,128)(2,1)S(1)} %pair.1.after_ref.rest_0_), channel_id=1, source_target_pairs={{0,2},{1,3},{2,4},{3,5},{4,6},{5,7},{6,0},{7,1},{8,10},{9,11},{10,... | collective-permute-start | bytes 430088 | tf_op jit(solution)/shard_map/ppermute | solution.py:437
  20.6 16.8 %collective-permute-start.2 = (bf16[112,640]{1,0:T(8,128)(2,1)S(1)}, bf16[112,640]{1,0:T(8,128)(2,1)S(1)}, u32[]{:S(2)}, u32[]{:S(2)}) collective-permute-start(bf16[112,640]{1,0:T(8,128)(2,1)S(1)} %pair.1.after_ref.rest_0_), channel_id=1, source_target_pairs={{0,7},{1,0},{2,1},{3,2},{4,3},{5,4},{6,5},{7,6},{8,15},{9,8},{10,9... | collective-permute-start | bytes 430088 | tf_op jit(solution)/shard_map/ppermute | solution.py:437
  22.5 14.9 %collective-permute-start.1 = (bf16[112,640]{1,0:T(8,128)(2,1)S(1)}, bf16[112,640]{1,0:T(8,128)(2,1)S(1)}, u32[]{:S(2)}, u32[]{:S(2)}) collective-permute-start(bf16[112,640]{1,0:T(8,128)(2,1)S(1)} %pair.1.after_ref.rest_0_), channel_id=1, source_target_pairs={{0,1},{1,2},{2,3},{3,4},{4,5},{5,6},{6,7},{7,0},{8,9},{9,10},{10,1... | collective-permute-start | bytes 430088 | tf_op jit(solution)/shard_map/ppermute | solution.py:437
  26.2 11.2 %copy-start = (bf16[384,768]{1,0:T(8,128)(2,1)S(1)}, bf16[384,768]{1,0:T(8,128)(2,1)}, u32[]{:S(2)}) copy-start(bf16[384,768]{1,0:T(8,128)(2,1)} %constant.4.clone.sel_ref) | copy-start | bytes 1769476
  26.2 11.2 %copy-start.4 = (f32[8,384]{1,0:T(8,128)S(1)}, f32[8,384]{1,0:T(8,128)}, u32[]{:S(2)}) copy-start(f32[8,384]{1,0:T(8,128)} %constant.5.clone.inc_ref) | copy-start | bytes 36868
  26.2 11.2 %copy-start.5 = (s32[1,192,1]{1,2,0:T(1,128)S(1)}, s32[1,192,1]{1,2,0:T(1,128)}, u32[]{:S(2)}) copy-start(s32[1,192,1]{1,2,0:T(1,128)} %param.20) | copy-start | bytes 2308
  26.2 11.2 %copy-start.6 = (s32[1,192]{1,0:T(1,128)S(1)}, s32[1,192]{1,0:T(1,128)}, u32[]{:S(2)}) copy-start(s32[1,192]{1,0:T(1,128)} %far_ref.1) | copy-start | bytes 2308
  26.2 11.2 %copy-start.7 = (s32[1,192]{1,0:T(1,128)S(1)}, s32[1,192]{1,0:T(1,128)}, u32[]{:S(2)}) copy-start(s32[1,192]{1,0:T(1,128)} %near_ref.1) | copy-start | bytes 2308
  26.2 11.2 %copy-start.8 = (s32[1,192]{1,0:T(1,128)S(1)}, s32[1,192]{1,0:T(1,128)}, u32[]{:S(2)}) copy-start(s32[1,192]{1,0:T(1,128)} %cls_ref.1) | copy-start | bytes 2308
  26.3 11.2 %copy-start.9 = (f32[16]{0:T(128)S(1)}, f32[16]{0:T(128)}, u32[]{:S(2)}) copy-start(f32[16]{0:T(128)} %param.19) | copy-start | bytes 196
  26.3 13.0 %copy-start.3 = (f32[1,15360]{1,0:T(1,128)S(1)}, f32[1,15360]{1,0:T(1,128)}, u32[]{:S(2)}) copy-start(f32[1,15360]{1,0:T(1,128)} %param.15) | copy-start | bytes 184324
  26.3 12.9 %all-to-all-start.1 = ((f32[32,8,128]{2,1,0:T(8,128)}), f32[32,8,128]{2,1,0:T(8,128)S(1)}, u32[]{:S(2)}, u32[]{:S(2)}) async-start(f32[32,8,128]{2,1,0:T(8,128)} %bitcast.5), calls=%async_computation.1 | async-start | bytes 262144 | tf_op jit(solution)/shard_map/all_to_all | solution.py:444

commit v5 on v4

--- a/solution.py
+++ b/solution.py
@@ -15,8 +15,8 @@
 NT = 32
 FLAT = E_DEV * DOF
 ROWS = FLAT // 128
-CHUNKS = 10
-GROUPS = 8
+CHUNKS = 5
+GROUPS = 16
 BLOCK = 16
 PIECE = GROUPS * 4 * DOF
 SPARE = 16
@@ -61,19 +61,38 @@
     return jnp.where(lane_half(low.shape[0]), swap(low), swap(high))
 
 
-def first_kernel(mark_ref):
-    mark_ref[...] = jnp.zeros((8, 128), F32)
-
-
-def first():
-    return pl.pallas_call(
-        first_kernel,
-        out_shape=jax.ShapeDtypeStruct((8, 128), F32),
+def circulant_parts():
+    j = np.arange(1, NT)
+    sign = 1.0 - 2.0 * (j % 2)
+    angle = np.pi * j / NT
+    first = np.concatenate([[0.0], 0.5 * sign * np.cos(angle) / np.sin(angle)])
+    second = np.concatenate([[-(NT * NT + 2) / 12.0], -sign / (2.0 * np.sin(angle) ** 2)])
+    return first, second
+
+
+def coef_kernel(freq_ref, visc_ref, coef_ref):
+    first, second = circulant_parts()
+    freq, visc = freq_ref[0], visc_ref[0]
+    half = NT // 2
+    for part, sgn in enumerate((1.0, -1.0)):
+        for j in range(half):
+            a = 0.5 * (first[j] + sgn * first[j + half])
+            b = 0.5 * (second[j] + sgn * second[j + half])
+            row = part * half + j
+            coef_ref[row : row + 1, :] = jnp.full((1, 128), freq * float(a) + visc * float(b), F32)
+
+
+def coefficients(frequency, viscosity):
+    smem = pl.BlockSpec(memory_space=pltpu.SMEM)
+    return pl.pallas_call(
+        coef_kernel,
+        out_shape=jax.ShapeDtypeStruct((NT, 128), F32),
+        in_specs=[smem, smem],
         out_specs=pl.BlockSpec(memory_space=pltpu.VMEM),
         compiler_params=pltpu.CompilerParams(vmem_limit_bytes=MIB),
         cost_estimate=pl.CostEstimate(flops=4 * 10**9, bytes_accessed=0, transcendentals=0),
-        name="first",
-    )()
+        name="coefficients",
+    )(frequency, viscosity)
 
 
 def prep_kernel(mark_ref, s_ref, d_ref, lin_ref, elem_ref, flat, wide):
@@ -130,29 +149,13 @@
     )(own, across)
 
 
-def circulant_parts():
-    j = np.arange(1, NT)
-    sign = 1.0 - 2.0 * (j % 2)
-    angle = np.pi * j / NT
-    first = np.concatenate([[0.0], 0.5 * sign * np.cos(angle) / np.sin(angle)])
-    second = np.concatenate([[-(NT * NT + 2) / 12.0], -sign / (2.0 * np.sin(angle) ** 2)])
-    return first, second
-
-
-def spectral_kernel(freq_ref, visc_ref, x_ref, after_ref, y_ref):
-    first, second = circulant_parts()
-    freq, visc = freq_ref[...], visc_ref[...]
+def spectral_kernel(coef_ref, x_ref, after_ref, y_ref):
     half = NT // 2
     x = x_ref[...].astype(F32).reshape(NT, 8, 128)
 
-    def coef(a, b):
-        return jnp.broadcast_to(freq * float(a) + visc * float(b), (8, 128))
-
     def part(sgn):
-        c = [
-            coef(0.5 * (first[j] + sgn * first[j + half]), 0.5 * (second[j] + sgn * second[j + half]))
-            for j in range(half)
-        ]
+        base = 0 if sgn > 0 else half
+        c = [jnp.broadcast_to(coef_ref[base + j : base + j + 1, :], (8, 128)) for j in range(half)]
         u = [x[s] + sgn * x[s + half] for s in range(half)]
         out = []
         for t in range(half):
@@ -179,17 +182,17 @@
         y_ref[(t + half) * 8 : (t + half + 1) * 8, :] = e - odd[t]
 
 
-def spectral_sum(frequency, viscosity, received, after):
+def spectral_sum(coef, received, after):
     vmem = pl.BlockSpec(memory_space=pltpu.VMEM)
     return pl.pallas_call(
         spectral_kernel,
         out_shape=jax.ShapeDtypeStruct((256, 128), F32),
-        in_specs=[vmem] * 3 + [pl.BlockSpec(memory_space=pl.ANY)],
+        in_specs=[vmem] * 2 + [pl.BlockSpec(memory_space=pl.ANY)],
         out_specs=vmem,
         compiler_params=pltpu.CompilerParams(vmem_limit_bytes=4 * MIB),
-        cost_estimate=pl.CostEstimate(flops=10**10, bytes_accessed=0, transcendentals=0),
+        cost_estimate=pl.CostEstimate(flops=10**11, bytes_accessed=0, transcendentals=0),
         name="spectral",
-    )(frequency.reshape(1, 1), viscosity.reshape(1, 1), received, after)
+    )(coef, received, after)
 
 
 def vector_tiles(elem):
@@ -201,12 +204,7 @@
     return s, d
 
 
-def jacobian_kernel(jac_hbm, elem_ref, after_ref, out_ref, held, weights, acc, rows, sems):
-    def piece(c, start):
-        return pltpu.make_async_copy(jac_hbm.at[0, :, pl.ds(start, PIECE)], held.at[c], sems.at[c])
-
-    for c in range(CHUNKS):
-        piece(c, c * PIECE).start()
+def jacobian_kernel(jac_ref, elem_ref, after_ref, out_ref, weights, acc, rows):
     s, d = vector_tiles(elem_ref[:E_DEV, :].astype(F32))
     pad = jnp.zeros((128 - 2 * E_DEV, 128), F32)
     blocks = E_DEV // BLOCK
@@ -227,11 +225,10 @@
     keep = (lax.broadcasted_iota(jnp.int32, (BLOCK, 128), 1) & (BLOCK - 1)) == e
 
     def step(c, carry):
-        piece(c, pl.multiple_of(c * PIECE, PIECE)).wait()
         for b in range(blocks):
             lhs = jnp.concatenate(
                 [
-                    held[c, b * BLOCK : (b + 1) * BLOCK, g * 4 * DOF : (g + 1) * 4 * DOF]
+                    jac_ref[0, b * BLOCK : (b + 1) * BLOCK, pl.ds(pl.multiple_of(c * PIECE, PIECE) + g * 4 * DOF, 4 * DOF)]
                     for g in range(GROUPS)
                 ],
                 axis=0,
@@ -265,19 +262,17 @@
         jacobian_kernel,
         out_shape=jax.ShapeDtypeStruct((2 * E_DEV, 384), F32),
         in_specs=[
-            pl.BlockSpec(memory_space=pltpu.HBM),
+            pl.BlockSpec(memory_space=pltpu.VMEM),
             pl.BlockSpec(memory_space=pltpu.VMEM),
             pl.BlockSpec(memory_space=pl.ANY),
         ],
         out_specs=pl.BlockSpec(memory_space=pltpu.VMEM),
         scratch_shapes=[
-            pltpu.VMEM((CHUNKS, E_DEV, PIECE), BF16),
             pltpu.VMEM((E_DEV // BLOCK, 4 * DOF, 128), BF16),
             pltpu.VMEM((E_DEV // BLOCK, CHUNKS * GROUPS, 128), F32),
             pltpu.VMEM((384, 128), F32),
-            pltpu.SemaphoreType.DMA((CHUNKS,)),
         ],
-        compiler_params=pltpu.CompilerParams(vmem_limit_bytes=49 * MIB),
+        compiler_params=pltpu.CompilerParams(vmem_limit_bytes=8 * MIB),
         cost_estimate=pl.CostEstimate(
             flops=2 * 2 * E_DEV * DOF * DOF * 48, bytes_accessed=2 * E_DEV * DOF * DOF, transcendentals=0
         ),
@@ -291,9 +286,9 @@
 
 
 def flux_kernel(
-    quad_ref, dev_ref, far_ref, near_ref, cls_ref, jac_ref, sel_ref, inc_ref, elem_ref, *rest
+    quad_ref, dev_ref, far_ref, near_ref, cls_ref, src_ref, time_ref, jac_ref, sel_ref, inc_ref, elem_ref, *rest
 ):
-    tables, out_ref = rest[:-1], rest[-1]
+    tables, (res_ref, prod_ref, scratch) = rest[:-3], rest[-3:]
     me = lax.axis_index("space")
     far = far_ref[...]
     near = near_ref[...]
@@ -360,35 +355,14 @@
     for f in range(6):
         coef = coef + weight_sum[f * E_DEV : (f + 1) * E_DEV] * inc_ref[f : f + 1, :]
     fields_own = vector_tiles(elem_ref[:E_DEV, :].astype(F32))
-    for k in range(2):
-        own = jnp.concatenate(fields_own[k][:3], axis=1)
-        rows_k = slice(k * E_DEV, (k + 1) * E_DEV)
-        out_ref[rows_k, :] = jac_ref[rows_k, :] + coef * own - lifted[rows_k]
-
-
-def space_terms(quad, dev, far, near, cls, jac_terms, elem, tables):
-    sel = np.zeros((384, 768), np.float32)
-    sel[:DOF] = face_selector()
-    vmem = pl.BlockSpec(memory_space=pltpu.VMEM)
-    return pl.pallas_call(
-        flux_kernel,
-        out_shape=jax.ShapeDtypeStruct((2 * E_DEV, 384), F32),
-        in_specs=[vmem] * (9 + len(tables)),
-        out_specs=vmem,
-        compiler_params=pltpu.CompilerParams(vmem_limit_bytes=12 * MIB),
-        name="space_terms",
-    )(
-        quad.reshape(1, 16), dev, far, near, cls, jac_terms,
-        jnp.asarray(sel, BF16), jnp.asarray(face_incidence()), elem, *tables,
-    )
-
-
-def final_kernel(src_ref, time_ref, space_ref, res_ref, prod_ref, scratch):
     half = E_DEV // 2
     low = lane_half(half)
     for k, out_ref in enumerate((res_ref, prod_ref)):
+        own = jnp.concatenate(fields_own[k][:3], axis=1)
+        rows_k = slice(k * E_DEV, (k + 1) * E_DEV)
+        total_k = jac_ref[rows_k, :] + coef * own - lifted[rows_k]
         for q in range(3):
-            scratch[q] = space_ref[k * E_DEV : (k + 1) * E_DEV, q * 128 : (q + 1) * 128]
+            scratch[q] = total_k[:, q * 128 : (q + 1) * 128]
         even = [scratch[q, pl.ds(0, half, stride=2), :] for q in range(3)]
         odd = [scratch[q, pl.ds(1, half, stride=2), :] for q in range(3)]
         tiles = [
@@ -405,17 +379,22 @@
             out_ref[pl.ds(q, half, stride=5), :] = at
 
 
-def finish(source, time_parts, space):
+def finish(quad, dev, far, near, cls, source, time_terms, jac_terms, elem, tables):
+    sel = np.zeros((384, 768), np.float32)
+    sel[:DOF] = face_selector()
     vmem = pl.BlockSpec(memory_space=pltpu.VMEM)
     return pl.pallas_call(
-        final_kernel,
+        flux_kernel,
         out_shape=(jax.ShapeDtypeStruct((ROWS, 128), F32),) * 2,
-        in_specs=[vmem] * 3,
+        in_specs=[vmem] * (11 + len(tables)),
         out_specs=(vmem, vmem),
         scratch_shapes=[pltpu.VMEM((3, E_DEV, 128), F32)],
-        compiler_params=pltpu.CompilerParams(vmem_limit_bytes=4 * MIB),
+        compiler_params=pltpu.CompilerParams(vmem_limit_bytes=12 * MIB),
         name="finish",
-    )(source, time_parts, space)
+    )(
+        quad.reshape(1, 16), dev, far, near, cls, source, time_terms, jac_terms,
+        jnp.asarray(sel, BF16), jnp.asarray(face_incidence()), elem, *tables,
+    )
 
 
 def per_device(
@@ -431,7 +410,8 @@
     local_face,
     weight_index,
 ):
-    lin, elem = prep(first(), harmonic_state, direction)
+    coef = coefficients(frequency, viscosity)
+    lin, elem = prep(coef, harmonic_state, direction)
 
     def over_space(x, turn):
         return lax.ppermute(x, "space", [(i, (i + turn) % N_SPACE) for i in range(N_SPACE)])
@@ -440,20 +420,21 @@
     received = lax.all_to_all(lin, "inst", 0, 0, tiled=True)
     pair = make_pair(elem, across)
     others = [over_space(pair, turn) for turn in (1, -1, 2)]
-    back = spectral_sum(frequency, viscosity, received, pair)
+    back = spectral_sum(coef, received, pair)
     time_terms = lax.all_to_all(back, "inst", 0, 0, tiled=True)
     jac_terms = jacobian_product(jacobian, elem, back)
-    space = space_terms(
+    residual, product = finish(
         quad_weight,
         partner_device.reshape(1, SLOTS_DEV),
         partner_face,
         local_face,
         weight_index,
+        source.reshape(ROWS, 128),
+        time_terms,
         jac_terms,
         elem,
         [pair] + others,
     )
-    residual, product = finish(source.reshape(ROWS, 128), time_terms, space)
     return residual.reshape(1, FLAT), product.reshape(1, FLAT)
 
 

time: 40.3 us -> 41.4 us (1.027)
  local copies, waits for them, and re-layouts: 0.87 us -> 3.83 us
  Pallas kernels: 9.9 us -> 8 us
  starting transfers between devices: 24.3 us -> 23 us
  waiting for transfers between devices: 2.8 us -> 4.09 us
    unnamed x20 -> x22, local copies, waits for them, and re-layouts: 0.87 us -> 3.83 us
    pallas_call x1, Pallas kernels: 5.79 us -> 3.98 us  [jacobian_product(): pl.pallas_call(jacobian_kernel, out_shape=jax.ShapeDtypeStruct((2 * E_DEV...]
    all_to_all x1, waiting for transfers between devices: 2.78 us -> 4.08 us  [per_device(): received = lax.all_to_all(lin, 'inst', 0, 0, tiled=True)]
    all_to_all x1, starting transfers between devices: 5.31 us -> 4.04 us  [per_device(): time_terms = lax.all_to_all(back, 'inst', 0, 0, tiled=True)]
    pallas_call x3 -> x2, Pallas kernels: 2.47 us -> 2.47 us  [the longest x1 2.44 us: finish(): pl.pallas_call(flux_kernel, out_shape=(jax.ShapeDtypeStruct((ROWS, 128),...]
  transfers between devices with their start and end apart: 6 -> 6, of which waited for: 1 -> 1; matrix products, arithmetic and copies ran while one was open for 0% -> 0% of each run, Pallas kernels for 21% -> 12%
where the time goes in v5:
time: 41.4 us; the launch traced here: 41.1 us
  starting transfers between devices  23 us (56%)
  Pallas kernels  8 us (19%)
  waiting for transfers between devices  4.09 us (10%)
  local copies, waits for them, and re-layouts  3.83 us (9%)
  between operations  2.14 us (5%)
    ppermute x4, starting transfers between devices, over_space(): lax.ppermute(x, 'space', [(i, (i + turn) % N_SPACE) for i in range(N_SPAC...  10.9 us
    all_to_all x1, starting transfers between devices, per_device(): received = lax.all_to_all(lin, 'inst', 0, 0, tiled=True)  8.04 us
    all_to_all x1, waiting for transfers between devices, per_device(): received = lax.all_to_all(lin, 'inst', 0, 0, tiled=True)  4.08 us
    all_to_all x1, starting transfers between devices, per_device(): time_terms = lax.all_to_all(back, 'inst', 0, 0, tiled=True)  4.04 us
    pallas_call x1, Pallas kernels, jacobian_product(): pl.pallas_call(jacobian_kernel, out_shape=jax.ShapeDtypeStruct((2 * E_DEV...  3.98 us
    unnamed x22, local copies, waits for them, and re-layouts  3.83 us
    pallas_call x1, Pallas kernels, finish(): pl.pallas_call(flux_kernel, out_shape=(jax.ShapeDtypeStruct((ROWS, 128),...  2.44 us
  transfers between devices with their start and end apart: 6, of which 1 were waited for; matrix products, arithmetic and copies ran while one was open for 0% of the time, Pallas kernels for 12%

profile of v5, /device:TPU:1, one launch (start us, length us, event | category | flops | bytes accessed | tf_op | source)
XLA Modules:
  0.0 41.1 jit_solution(9947891690937075063)
XLA Ops:
  0.6 0.0 copy-start.3
  0.6 0.0 copy-start.2
  2.0 0.0 copy-done.3
  2.0 0.0 copy-done.2
  2.0 0.7 %prep.1 = (bf16[256,128]{1,0:T(8,128)(2,1)}, bf16[64,640]{1,0:T(8,128)(2,1)S(1)}) custom-call(f32[32,128]{1,0:T(8,128)S(1)} %coefficients.1.mark_ref.coef_ref, bf16[1,15360]{1,0:T(2,128)(2,1)S(1)} %copy-done.2, bf16[1,15360]{1,0:T(2,128)(2,1)S(1)} %copy-done.3), custom_call_target="tpu_custom_call" | custom-call | tf_op jit(solution)/shard_map/prep/pallas_call | solution.py:120
  2.7 7.7 %collective-permute-start = (bf16[64,640]{1,0:T(8,128)(2,1)S(1)}, bf16[64,640]{1,0:T(8,128)(2,1)S(1)}, u32[]{:S(2)}, u32[]{:S(2)}) collective-permute-start(bf16[64,640]{1,0:T(8,128)(2,1)S(1)} %get-tuple-element.7.own_ref.elem_ref), channel_id=1, source_target_pairs={{0,4},{1,5},{2,6},{3,7},{4,0},{5,1},{6,2},{7,3},{8,12},{9,13},{10,... | collective-permute-start | bytes 245768 | tf_op jit(solution)/shard_map/ppermute | solution.py:417
  10.5 8.0 %all-to-all-start = ((bf16[32,8,128]{2,1,0:T(8,128)(2,1)}), bf16[32,8,128]{2,1,0:T(8,128)(2,1)S(1)}, u32[]{:S(2)}, u32[]{:S(2)}) async-start(bf16[32,8,128]{2,1,0:T(8,128)(2,1)} %bitcast.3), calls=%async_computation | async-start | bytes 131072 | tf_op jit(solution)/shard_map/all_to_all | solution.py:420
  18.5 0.0 collective-permute-done.across_ref
  18.6 1.3 %collective-permute-start.3 = (bf16[112,640]{1,0:T(8,128)(2,1)S(1)}, bf16[112,640]{1,0:T(8,128)(2,1)S(1)}, u32[]{:S(2)}, u32[]{:S(2)}) collective-permute-start(bf16[112,640]{1,0:T(8,128)(2,1)S(1)} %pair.1.after_ref.rest_0_), channel_id=1, source_target_pairs={{0,2},{1,3},{2,4},{3,5},{4,6},{5,7},{6,0},{7,1},{8,10},{9,11},{10,... | collective-permute-start | bytes 430088 | tf_op jit(solution)/shard_map/ppermute | solution.py:417
  19.8 1.9 %collective-permute-start.2 = (bf16[112,640]{1,0:T(8,128)(2,1)S(1)}, bf16[112,640]{1,0:T(8,128)(2,1)S(1)}, u32[]{:S(2)}, u32[]{:S(2)}) collective-permute-start(bf16[112,640]{1,0:T(8,128)(2,1)S(1)} %pair.1.after_ref.rest_0_), channel_id=1, source_target_pairs={{0,7},{1,0},{2,1},{3,2},{4,3},{5,4},{6,5},{7,6},{8,15},{9,8},{10,9... | collective-permute-start | bytes 430088 | tf_op jit(solution)/shard_map/ppermute | solution.py:417
  21.8 0.0 collective-permute-start.1
  21.8 4.1 %all-to-all-done = bf16[32,8,128]{2,1,0:T(8,128)(2,1)S(1)} async-done(((bf16[32,8,128]{2,1,0:T(8,128)(2,1)}), bf16[32,8,128]{2,1,0:T(8,128)(2,1)S(1)}, u32[]{:S(2)}, u32[]{:S(2)}) %all-to-all-start) | async-done | bytes 65568 | tf_op jit(solution)/shard_map/all_to_all | solution.py:420
  25.8 0.0 copy-start.1
  25.8 0.8 %spectral.1.after_ref = f32[256,128]{1,0:T(8,128)} custom-call(f32[32,128]{1,0:T(8,128)S(1)} %coefficients.1.mark_ref.coef_ref, bf16[256,128]{1,0:T(8,128)(2,1)S(1)} %bitcast.10, bf16[112,640]{1,0:T(8,128)(2,1)S(1)} %pair.1.after_ref.rest_0_), custom_call_target="tpu_custom_call" | custom-call | flops 99999997952 | tf_op jit(solution)/shard_map/spectral/pallas_call | solution.py:187
  26.7 0.0 copy-start.4
  26.7 0.0 copy-start.5
  26.7 0.0 copy-start.6
  26.7 0.0 copy-start.7
  26.7 0.0 copy-start.8
  26.7 0.0 copy-start.9
  26.7 0.0 copy-start.10
  26.7 4.0 %all-to-all-start.1 = ((f32[32,8,128]{2,1,0:T(8,128)}), f32[32,8,128]{2,1,0:T(8,128)S(1)}, u32[]{:S(2)}, u32[]{:S(2)}) async-start(f32[32,8,128]{2,1,0:T(8,128)} %bitcast.5), calls=%async_computation.1 | async-start | bytes 262144 | tf_op jit(solution)/shard_map/all_to_all | solution.py:424
  30.8 0.0 copy-start
  30.8 3.8 %copy-done = bf16[1,48,102400]{2,1,0:T(8,128)(2,1)S(1)} copy-done((bf16[1,48,102400]{2,1,0:T(8,128)(2,1)S(1)}, bf16[1,48,102400]{2,1,0:T(8,128)(2,1)}, u32[]{:S(2)}) %copy-start) | copy-done | bytes 9830424
  34.5 4.0 %jacobian.1.jac_ref = f32[96,384]{1,0:T(8,128)S(1)} custom-call(bf16[1,48,102400]{2,1,0:T(8,128)(2,1)S(1)} %copy-done, bf16[64,640]{1,0:T(8,128)(2,1)S(1)} %get-tuple-element.7.own_ref.elem_ref, f32[256,128]{1,0:T(8,128)} %spectral.1.after_ref), custom_call_target="tpu_custom_call" | custom-call | flops 943718400 | bytes 9830400 | tf_op jit(solution)/shard_map/jacobian/pallas_call | solution.py:261
  38.5 0.0 all-to-all-done.1
  38.5 0.0 collective-permute-done.3.rest_3_
  38.5 0.0 collective-permute-done.2.rest_2_
  38.6 0.0 collective-permute-done.1.rest_1_
  38.6 0.0 copy-done.1
  38.6 0.0 copy-done.4
  38.6 0.0 copy-done.5
  38.6 0.0 copy-done.6
  38.6 0.0 copy-done.7
  38.6 0.0 copy-done.8
  38.6 0.0 copy-done.9
  38.6 0.0 copy-done.10
  38.6 2.4 %finish.1 = (f32[120,128]{1,0:T(8,128)}, f32[120,128]{1,0:T(8,128)}) custom-call(f32[1,16]{1,0:T(1,128)S(1)} %bitcast.13, s32[1,192]{1,0:T(1,128)S(1)} %bitcast.12, s32[1,192]{1,0:T(1,128)S(1)} %copy-done.7, s32[1,192]{1,0:T(1,128)S(1)} %copy-done.8, s32[1,192]{1,0:T(1,128)S(1)} %copy-done.9, f32[120,128]{1,0:T(8,128)S(1)} %bitcast.11, ...), custom_call_target="tpu_custom_call" | custom-call | tf_op jit(solution)/shard_map/finish/pallas_call | solution.py:386
  (2 shorter events, 0.0 us)
Async XLA Ops:
  0.6 1.4 %copy-start.3 = (bf16[1,15360]{1,0:T(2,128)(2,1)S(1)}, bf16[1,15360]{1,0:T(2,128)(2,1)}, u32[]{:S(2)}) copy-start(bf16[1,15360]{1,0:T(2,128)(2,1)} %d_ref.1) | copy-start | bytes 92164
  0.6 1.4 %copy-start.2 = (bf16[1,15360]{1,0:T(2,128)(2,1)S(1)}, bf16[1,15360]{1,0:T(2,128)(2,1)}, u32[]{:S(2)}) copy-start(bf16[1,15360]{1,0:T(2,128)(2,1)} %s_ref.1) | copy-start | bytes 92164
  2.7 15.8 %collective-permute-start = (bf16[64,640]{1,0:T(8,128)(2,1)S(1)}, bf16[64,640]{1,0:T(8,128)(2,1)S(1)}, u32[]{:S(2)}, u32[]{:S(2)}) collective-permute-start(bf16[64,640]{1,0:T(8,128)(2,1)S(1)} %get-tuple-element.7.own_ref.elem_ref), channel_id=1, source_target_pairs={{0,4},{1,5},{2,6},{3,7},{4,0},{5,1},{6,2},{7,3},{8,12},{9,13},{10,... | collective-permute-start | bytes 245768 | tf_op jit(solution)/shard_map/ppermute | solution.py:417
  10.5 15.4 %all-to-all-start = ((bf16[32,8,128]{2,1,0:T(8,128)(2,1)}), bf16[32,8,128]{2,1,0:T(8,128)(2,1)S(1)}, u32[]{:S(2)}, u32[]{:S(2)}) async-start(bf16[32,8,128]{2,1,0:T(8,128)(2,1)} %bitcast.3), calls=%async_computation | async-start | bytes 131072 | tf_op jit(solution)/shard_map/all_to_all | solution.py:420
  18.6 20.0 %collective-permute-start.3 = (bf16[112,640]{1,0:T(8,128)(2,1)S(1)}, bf16[112,640]{1,0:T(8,128)(2,1)S(1)}, u32[]{:S(2)}, u32[]{:S(2)}) collective-permute-start(bf16[112,640]{1,0:T(8,128)(2,1)S(1)} %pair.1.after_ref.rest_0_), channel_id=1, source_target_pairs={{0,2},{1,3},{2,4},{3,5},{4,6},{5,7},{6,0},{7,1},{8,10},{9,11},{10,... | collective-permute-start | bytes 430088 | tf_op jit(solution)/shard_map/ppermute | solution.py:417
  19.8 18.7 %collective-permute-start.2 = (bf16[112,640]{1,0:T(8,128)(2,1)S(1)}, bf16[112,640]{1,0:T(8,128)(2,1)S(1)}, u32[]{:S(2)}, u32[]{:S(2)}) collective-permute-start(bf16[112,640]{1,0:T(8,128)(2,1)S(1)} %pair.1.after_ref.rest_0_), channel_id=1, source_target_pairs={{0,7},{1,0},{2,1},{3,2},{4,3},{5,4},{6,5},{7,6},{8,15},{9,8},{10,9... | collective-permute-start | bytes 430088 | tf_op jit(solution)/shard_map/ppermute | solution.py:417
  21.8 16.8 %collective-permute-start.1 = (bf16[112,640]{1,0:T(8,128)(2,1)S(1)}, bf16[112,640]{1,0:T(8,128)(2,1)S(1)}, u32[]{:S(2)}, u32[]{:S(2)}) collective-permute-start(bf16[112,640]{1,0:T(8,128)(2,1)S(1)} %pair.1.after_ref.rest_0_), channel_id=1, source_target_pairs={{0,1},{1,2},{2,3},{3,4},{4,5},{5,6},{6,7},{7,0},{8,9},{9,10},{10,1... | collective-permute-start | bytes 430088 | tf_op jit(solution)/shard_map/ppermute | solution.py:417
  25.8 12.7 %copy-start.1 = (bf16[384,768]{1,0:T(8,128)(2,1)S(1)}, bf16[384,768]{1,0:T(8,128)(2,1)}, u32[]{:S(2)}) copy-start(bf16[384,768]{1,0:T(8,128)(2,1)} %constant.4.clone.sel_ref) | copy-start | bytes 1769476
  26.7 11.9 %copy-start.4 = (f32[1,15360]{1,0:T(1,128)S(1)}, f32[1,15360]{1,0:T(1,128)}, u32[]{:S(2)}) copy-start(f32[1,15360]{1,0:T(1,128)} %param.15) | copy-start | bytes 184324
  26.7 11.9 %copy-start.5 = (f32[8,384]{1,0:T(8,128)S(1)}, f32[8,384]{1,0:T(8,128)}, u32[]{:S(2)}) copy-start(f32[8,384]{1,0:T(8,128)} %constant.5.clone.inc_ref) | copy-start | bytes 36868
  26.7 11.9 %copy-start.6 = (s32[1,192,1]{1,2,0:T(1,128)S(1)}, s32[1,192,1]{1,2,0:T(1,128)}, u32[]{:S(2)}) copy-start(s32[1,192,1]{1,2,0:T(1,128)} %param.20) | copy-start | bytes 2308
  26.7 11.9 %copy-start.7 = (s32[1,192]{1,0:T(1,128)S(1)}, s32[1,192]{1,0:T(1,128)}, u32[]{:S(2)}) copy-start(s32[1,192]{1,0:T(1,128)} %far_ref.1) | copy-start | bytes 2308
  26.7 12.0 %copy-start.8 = (s32[1,192]{1,0:T(1,128)S(1)}, s32[1,192]{1,0:T(1,128)}, u32[]{:S(2)}) copy-start(s32[1,192]{1,0:T(1,128)} %near_ref.1) | copy-start | bytes 2308
  26.7 11.9 %copy-start.9 = (s32[1,192]{1,0:T(1,128)S(1)}, s32[1,192]{1,0:T(1,128)}, u32[]{:S(2)}) copy-start(s32[1,192]{1,0:T(1,128)} %cls_ref.1) | copy-start | bytes 2308
  26.7 11.9 %copy-start.10 = (f32[16]{0:T(128)S(1)}, f32[16]{0:T(128)}, u32[]{:S(2)}) copy-start(f32[16]{0:T(128)} %param.19) | copy-start | bytes 196
  26.7 11.8 %all-to-all-start.1 = ((f32[32,8,128]{2,1,0:T(8,128)}), f32[32,8,128]{2,1,0:T(8,128)S(1)}, u32[]{:S(2)}, u32[]{:S(2)}) async-start(f32[32,8,128]{2,1,0:T(8,128)} %bitcast.5), calls=%async_computation.1 | async-start | bytes 262144 | tf_op jit(solution)/shard_map/all_to_all | solution.py:424
  30.8 3.8 %copy-start = (bf16[1,48,102400]{2,1,0:T(8,128)(2,1)S(1)}, bf16[1,48,102400]{2,1,0:T(8,128)(2,1)}, u32[]{:S(2)}) copy-start(bf16[1,48,102400]{2,1,0:T(8,128)(2,1)} %jac_ref.1) | copy-start | bytes 29491204

commit v6 on v5

--- a/solution.py
+++ b/solution.py
@@ -112,7 +112,7 @@
         wide[q, pl.ds(1, half, stride=2), :] = odd[q]
     for q in range(5):
         elem_ref[:E_DEV, q * 128 : (q + 1) * 128] = wide[q].astype(BF16)
-    elem_ref[E_DEV:, :] = jnp.zeros((SPARE, 2 * DOF), BF16)
+    elem_ref[E_DEV:, :] = jnp.zeros((SPARE // 2, 2 * DOF), BF16)
 
 
 def prep(mark, state, direction):
@@ -121,7 +121,7 @@
         prep_kernel,
         out_shape=(
             jax.ShapeDtypeStruct((256, 128), BF16),
-            jax.ShapeDtypeStruct((E_DEV + SPARE, 2 * DOF), BF16),
+            jax.ShapeDtypeStruct((E_DEV + SPARE // 2, 2 * DOF), BF16),
         ),
         in_specs=[pl.BlockSpec(memory_space=pl.ANY), vmem, vmem],
         out_specs=(vmem, vmem),
@@ -190,7 +190,7 @@
         in_specs=[vmem] * 2 + [pl.BlockSpec(memory_space=pl.ANY)],
         out_specs=vmem,
         compiler_params=pltpu.CompilerParams(vmem_limit_bytes=4 * MIB),
-        cost_estimate=pl.CostEstimate(flops=10**11, bytes_accessed=0, transcendentals=0),
+        cost_estimate=pl.CostEstimate(flops=10**10, bytes_accessed=0, transcendentals=0),
         name="spectral",
     )(coef, received, after)
 
@@ -204,7 +204,12 @@
     return s, d
 
 
-def jacobian_kernel(jac_ref, elem_ref, after_ref, out_ref, weights, acc, rows):
+def jacobian_kernel(jac_hbm, elem_ref, after_ref, out_ref, held, weights, acc, rows, sems):
+    def piece(c, start):
+        return pltpu.make_async_copy(jac_hbm.at[0, :, pl.ds(start, PIECE)], held.at[c], sems.at[c])
+
+    for c in range(CHUNKS):
+        piece(c, c * PIECE).start()
     s, d = vector_tiles(elem_ref[:E_DEV, :].astype(F32))
     pad = jnp.zeros((128 - 2 * E_DEV, 128), F32)
     blocks = E_DEV // BLOCK
@@ -225,10 +230,11 @@
     keep = (lax.broadcasted_iota(jnp.int32, (BLOCK, 128), 1) & (BLOCK - 1)) == e
 
     def step(c, carry):
+        piece(c, pl.multiple_of(c * PIECE, PIECE)).wait()
         for b in range(blocks):
             lhs = jnp.concatenate(
                 [
-                    jac_ref[0, b * BLOCK : (b + 1) * BLOCK, pl.ds(pl.multiple_of(c * PIECE, PIECE) + g * 4 * DOF, 4 * DOF)]
+                    held[c, b * BLOCK : (b + 1) * BLOCK, g * 4 * DOF : (g + 1) * 4 * DOF]
                     for g in range(GROUPS)
                 ],
                 axis=0,
@@ -262,17 +268,19 @@
         jacobian_kernel,
         out_shape=jax.ShapeDtypeStruct((2 * E_DEV, 384), F32),
         in_specs=[
-            pl.BlockSpec(memory_space=pltpu.VMEM),
+            pl.BlockSpec(memory_space=pltpu.HBM),
             pl.BlockSpec(memory_space=pltpu.VMEM),
             pl.BlockSpec(memory_space=pl.ANY),
         ],
         out_specs=pl.BlockSpec(memory_space=pltpu.VMEM),
         scratch_shapes=[
+            pltpu.VMEM((CHUNKS, E_DEV, PIECE), BF16),
             pltpu.VMEM((E_DEV // BLOCK, 4 * DOF, 128), BF16),
             pltpu.VMEM((E_DEV // BLOCK, CHUNKS * GROUPS, 128), F32),
             pltpu.VMEM((384, 128), F32),
+            pltpu.SemaphoreType.DMA((CHUNKS,)),
         ],
-        compiler_params=pltpu.CompilerParams(vmem_limit_bytes=8 * MIB),
+        compiler_params=pltpu.CompilerParams(vmem_limit_bytes=49 * MIB),
         cost_estimate=pl.CostEstimate(
             flops=2 * 2 * E_DEV * DOF * DOF * 48, bytes_accessed=2 * E_DEV * DOF * DOF, transcendentals=0
         ),
@@ -286,7 +294,7 @@
 
 
 def flux_kernel(
-    quad_ref, dev_ref, far_ref, near_ref, cls_ref, src_ref, time_ref, jac_ref, sel_ref, inc_ref, elem_ref, *rest
+    quad_ref, dev_ref, far_ref, near_ref, cls_ref, src_ref, time_ref, jac_ref, sel_ref, lift_ref, inc_ref, elem_ref, *rest
 ):
     tables, (res_ref, prod_ref, scratch) = rest[:-3], rest[-3:]
     me = lax.axis_index("space")
@@ -325,8 +333,7 @@
         ],
         axis=0,
     ).astype(BF16)
-    sel = sel_ref[...]
-    faces = jnp.dot(fields, sel, preferred_element_type=F32)
+    faces = jnp.dot(fields, sel_ref[...], preferred_element_type=F32)
     which = jnp.concatenate([far_ls, far_ls], axis=0)
     trace = jnp.zeros((2 * SLOTS_DEV, 128), F32)
     for face in range(6):
@@ -334,8 +341,8 @@
     trace = jnp.concatenate([trace[:SLOTS_DEV], trace[SLOTS_DEV:]], axis=1).astype(BF16)
     rows = lax.broadcasted_iota(jnp.int32, (6 * E_DEV, SLOTS_DEV), 0)
     spread = jnp.where(rows == near_row, w, 0.0)
-    high, rest_w = split(spread)
-    flux = jnp.dot(high, trace, preferred_element_type=F32) + jnp.dot(rest_w, trace, preferred_element_type=F32)
+    flux = jnp.dot(jnp.concatenate(split(spread), axis=0), trace, preferred_element_type=F32)
+    flux = flux[: 6 * E_DEV] + flux[6 * E_DEV :]
     weight_sum = jnp.sum(spread, axis=1, keepdims=True)
     lhs = jnp.concatenate(
         [
@@ -346,11 +353,8 @@
         ],
         axis=1,
     )
-    high, rest_f = split(lhs)
-    dims = (((1,), (1,)), ((), ()))
-    lifted = lax.dot_general(high, sel, dims, preferred_element_type=F32) + lax.dot_general(
-        rest_f, sel, dims, preferred_element_type=F32
-    )
+    lifted = jnp.dot(jnp.concatenate(split(lhs), axis=0), lift_ref[...], preferred_element_type=F32)
+    lifted = lifted[: 2 * E_DEV] + lifted[2 * E_DEV :]
     coef = jnp.zeros((E_DEV, 384), F32)
     for f in range(6):
         coef = coef + weight_sum[f * E_DEV : (f + 1) * E_DEV] * inc_ref[f : f + 1, :]
@@ -386,14 +390,14 @@
     return pl.pallas_call(
         flux_kernel,
         out_shape=(jax.ShapeDtypeStruct((ROWS, 128), F32),) * 2,
-        in_specs=[vmem] * (11 + len(tables)),
+        in_specs=[vmem] * (12 + len(tables)),
         out_specs=(vmem, vmem),
         scratch_shapes=[pltpu.VMEM((3, E_DEV, 128), F32)],
         compiler_params=pltpu.CompilerParams(vmem_limit_bytes=12 * MIB),
         name="finish",
     )(
         quad.reshape(1, 16), dev, far, near, cls, source, time_terms, jac_terms,
-        jnp.asarray(sel, BF16), jnp.asarray(face_incidence()), elem, *tables,
+        jnp.asarray(sel, BF16), jnp.asarray(sel.T, BF16), jnp.asarray(face_incidence()), elem, *tables,
     )
 
 

time: 41.4 us -> 41.1 us (level)
  local copies, waits for them, and re-layouts: 3.83 us -> 0.05 us
  waiting for transfers between devices: 4.09 us -> 6.58 us
  Pallas kernels: 8 us -> 9.01 us
    unnamed x22, local copies, waits for them, and re-layouts: 3.83 us -> 0.05 us
    all_to_all x1, waiting for transfers between devices: 0.01 us -> 2.49 us  [per_device(): time_terms = lax.all_to_all(back, 'inst', 0, 0, tiled=True)]
    pallas_call x1, Pallas kernels: 3.98 us -> 5.24 us  [jacobian_product(): pl.pallas_call(jacobian_kernel, out_shape=jax.ShapeDtypeStruct((2 * E_DEV...]
  transfers between devices with their start and end apart: 6 -> 6, of which waited for: 1 -> 2; matrix products, arithmetic and copies ran while one was open for 0% -> 0% of each run, Pallas kernels for 12% -> 15%
where the time goes in v6:
time: 41.1 us; the launch traced here: 40.8 us
  starting transfers between devices  23 us (56%)
  Pallas kernels  9.01 us (22%)
  waiting for transfers between devices  6.58 us (16%)
  between operations  2.14 us (5%)
    ppermute x4, starting transfers between devices, over_space(): lax.ppermute(x, 'space', [(i, (i + turn) % N_SPACE) for i in range(N_SPAC...  10.9 us
    all_to_all x1, starting transfers between devices, per_device(): received = lax.all_to_all(lin, 'inst', 0, 0, tiled=True)  8.04 us
    pallas_call x1, Pallas kernels, jacobian_product(): pl.pallas_call(jacobian_kernel, out_shape=jax.ShapeDtypeStruct((2 * E_DEV...  5.24 us
    all_to_all x1, waiting for transfers between devices, per_device(): received = lax.all_to_all(lin, 'inst', 0, 0, tiled=True)  4.08 us
    all_to_all x1, starting transfers between devices, per_device(): time_terms = lax.all_to_all(back, 'inst', 0, 0, tiled=True)  4.04 us
    all_to_all x1, waiting for transfers between devices, per_device(): time_terms = lax.all_to_all(back, 'inst', 0, 0, tiled=True)  2.49 us
    pallas_call x1, Pallas kernels, finish(): pl.pallas_call(flux_kernel, out_shape=(jax.ShapeDtypeStruct((ROWS, 128),...  2.2 us
  transfers between devices with their start and end apart: 6, of which 2 were waited for; matrix products, arithmetic and copies ran while one was open for 0% of the time, Pallas kernels for 15%

profile of v6, /device:TPU:1, one launch (start us, length us, event | category | flops | bytes accessed | tf_op | source)
XLA Modules:
  0.0 40.8 jit_solution(18093708730712583291)
XLA Ops:
  0.6 0.0 copy-start.3
  0.6 0.0 copy-start.2
  2.0 0.0 copy-done.3
  2.0 0.0 copy-done.2
  2.0 0.7 %prep.1 = (bf16[256,128]{1,0:T(8,128)(2,1)}, bf16[56,640]{1,0:T(8,128)(2,1)S(1)}) custom-call(f32[32,128]{1,0:T(8,128)S(1)} %coefficients.1.mark_ref.coef_ref, bf16[1,15360]{1,0:T(2,128)(2,1)S(1)} %copy-done.2, bf16[1,15360]{1,0:T(2,128)(2,1)S(1)} %copy-done.3), custom_call_target="tpu_custom_call" | custom-call | tf_op jit(solution)/shard_map/prep/pallas_call | solution.py:120
  2.7 7.7 %collective-permute-start = (bf16[56,640]{1,0:T(8,128)(2,1)S(1)}, bf16[56,640]{1,0:T(8,128)(2,1)S(1)}, u32[]{:S(2)}, u32[]{:S(2)}) collective-permute-start(bf16[56,640]{1,0:T(8,128)(2,1)S(1)} %get-tuple-element.7.own_ref.elem_ref), channel_id=1, source_target_pairs={{0,4},{1,5},{2,6},{3,7},{4,0},{5,1},{6,2},{7,3},{8,12},{9,13},{10,... | collective-permute-start | bytes 215048 | tf_op jit(solution)/shard_map/ppermute | solution.py:421
  10.5 8.0 %all-to-all-start = ((bf16[32,8,128]{2,1,0:T(8,128)(2,1)}), bf16[32,8,128]{2,1,0:T(8,128)(2,1)S(1)}, u32[]{:S(2)}, u32[]{:S(2)}) async-start(bf16[32,8,128]{2,1,0:T(8,128)(2,1)} %bitcast.3), calls=%async_computation | async-start | bytes 131072 | tf_op jit(solution)/shard_map/all_to_all | solution.py:424
  18.5 0.0 collective-permute-done.across_ref
  18.6 1.3 %collective-permute-start.3 = (bf16[112,640]{1,0:T(8,128)(2,1)S(1)}, bf16[112,640]{1,0:T(8,128)(2,1)S(1)}, u32[]{:S(2)}, u32[]{:S(2)}) collective-permute-start(bf16[112,640]{1,0:T(8,128)(2,1)S(1)} %pair.1.after_ref.rest_0_), channel_id=1, source_target_pairs={{0,2},{1,3},{2,4},{3,5},{4,6},{5,7},{6,0},{7,1},{8,10},{9,11},{10,... | collective-permute-start | bytes 430088 | tf_op jit(solution)/shard_map/ppermute | solution.py:421
  19.8 1.9 %collective-permute-start.2 = (bf16[112,640]{1,0:T(8,128)(2,1)S(1)}, bf16[112,640]{1,0:T(8,128)(2,1)S(1)}, u32[]{:S(2)}, u32[]{:S(2)}) collective-permute-start(bf16[112,640]{1,0:T(8,128)(2,1)S(1)} %pair.1.after_ref.rest_0_), channel_id=1, source_target_pairs={{0,7},{1,0},{2,1},{3,2},{4,3},{5,4},{6,5},{7,6},{8,15},{9,8},{10,9... | collective-permute-start | bytes 430088 | tf_op jit(solution)/shard_map/ppermute | solution.py:421
  21.8 0.0 collective-permute-start.1
  21.8 4.1 %all-to-all-done = bf16[32,8,128]{2,1,0:T(8,128)(2,1)S(1)} async-done(((bf16[32,8,128]{2,1,0:T(8,128)(2,1)}), bf16[32,8,128]{2,1,0:T(8,128)(2,1)S(1)}, u32[]{:S(2)}, u32[]{:S(2)}) %all-to-all-start) | async-done | bytes 65568 | tf_op jit(solution)/shard_map/all_to_all | solution.py:424
  25.8 0.8 %spectral.1.after_ref = f32[256,128]{1,0:T(8,128)} custom-call(f32[32,128]{1,0:T(8,128)S(1)} %coefficients.1.mark_ref.coef_ref, bf16[256,128]{1,0:T(8,128)(2,1)S(1)} %bitcast.10, bf16[112,640]{1,0:T(8,128)(2,1)S(1)} %pair.1.after_ref.rest_0_), custom_call_target="tpu_custom_call" | custom-call | flops 10000000000 | tf_op jit(solution)/shard_map/spectral/pallas_call | solution.py:187
  26.7 0.0 copy-start
  26.7 0.0 copy-start.1
  26.7 0.0 copy-start.4
  26.7 0.0 copy-start.5
  26.7 0.0 copy-start.6
  26.7 0.0 copy-start.7
  26.7 0.0 copy-start.8
  26.7 0.0 copy-start.9
  26.7 0.0 copy-start.10
  26.7 4.0 %all-to-all-start.1 = ((f32[32,8,128]{2,1,0:T(8,128)}), f32[32,8,128]{2,1,0:T(8,128)S(1)}, u32[]{:S(2)}, u32[]{:S(2)}) async-start(f32[32,8,128]{2,1,0:T(8,128)} %bitcast.5), calls=%async_computation.1 | async-start | bytes 262144 | tf_op jit(solution)/shard_map/all_to_all | solution.py:428
  30.8 5.2 %jacobian.1.jac_ref = f32[96,384]{1,0:T(8,128)S(1)} custom-call(bf16[1,48,102400]{2,1,0:T(8,128)(2,1)} %jac_hbm.1, bf16[56,640]{1,0:T(8,128)(2,1)S(1)} %get-tuple-element.7.own_ref.elem_ref, f32[256,128]{1,0:T(8,128)} %spectral.1.after_ref), custom_call_target="tpu_custom_call" | custom-call | flops 943718400 | bytes 9830400 | tf_op jit(solution)/shard_map/jacobian/pallas_call | solution.py:267
  36.0 2.5 %all-to-all-done.1 = f32[32,8,128]{2,1,0:T(8,128)S(1)} async-done(((f32[32,8,128]{2,1,0:T(8,128)}), f32[32,8,128]{2,1,0:T(8,128)S(1)}, u32[]{:S(2)}, u32[]{:S(2)}) %all-to-all-start.1) | async-done | bytes 131104 | tf_op jit(solution)/shard_map/all_to_all | solution.py:428
  38.5 0.0 collective-permute-done.3.rest_3_
  38.5 0.0 collective-permute-done.2.rest_2_
  38.5 0.0 collective-permute-done.1.rest_1_
  38.5 0.0 copy-done
  38.5 0.0 copy-done.1
  38.5 0.0 copy-done.4
  38.6 0.0 copy-done.5
  38.6 0.0 copy-done.6
  38.6 0.0 copy-done.7
  38.6 0.0 copy-done.8
  38.6 0.0 copy-done.9
  38.6 0.0 copy-done.10
  38.6 2.2 %finish.1 = (f32[120,128]{1,0:T(8,128)}, f32[120,128]{1,0:T(8,128)}) custom-call(f32[1,16]{1,0:T(1,128)S(1)} %bitcast.13, s32[1,192]{1,0:T(1,128)S(1)} %bitcast.12, s32[1,192]{1,0:T(1,128)S(1)} %copy-done.7, s32[1,192]{1,0:T(1,128)S(1)} %copy-done.8, s32[1,192]{1,0:T(1,128)S(1)} %copy-done.9, f32[120,128]{1,0:T(8,128)S(1)} %bitcast.11, ...), custom_call_target="tpu_custom_call" | custom-call | tf_op jit(solution)/shard_map/finish/pallas_call | solution.py:390
  (2 shorter events, 0.0 us)
Async XLA Ops:
  0.6 1.4 %copy-start.3 = (bf16[1,15360]{1,0:T(2,128)(2,1)S(1)}, bf16[1,15360]{1,0:T(2,128)(2,1)}, u32[]{:S(2)}) copy-start(bf16[1,15360]{1,0:T(2,128)(2,1)} %d_ref.1) | copy-start | bytes 92164
  0.6 1.4 %copy-start.2 = (bf16[1,15360]{1,0:T(2,128)(2,1)S(1)}, bf16[1,15360]{1,0:T(2,128)(2,1)}, u32[]{:S(2)}) copy-start(bf16[1,15360]{1,0:T(2,128)(2,1)} %s_ref.1) | copy-start | bytes 92164
  2.7 15.8 %collective-permute-start = (bf16[56,640]{1,0:T(8,128)(2,1)S(1)}, bf16[56,640]{1,0:T(8,128)(2,1)S(1)}, u32[]{:S(2)}, u32[]{:S(2)}) collective-permute-start(bf16[56,640]{1,0:T(8,128)(2,1)S(1)} %get-tuple-element.7.own_ref.elem_ref), channel_id=1, source_target_pairs={{0,4},{1,5},{2,6},{3,7},{4,0},{5,1},{6,2},{7,3},{8,12},{9,13},{10,... | collective-permute-start | bytes 215048 | tf_op jit(solution)/shard_map/ppermute | solution.py:421
  10.5 15.4 %all-to-all-start = ((bf16[32,8,128]{2,1,0:T(8,128)(2,1)}), bf16[32,8,128]{2,1,0:T(8,128)(2,1)S(1)}, u32[]{:S(2)}, u32[]{:S(2)}) async-start(bf16[32,8,128]{2,1,0:T(8,128)(2,1)} %bitcast.3), calls=%async_computation | async-start | bytes 131072 | tf_op jit(solution)/shard_map/all_to_all | solution.py:424
  18.6 20.0 %collective-permute-start.3 = (bf16[112,640]{1,0:T(8,128)(2,1)S(1)}, bf16[112,640]{1,0:T(8,128)(2,1)S(1)}, u32[]{:S(2)}, u32[]{:S(2)}) collective-permute-start(bf16[112,640]{1,0:T(8,128)(2,1)S(1)} %pair.1.after_ref.rest_0_), channel_id=1, source_target_pairs={{0,2},{1,3},{2,4},{3,5},{4,6},{5,7},{6,0},{7,1},{8,10},{9,11},{10,... | collective-permute-start | bytes 430088 | tf_op jit(solution)/shard_map/ppermute | solution.py:421
  19.8 18.7 %collective-permute-start.2 = (bf16[112,640]{1,0:T(8,128)(2,1)S(1)}, bf16[112,640]{1,0:T(8,128)(2,1)S(1)}, u32[]{:S(2)}, u32[]{:S(2)}) collective-permute-start(bf16[112,640]{1,0:T(8,128)(2,1)S(1)} %pair.1.after_ref.rest_0_), channel_id=1, source_target_pairs={{0,7},{1,0},{2,1},{3,2},{4,3},{5,4},{6,5},{7,6},{8,15},{9,8},{10,9... | collective-permute-start | bytes 430088 | tf_op jit(solution)/shard_map/ppermute | solution.py:421
  21.8 16.8 %collective-permute-start.1 = (bf16[112,640]{1,0:T(8,128)(2,1)S(1)}, bf16[112,640]{1,0:T(8,128)(2,1)S(1)}, u32[]{:S(2)}, u32[]{:S(2)}) collective-permute-start(bf16[112,640]{1,0:T(8,128)(2,1)S(1)} %pair.1.after_ref.rest_0_), channel_id=1, source_target_pairs={{0,1},{1,2},{2,3},{3,4},{4,5},{5,6},{6,7},{7,0},{8,9},{9,10},{10,1... | collective-permute-start | bytes 430088 | tf_op jit(solution)/shard_map/ppermute | solution.py:421
  26.7 11.9 %copy-start = (bf16[768,384]{1,0:T(8,128)(2,1)S(1)}, bf16[768,384]{1,0:T(8,128)(2,1)}, u32[]{:S(2)}) copy-start(bf16[768,384]{1,0:T(8,128)(2,1)} %constant.7.clone.lift_ref) | copy-start | bytes 1769476
  26.7 11.9 %copy-start.1 = (bf16[384,768]{1,0:T(8,128)(2,1)S(1)}, bf16[384,768]{1,0:T(8,128)(2,1)}, u32[]{:S(2)}) copy-start(bf16[384,768]{1,0:T(8,128)(2,1)} %constant.6.clone.sel_ref) | copy-start | bytes 1769476
  26.7 11.9 %copy-start.4 = (f32[1,15360]{1,0:T(1,128)S(1)}, f32[1,15360]{1,0:T(1,128)}, u32[]{:S(2)}) copy-start(f32[1,15360]{1,0:T(1,128)} %param.16) | copy-start | bytes 184324
  26.7 11.9 %copy-start.5 = (f32[8,384]{1,0:T(8,128)S(1)}, f32[8,384]{1,0:T(8,128)}, u32[]{:S(2)}) copy-start(f32[8,384]{1,0:T(8,128)} %constant.8.clone.inc_ref) | copy-start | bytes 36868
  26.7 11.9 %copy-start.6 = (s32[1,192,1]{1,2,0:T(1,128)S(1)}, s32[1,192,1]{1,2,0:T(1,128)}, u32[]{:S(2)}) copy-start(s32[1,192,1]{1,2,0:T(1,128)} %param.21) | copy-start | bytes 2308
  26.7 11.9 %copy-start.7 = (s32[1,192]{1,0:T(1,128)S(1)}, s32[1,192]{1,0:T(1,128)}, u32[]{:S(2)}) copy-start(s32[1,192]{1,0:T(1,128)} %far_ref.1) | copy-start | bytes 2308
  26.7 11.9 %copy-start.8 = (s32[1,192]{1,0:T(1,128)S(1)}, s32[1,192]{1,0:T(1,128)}, u32[]{:S(2)}) copy-start(s32[1,192]{1,0:T(1,128)} %near_ref.1) | copy-start | bytes 2308
  26.7 11.9 %copy-start.9 = (s32[1,192]{1,0:T(1,128)S(1)}, s32[1,192]{1,0:T(1,128)}, u32[]{:S(2)}) copy-start(s32[1,192]{1,0:T(1,128)} %cls_ref.1) | copy-start | bytes 2308
  26.7 11.9 %copy-start.10 = (f32[16]{0:T(128)S(1)}, f32[16]{0:T(128)}, u32[]{:S(2)}) copy-start(f32[16]{0:T(128)} %param.20) | copy-start | bytes 196
  26.7 11.8 %all-to-all-start.1 = ((f32[32,8,128]{2,1,0:T(8,128)}), f32[32,8,128]{2,1,0:T(8,128)S(1)}, u32[]{:S(2)}, u32[]{:S(2)}) async-start(f32[32,8,128]{2,1,0:T(8,128)} %bitcast.5), calls=%async_computation.1 | async-start | bytes 262144 | tf_op jit(solution)/shard_map/all_to_all | solution.py:428

commit v7 on v6

--- a/solution.py
+++ b/solution.py
@@ -294,9 +294,9 @@
 
 
 def flux_kernel(
-    quad_ref, dev_ref, far_ref, near_ref, cls_ref, src_ref, time_ref, jac_ref, sel_ref, lift_ref, inc_ref, elem_ref, *rest
+    quad_ref, dev_ref, far_ref, near_ref, cls_ref, jac_ref, sel_ref, lift_ref, inc_ref, elem_ref, *rest
 ):
-    tables, (res_ref, prod_ref, scratch) = rest[:-3], rest[-3:]
+    tables, out_ref = rest[:-1], rest[-1]
     me = lax.axis_index("space")
     far = far_ref[...]
     near = near_ref[...]
@@ -359,14 +359,35 @@
     for f in range(6):
         coef = coef + weight_sum[f * E_DEV : (f + 1) * E_DEV] * inc_ref[f : f + 1, :]
     fields_own = vector_tiles(elem_ref[:E_DEV, :].astype(F32))
+    for k in range(2):
+        own = jnp.concatenate(fields_own[k][:3], axis=1)
+        rows_k = slice(k * E_DEV, (k + 1) * E_DEV)
+        out_ref[rows_k, :] = jac_ref[rows_k, :] + coef * own - lifted[rows_k]
+
+
+def space_terms(quad, dev, far, near, cls, jac_terms, elem, tables):
+    sel = np.zeros((384, 768), np.float32)
+    sel[:DOF] = face_selector()
+    vmem = pl.BlockSpec(memory_space=pltpu.VMEM)
+    return pl.pallas_call(
+        flux_kernel,
+        out_shape=jax.ShapeDtypeStruct((2 * E_DEV, 384), F32),
+        in_specs=[vmem] * (10 + len(tables)),
+        out_specs=vmem,
+        compiler_params=pltpu.CompilerParams(vmem_limit_bytes=12 * MIB),
+        name="space_terms",
+    )(
+        quad.reshape(1, 16), dev, far, near, cls, jac_terms,
+        jnp.asarray(sel, BF16), jnp.asarray(sel.T, BF16), jnp.asarray(face_incidence()), elem, *tables,
+    )
+
+
+def final_kernel(src_ref, time_ref, space_ref, res_ref, prod_ref, scratch):
     half = E_DEV // 2
     low = lane_half(half)
     for k, out_ref in enumerate((res_ref, prod_ref)):
-        own = jnp.concatenate(fields_own[k][:3], axis=1)
-        rows_k = slice(k * E_DEV, (k + 1) * E_DEV)
-        total_k = jac_ref[rows_k, :] + coef * own - lifted[rows_k]
         for q in range(3):
-            scratch[q] = total_k[:, q * 128 : (q + 1) * 128]
+            scratch[q] = space_ref[k * E_DEV : (k + 1) * E_DEV, q * 128 : (q + 1) * 128]
         even = [scratch[q, pl.ds(0, half, stride=2), :] for q in range(3)]
         odd = [scratch[q, pl.ds(1, half, stride=2), :] for q in range(3)]
         tiles = [
@@ -383,22 +404,17 @@
             out_ref[pl.ds(q, half, stride=5), :] = at
 
 
-def finish(quad, dev, far, near, cls, source, time_terms, jac_terms, elem, tables):
-    sel = np.zeros((384, 768), np.float32)
-    sel[:DOF] = face_selector()
+def finish(source, time_parts, space):
     vmem = pl.BlockSpec(memory_space=pltpu.VMEM)
     return pl.pallas_call(
-        flux_kernel,
+        final_kernel,
         out_shape=(jax.ShapeDtypeStruct((ROWS, 128), F32),) * 2,
-        in_specs=[vmem] * (12 + len(tables)),
+        in_specs=[vmem] * 3,
         out_specs=(vmem, vmem),
         scratch_shapes=[pltpu.VMEM((3, E_DEV, 128), F32)],
-        compiler_params=pltpu.CompilerParams(vmem_limit_bytes=12 * MIB),
+        compiler_params=pltpu.CompilerParams(vmem_limit_bytes=4 * MIB),
         name="finish",
-    )(
-        quad.reshape(1, 16), dev, far, near, cls, source, time_terms, jac_terms,
-        jnp.asarray(sel, BF16), jnp.asarray(sel.T, BF16), jnp.asarray(face_incidence()), elem, *tables,
-    )
+    )(source, time_parts, space)
 
 
 def per_device(
@@ -427,18 +443,17 @@
     back = spectral_sum(coef, received, pair)
     time_terms = lax.all_to_all(back, "inst", 0, 0, tiled=True)
     jac_terms = jacobian_product(jacobian, elem, back)
-    residual, product = finish(
+    space = space_terms(
         quad_weight,
         partner_device.reshape(1, SLOTS_DEV),
         partner_face,
         local_face,
         weight_index,
-        source.reshape(ROWS, 128),
-        time_terms,
         jac_terms,
         elem,
         [pair] + others,
     )
+    residual, product = finish(source.reshape(ROWS, 128), time_terms, space)
     return residual.reshape(1, FLAT), product.reshape(1, FLAT)
 
 

time: 41.1 us -> 39.5 us (0.961)
  waiting for transfers between devices: 6.58 us -> 4.98 us
    all_to_all x1, waiting for transfers between devices: 2.49 us -> 0.89 us  [per_device(): time_terms = lax.all_to_all(back, 'inst', 0, 0, tiled=True)]
    pallas_call x1 -> x2, Pallas kernels: 2.2 us -> 2.22 us  [the longest x1 1.48 us: space_terms(): pl.pallas_call(flux_kernel, out_shape=jax.ShapeDtypeStruct((2 * E_DEV, 38...]
  transfers between devices with their start and end apart: 6 -> 6, of which waited for: 2 -> 2; matrix products, arithmetic and copies ran while one was open for 0% -> 0% of each run, Pallas kernels for 15% -> 19%
where the time goes in v7:
time: 39.5 us; the launch traced here: 39.3 us
  starting transfers between devices  23 us (58%)
  Pallas kernels  9.04 us (23%)
  waiting for transfers between devices  4.98 us (13%)
  between operations  2.16 us (5%)
    ppermute x4, starting transfers between devices, over_space(): lax.ppermute(x, 'space', [(i, (i + turn) % N_SPACE) for i in range(N_SPAC...  10.9 us
    all_to_all x1, starting transfers between devices, per_device(): received = lax.all_to_all(lin, 'inst', 0, 0, tiled=True)  8.04 us
    pallas_call x1, Pallas kernels, jacobian_product(): pl.pallas_call(jacobian_kernel, out_shape=jax.ShapeDtypeStruct((2 * E_DEV...  5.24 us
    all_to_all x1, waiting for transfers between devices, per_device(): received = lax.all_to_all(lin, 'inst', 0, 0, tiled=True)  4.08 us
    all_to_all x1, starting transfers between devices, per_device(): time_terms = lax.all_to_all(back, 'inst', 0, 0, tiled=True)  4.04 us
    pallas_call x1, Pallas kernels, space_terms(): pl.pallas_call(flux_kernel, out_shape=jax.ShapeDtypeStruct((2 * E_DEV, 38...  1.48 us
    all_to_all x1, waiting for transfers between devices, per_device(): time_terms = lax.all_to_all(back, 'inst', 0, 0, tiled=True)  0.89 us
    pallas_call x1, Pallas kernels, spectral_sum(): pl.pallas_call(spectral_kernel, out_shape=jax.ShapeDtypeStruct((256, 128)...  0.81 us
  transfers between devices with their start and end apart: 6, of which 2 were waited for; matrix products, arithmetic and copies ran while one was open for 0% of the time, Pallas kernels for 19%

profile of v7, /device:TPU:1, one launch (start us, length us, event | category | flops | bytes accessed | tf_op | source)
XLA Modules:
  0.0 39.3 jit_solution(17624582097635862805)
XLA Ops:
  0.6 0.0 copy-start.3
  0.6 0.0 copy-start.2
  2.0 0.0 copy-done.3
  2.0 0.0 copy-done.2
  2.0 0.7 %prep.1 = (bf16[256,128]{1,0:T(8,128)(2,1)}, bf16[56,640]{1,0:T(8,128)(2,1)S(1)}) custom-call(f32[32,128]{1,0:T(8,128)S(1)} %coefficients.1.mark_ref.coef_ref, bf16[1,15360]{1,0:T(2,128)(2,1)S(1)} %copy-done.2, bf16[1,15360]{1,0:T(2,128)(2,1)S(1)} %copy-done.3), custom_call_target="tpu_custom_call" | custom-call | tf_op jit(solution)/shard_map/prep/pallas_call | solution.py:120
  2.7 7.7 %collective-permute-start = (bf16[56,640]{1,0:T(8,128)(2,1)S(1)}, bf16[56,640]{1,0:T(8,128)(2,1)S(1)}, u32[]{:S(2)}, u32[]{:S(2)}) collective-permute-start(bf16[56,640]{1,0:T(8,128)(2,1)S(1)} %get-tuple-element.7.own_ref.elem_ref), channel_id=1, source_target_pairs={{0,4},{1,5},{2,6},{3,7},{4,0},{5,1},{6,2},{7,3},{8,12},{9,13},{10,... | collective-permute-start | bytes 215048 | tf_op jit(solution)/shard_map/ppermute | solution.py:437
  10.5 8.0 %all-to-all-start = ((bf16[32,8,128]{2,1,0:T(8,128)(2,1)}), bf16[32,8,128]{2,1,0:T(8,128)(2,1)S(1)}, u32[]{:S(2)}, u32[]{:S(2)}) async-start(bf16[32,8,128]{2,1,0:T(8,128)(2,1)} %bitcast.1), calls=%async_computation | async-start | bytes 131072 | tf_op jit(solution)/shard_map/all_to_all | solution.py:440
  18.5 0.0 collective-permute-done.across_ref
  18.6 1.3 %collective-permute-start.3 = (bf16[112,640]{1,0:T(8,128)(2,1)S(1)}, bf16[112,640]{1,0:T(8,128)(2,1)S(1)}, u32[]{:S(2)}, u32[]{:S(2)}) collective-permute-start(bf16[112,640]{1,0:T(8,128)(2,1)S(1)} %pair.1.after_ref.rest_0_), channel_id=1, source_target_pairs={{0,2},{1,3},{2,4},{3,5},{4,6},{5,7},{6,0},{7,1},{8,10},{9,11},{10,... | collective-permute-start | bytes 430088 | tf_op jit(solution)/shard_map/ppermute | solution.py:437
  19.8 1.9 %collective-permute-start.2 = (bf16[112,640]{1,0:T(8,128)(2,1)S(1)}, bf16[112,640]{1,0:T(8,128)(2,1)S(1)}, u32[]{:S(2)}, u32[]{:S(2)}) collective-permute-start(bf16[112,640]{1,0:T(8,128)(2,1)S(1)} %pair.1.after_ref.rest_0_), channel_id=1, source_target_pairs={{0,7},{1,0},{2,1},{3,2},{4,3},{5,4},{6,5},{7,6},{8,15},{9,8},{10,9... | collective-permute-start | bytes 430088 | tf_op jit(solution)/shard_map/ppermute | solution.py:437
  21.8 0.0 collective-permute-start.1
  21.8 4.1 %all-to-all-done = bf16[32,8,128]{2,1,0:T(8,128)(2,1)S(1)} async-done(((bf16[32,8,128]{2,1,0:T(8,128)(2,1)}), bf16[32,8,128]{2,1,0:T(8,128)(2,1)S(1)}, u32[]{:S(2)}, u32[]{:S(2)}) %all-to-all-start) | async-done | bytes 65568 | tf_op jit(solution)/shard_map/all_to_all | solution.py:440
  25.8 0.8 %spectral.1.after_ref = f32[256,128]{1,0:T(8,128)} custom-call(f32[32,128]{1,0:T(8,128)S(1)} %coefficients.1.mark_ref.coef_ref, bf16[256,128]{1,0:T(8,128)(2,1)S(1)} %bitcast.10, bf16[112,640]{1,0:T(8,128)(2,1)S(1)} %pair.1.after_ref.rest_0_), custom_call_target="tpu_custom_call" | custom-call | flops 10000000000 | tf_op jit(solution)/shard_map/spectral/pallas_call | solution.py:187
  26.7 0.0 copy-start
  26.7 0.0 copy-start.1
  26.7 0.0 copy-start.5
  26.7 0.0 copy-start.6
  26.7 0.0 copy-start.7
  26.7 0.0 copy-start.8
  26.7 0.0 copy-start.9
  26.7 0.0 copy-start.10
  26.7 0.0 copy-start.4
  26.7 4.0 %all-to-all-start.1 = ((f32[32,8,128]{2,1,0:T(8,128)}), f32[32,8,128]{2,1,0:T(8,128)S(1)}, u32[]{:S(2)}, u32[]{:S(2)}) async-start(f32[32,8,128]{2,1,0:T(8,128)} %bitcast.3), calls=%async_computation.1 | async-start | bytes 262144 | tf_op jit(solution)/shard_map/all_to_all | solution.py:444
  30.8 5.2 %jacobian.1.jac_ref = f32[96,384]{1,0:T(8,128)S(1)} custom-call(bf16[1,48,102400]{2,1,0:T(8,128)(2,1)} %jac_hbm.1, bf16[56,640]{1,0:T(8,128)(2,1)S(1)} %get-tuple-element.7.own_ref.elem_ref, f32[256,128]{1,0:T(8,128)} %spectral.1.after_ref), custom_call_target="tpu_custom_call" | custom-call | flops 943718400 | bytes 9830400 | tf_op jit(solution)/shard_map/jacobian/pallas_call | solution.py:267
  36.0 0.0 collective-permute-done.3.rest_3_
  36.0 0.0 collective-permute-done.2.rest_2_
  36.0 0.0 collective-permute-done.1.rest_1_
  36.1 0.0 copy-done
  36.1 0.0 copy-done.1
  36.1 0.0 copy-done.5
  36.1 0.0 copy-done.6
  36.1 0.0 copy-done.7
  36.1 0.0 copy-done.8
  36.1 0.0 copy-done.9
  36.1 0.0 copy-done.10
  36.1 1.5 %space_terms.1.space_ref = f32[96,384]{1,0:T(8,128)S(1)} custom-call(f32[1,16]{1,0:T(1,128)S(1)} %bitcast.13, s32[1,192]{1,0:T(1,128)S(1)} %bitcast.12, s32[1,192]{1,0:T(1,128)S(1)} %copy-done.7, s32[1,192]{1,0:T(1,128)S(1)} %copy-done.8, s32[1,192]{1,0:T(1,128)S(1)} %copy-done.9, f32[96,384]{1,0:T(8,128)S(1)} %jacobian.1.jac_ref, ...), custom_call_target="tpu_custom_call" | custom-call | tf_op jit(solution)/shard_map/space_terms/pallas_call | solution.py:372
  37.6 0.9 %all-to-all-done.1 = f32[32,8,128]{2,1,0:T(8,128)S(1)} async-done(((f32[32,8,128]{2,1,0:T(8,128)}), f32[32,8,128]{2,1,0:T(8,128)S(1)}, u32[]{:S(2)}, u32[]{:S(2)}) %all-to-all-start.1) | async-done | bytes 131104 | tf_op jit(solution)/shard_map/all_to_all | solution.py:444
  38.5 0.0 copy-done.4
  38.5 0.7 %finish.1 = (f32[120,128]{1,0:T(8,128)}, f32[120,128]{1,0:T(8,128)}) custom-call(f32[120,128]{1,0:T(8,128)S(1)} %bitcast.11, f32[256,128]{1,0:T(8,128)S(1)} %bitcast.9, f32[96,384]{1,0:T(8,128)S(1)} %space_terms.1.space_ref), custom_call_target="tpu_custom_call" | custom-call | tf_op jit(solution)/shard_map/finish/pallas_call | solution.py:409
  (2 shorter events, 0.0 us)
Async XLA Ops:
  0.6 1.4 %copy-start.3 = (bf16[1,15360]{1,0:T(2,128)(2,1)S(1)}, bf16[1,15360]{1,0:T(2,128)(2,1)}, u32[]{:S(2)}) copy-start(bf16[1,15360]{1,0:T(2,128)(2,1)} %d_ref.1) | copy-start | bytes 92164
  0.6 1.4 %copy-start.2 = (bf16[1,15360]{1,0:T(2,128)(2,1)S(1)}, bf16[1,15360]{1,0:T(2,128)(2,1)}, u32[]{:S(2)}) copy-start(bf16[1,15360]{1,0:T(2,128)(2,1)} %s_ref.1) | copy-start | bytes 92164
  2.7 15.8 %collective-permute-start = (bf16[56,640]{1,0:T(8,128)(2,1)S(1)}, bf16[56,640]{1,0:T(8,128)(2,1)S(1)}, u32[]{:S(2)}, u32[]{:S(2)}) collective-permute-start(bf16[56,640]{1,0:T(8,128)(2,1)S(1)} %get-tuple-element.7.own_ref.elem_ref), channel_id=1, source_target_pairs={{0,4},{1,5},{2,6},{3,7},{4,0},{5,1},{6,2},{7,3},{8,12},{9,13},{10,... | collective-permute-start | bytes 215048 | tf_op jit(solution)/shard_map/ppermute | solution.py:437
  10.5 15.4 %all-to-all-start = ((bf16[32,8,128]{2,1,0:T(8,128)(2,1)}), bf16[32,8,128]{2,1,0:T(8,128)(2,1)S(1)}, u32[]{:S(2)}, u32[]{:S(2)}) async-start(bf16[32,8,128]{2,1,0:T(8,128)(2,1)} %bitcast.1), calls=%async_computation | async-start | bytes 131072 | tf_op jit(solution)/shard_map/all_to_all | solution.py:440
  18.6 17.5 %collective-permute-start.3 = (bf16[112,640]{1,0:T(8,128)(2,1)S(1)}, bf16[112,640]{1,0:T(8,128)(2,1)S(1)}, u32[]{:S(2)}, u32[]{:S(2)}) collective-permute-start(bf16[112,640]{1,0:T(8,128)(2,1)S(1)} %pair.1.after_ref.rest_0_), channel_id=1, source_target_pairs={{0,2},{1,3},{2,4},{3,5},{4,6},{5,7},{6,0},{7,1},{8,10},{9,11},{10,... | collective-permute-start | bytes 430088 | tf_op jit(solution)/shard_map/ppermute | solution.py:437
  19.8 16.2 %collective-permute-start.2 = (bf16[112,640]{1,0:T(8,128)(2,1)S(1)}, bf16[112,640]{1,0:T(8,128)(2,1)S(1)}, u32[]{:S(2)}, u32[]{:S(2)}) collective-permute-start(bf16[112,640]{1,0:T(8,128)(2,1)S(1)} %pair.1.after_ref.rest_0_), channel_id=1, source_target_pairs={{0,7},{1,0},{2,1},{3,2},{4,3},{5,4},{6,5},{7,6},{8,15},{9,8},{10,9... | collective-permute-start | bytes 430088 | tf_op jit(solution)/shard_map/ppermute | solution.py:437
  21.8 14.3 %collective-permute-start.1 = (bf16[112,640]{1,0:T(8,128)(2,1)S(1)}, bf16[112,640]{1,0:T(8,128)(2,1)S(1)}, u32[]{:S(2)}, u32[]{:S(2)}) collective-permute-start(bf16[112,640]{1,0:T(8,128)(2,1)S(1)} %pair.1.after_ref.rest_0_), channel_id=1, source_target_pairs={{0,1},{1,2},{2,3},{3,4},{4,5},{5,6},{6,7},{7,0},{8,9},{9,10},{10,1... | collective-permute-start | bytes 430088 | tf_op jit(solution)/shard_map/ppermute | solution.py:437
  26.7 9.4 %copy-start = (bf16[768,384]{1,0:T(8,128)(2,1)S(1)}, bf16[768,384]{1,0:T(8,128)(2,1)}, u32[]{:S(2)}) copy-start(bf16[768,384]{1,0:T(8,128)(2,1)} %constant.7.clone.lift_ref) | copy-start | bytes 1769476
  26.7 9.4 %copy-start.1 = (bf16[384,768]{1,0:T(8,128)(2,1)S(1)}, bf16[384,768]{1,0:T(8,128)(2,1)}, u32[]{:S(2)}) copy-start(bf16[384,768]{1,0:T(8,128)(2,1)} %constant.6.clone.sel_ref) | copy-start | bytes 1769476
  26.7 9.4 %copy-start.5 = (f32[8,384]{1,0:T(8,128)S(1)}, f32[8,384]{1,0:T(8,128)}, u32[]{:S(2)}) copy-start(f32[8,384]{1,0:T(8,128)} %constant.8.clone.inc_ref) | copy-start | bytes 36868
  26.7 9.4 %copy-start.6 = (s32[1,192,1]{1,2,0:T(1,128)S(1)}, s32[1,192,1]{1,2,0:T(1,128)}, u32[]{:S(2)}) copy-start(s32[1,192,1]{1,2,0:T(1,128)} %param.21) | copy-start | bytes 2308
  26.7 9.4 %copy-start.7 = (s32[1,192]{1,0:T(1,128)S(1)}, s32[1,192]{1,0:T(1,128)}, u32[]{:S(2)}) copy-start(s32[1,192]{1,0:T(1,128)} %far_ref.1) | copy-start | bytes 2308
  26.7 9.4 %copy-start.8 = (s32[1,192]{1,0:T(1,128)S(1)}, s32[1,192]{1,0:T(1,128)}, u32[]{:S(2)}) copy-start(s32[1,192]{1,0:T(1,128)} %near_ref.1) | copy-start | bytes 2308
  26.7 9.4 %copy-start.9 = (s32[1,192]{1,0:T(1,128)S(1)}, s32[1,192]{1,0:T(1,128)}, u32[]{:S(2)}) copy-start(s32[1,192]{1,0:T(1,128)} %cls_ref.1) | copy-start | bytes 2308
  26.7 9.4 %copy-start.10 = (f32[16]{0:T(128)S(1)}, f32[16]{0:T(128)}, u32[]{:S(2)}) copy-start(f32[16]{0:T(128)} %param.20) | copy-start | bytes 196
  26.7 11.8 %copy-start.4 = (f32[1,15360]{1,0:T(1,128)S(1)}, f32[1,15360]{1,0:T(1,128)}, u32[]{:S(2)}) copy-start(f32[1,15360]{1,0:T(1,128)} %param.16) | copy-start | bytes 184324
  26.7 11.8 %all-to-all-start.1 = ((f32[32,8,128]{2,1,0:T(8,128)}), f32[32,8,128]{2,1,0:T(8,128)S(1)}, u32[]{:S(2)}, u32[]{:S(2)}) async-start(f32[32,8,128]{2,1,0:T(8,128)} %bitcast.3), calls=%async_computation.1 | async-start | bytes 262144 | tf_op jit(solution)/shard_map/all_to_all | solution.py:444

commit v8 on v7

--- a/solution.py
+++ b/solution.py
@@ -131,22 +131,22 @@
     )(mark, state, direction)
 
 
-def pair_kernel(own_ref, across_ref, pair_ref):
+def pair_kernel(own_ref, across_ref, after_ref, pair_ref):
     pair_ref[:E_DEV, :] = own_ref[:E_DEV, :]
     pair_ref[E_DEV : 2 * E_DEV, :] = across_ref[:E_DEV, :]
     pair_ref[2 * E_DEV :, :] = jnp.zeros((SPARE, 2 * DOF), BF16)
 
 
-def make_pair(own, across):
+def make_pair(own, across, after):
     vmem = pl.BlockSpec(memory_space=pltpu.VMEM)
     return pl.pallas_call(
         pair_kernel,
         out_shape=jax.ShapeDtypeStruct((2 * E_DEV + SPARE, 2 * DOF), BF16),
-        in_specs=[vmem, vmem],
+        in_specs=[vmem, vmem, pl.BlockSpec(memory_space=pl.ANY)],
         out_specs=vmem,
         compiler_params=pltpu.CompilerParams(vmem_limit_bytes=2 * MIB),
         name="pair",
-    )(own, across)
+    )(own, across, after)
 
 
 def spectral_kernel(coef_ref, x_ref, after_ref, y_ref):
@@ -307,7 +307,7 @@
     near_row = (near - near_e * 6) * E_DEV + near_e
     turn = (dev_ref[...] - me) & (N_SPACE - 1)
     block = jnp.zeros((1, SLOTS_DEV), jnp.int32)
-    for at, which in enumerate((0, 4, 7, 3, 1, 5, 6, 2)):
+    for at, which in enumerate((0, 4, 7, 3, 6, 2, 1, 5)):
         block = jnp.where(turn == which, at, block)
     column = block * E_DEV + far_e
     w = jnp.zeros((1, SLOTS_DEV), F32)
@@ -321,7 +321,7 @@
     far_ls = code >> 9
     total = N_SPACE * E_DEV
     pick = (lax.broadcasted_iota(jnp.int32, (SLOTS_DEV, total), 1) == column_s).astype(F32).astype(BF16)
-    table = jnp.concatenate([t[: 2 * E_DEV, :] for t in tables], axis=0)
+    table = jnp.concatenate([t[: (2 if at < 3 else 1) * E_DEV, :] for at, t in enumerate(tables)], axis=0)
     got = jnp.dot(pick, table, preferred_element_type=F32)
     p = [got[:, q * 128 : (q + 1) * 128] for q in range(5)]
     low = lane_half(SLOTS_DEV)
@@ -436,10 +436,11 @@
     def over_space(x, turn):
         return lax.ppermute(x, "space", [(i, (i + turn) % N_SPACE) for i in range(N_SPACE)])
 
+    right = over_space(elem, -1)
     across = over_space(elem, 4)
     received = lax.all_to_all(lin, "inst", 0, 0, tiled=True)
-    pair = make_pair(elem, across)
-    others = [over_space(pair, turn) for turn in (1, -1, 2)]
+    pair = make_pair(elem, across, right)
+    others = [over_space(pair, 1), over_space(pair, 2), right, over_space(elem, 3)]
     back = spectral_sum(coef, received, pair)
     time_terms = lax.all_to_all(back, "inst", 0, 0, tiled=True)
     jac_terms = jacobian_product(jacobian, elem, back)

time: 39.5 us -> 42.5 us (1.076); the launches traced: 39.3 us -> 41.6 us
  starting transfers between devices: 23 us -> 25.4 us
    ppermute x4 -> x5, starting transfers between devices: 10.9 us -> 13.3 us  [over_space(): lax.ppermute(x, 'space', [(i, (i + turn) % N_SPACE) for i in range(N_SPAC...]
    all_to_all x1, waiting for transfers between devices: 0.89 us -> 0.01 us  [per_device(): time_terms = lax.all_to_all(back, 'inst', 0, 0, tiled=True)]
    ppermute x4 -> x5, waiting for transfers between devices: 0.01 us -> 0.56 us  [over_space(): lax.ppermute(x, 'space', [(i, (i + turn) % N_SPACE) for i in range(N_SPAC...]
  transfers between devices with their start and end apart: 6 -> 7, of which waited for: 2 -> 2; matrix products, arithmetic and copies ran while one was open for 0% -> 0% of each run, Pallas kernels for 19% -> 18%
where the time goes in v8:
time: 42.5 us; the launch traced here: 41.6 us
  starting transfers between devices  25.4 us (60%)
  Pallas kernels  9.05 us (21%)
  waiting for transfers between devices  4.93 us (12%)
  between operations  2.15 us (5%)
    ppermute x5, starting transfers between devices, over_space(): lax.ppermute(x, 'space', [(i, (i + turn) % N_SPACE) for i in range(N_SPAC...  13.3 us
    all_to_all x1, starting transfers between devices, per_device(): received = lax.all_to_all(lin, 'inst', 0, 0, tiled=True)  8.14 us
    pallas_call x1, Pallas kernels, jacobian_product(): pl.pallas_call(jacobian_kernel, out_shape=jax.ShapeDtypeStruct((2 * E_DEV...  5.24 us
    all_to_all x1, waiting for transfers between devices, per_device(): received = lax.all_to_all(lin, 'inst', 0, 0, tiled=True)  4.37 us
    all_to_all x1, starting transfers between devices, per_device(): time_terms = lax.all_to_all(back, 'inst', 0, 0, tiled=True)  4.03 us
    pallas_call x1, Pallas kernels, space_terms(): pl.pallas_call(flux_kernel, out_shape=jax.ShapeDtypeStruct((2 * E_DEV, 38...  1.48 us
  transfers between devices with their start and end apart: 7, of which 2 were waited for; matrix products, arithmetic and copies ran while one was open for 0% of the time, Pallas kernels for 18%

profile of v8, /device:TPU:1, one launch (start us, length us, event | category | flops | bytes accessed | tf_op | source)
XLA Modules:
  0.0 41.6 jit_solution(9312812525010929428)
XLA Ops:
  0.6 0.0 copy-start.3
  0.6 0.0 copy-start.2
  2.0 0.0 copy-done.3
  2.0 0.0 copy-done.2
  2.0 0.7 %prep.1 = (bf16[256,128]{1,0:T(8,128)(2,1)}, bf16[56,640]{1,0:T(8,128)(2,1)S(1)}) custom-call(f32[32,128]{1,0:T(8,128)S(1)} %coefficients.1.mark_ref.coef_ref, bf16[1,15360]{1,0:T(2,128)(2,1)S(1)} %copy-done.2, bf16[1,15360]{1,0:T(2,128)(2,1)S(1)} %copy-done.3), custom_call_target="tpu_custom_call" | custom-call | tf_op jit(solution)/shard_map/prep/pallas_call | solution.py:120
  2.7 6.4 %collective-permute-start.1 = (bf16[56,640]{1,0:T(8,128)(2,1)S(1)}, bf16[56,640]{1,0:T(8,128)(2,1)S(1)}, u32[]{:S(2)}, u32[]{:S(2)}) collective-permute-start(bf16[56,640]{1,0:T(8,128)(2,1)S(1)} %get-tuple-element.7.own_ref.elem_ref), channel_id=1, source_target_pairs={{0,7},{1,0},{2,1},{3,2},{4,3},{5,4},{6,5},{7,6},{8,15},{9,8},{10,9... | collective-permute-start | bytes 215048 | tf_op jit(solution)/shard_map/ppermute | solution.py:437
  9.2 1.3 %collective-permute-start = (bf16[56,640]{1,0:T(8,128)(2,1)S(1)}, bf16[56,640]{1,0:T(8,128)(2,1)S(1)}, u32[]{:S(2)}, u32[]{:S(2)}) collective-permute-start(bf16[56,640]{1,0:T(8,128)(2,1)S(1)} %get-tuple-element.7.own_ref.elem_ref), channel_id=1, source_target_pairs={{0,4},{1,5},{2,6},{3,7},{4,0},{5,1},{6,2},{7,3},{8,12},{9,13},{10,... | collective-permute-start | bytes 215048 | tf_op jit(solution)/shard_map/ppermute | solution.py:437
  10.5 8.1 %all-to-all-start = ((bf16[32,8,128]{2,1,0:T(8,128)(2,1)}), bf16[32,8,128]{2,1,0:T(8,128)(2,1)S(1)}, u32[]{:S(2)}, u32[]{:S(2)}) async-start(bf16[32,8,128]{2,1,0:T(8,128)(2,1)} %bitcast.1), calls=%async_computation | async-start | bytes 131072 | tf_op jit(solution)/shard_map/all_to_all | solution.py:441
  18.6 0.0 collective-permute-done.1.after_ref.rest_3_
  18.6 0.0 collective-permute-done.across_ref
  18.7 2.2 %collective-permute-start.3 = (bf16[112,640]{1,0:T(8,128)(2,1)S(1)}, bf16[112,640]{1,0:T(8,128)(2,1)S(1)}, u32[]{:S(2)}, u32[]{:S(2)}) collective-permute-start(bf16[112,640]{1,0:T(8,128)(2,1)S(1)} %pair.1.after_ref.rest_0_), channel_id=1, source_target_pairs={{0,2},{1,3},{2,4},{3,5},{4,6},{5,7},{6,0},{7,1},{8,10},{9,11},{10,... | collective-permute-start | bytes 430088 | tf_op jit(solution)/shard_map/ppermute | solution.py:437
  20.9 0.7 %collective-permute-start.2 = (bf16[112,640]{1,0:T(8,128)(2,1)S(1)}, bf16[112,640]{1,0:T(8,128)(2,1)S(1)}, u32[]{:S(2)}, u32[]{:S(2)}) collective-permute-start(bf16[112,640]{1,0:T(8,128)(2,1)S(1)} %pair.1.after_ref.rest_0_), channel_id=1, source_target_pairs={{0,1},{1,2},{2,3},{3,4},{4,5},{5,6},{6,7},{7,0},{8,9},{9,10},{10,1... | collective-permute-start | bytes 430088 | tf_op jit(solution)/shard_map/ppermute | solution.py:437
  21.6 4.4 %all-to-all-done = bf16[32,8,128]{2,1,0:T(8,128)(2,1)S(1)} async-done(((bf16[32,8,128]{2,1,0:T(8,128)(2,1)}), bf16[32,8,128]{2,1,0:T(8,128)(2,1)S(1)}, u32[]{:S(2)}, u32[]{:S(2)}) %all-to-all-start) | async-done | bytes 65568 | tf_op jit(solution)/shard_map/all_to_all | solution.py:441
  26.0 0.8 %spectral.1.after_ref = f32[256,128]{1,0:T(8,128)} custom-call(f32[32,128]{1,0:T(8,128)S(1)} %coefficients.1.mark_ref.coef_ref, bf16[256,128]{1,0:T(8,128)(2,1)S(1)} %bitcast.10, bf16[112,640]{1,0:T(8,128)(2,1)S(1)} %pair.1.after_ref.rest_0_), custom_call_target="tpu_custom_call" | custom-call | flops 10000000000 | tf_op jit(solution)/shard_map/spectral/pallas_call | solution.py:187
  26.8 0.0 copy-start
  26.8 0.0 copy-start.1
  26.8 0.0 copy-start.5
  26.8 0.0 copy-start.6
  26.8 0.0 copy-start.7
  26.8 0.0 copy-start.8
  26.8 0.0 copy-start.9
  26.8 0.0 copy-start.10
  26.8 0.0 copy-start.4
  26.8 4.0 %all-to-all-start.1 = ((f32[32,8,128]{2,1,0:T(8,128)}), f32[32,8,128]{2,1,0:T(8,128)S(1)}, u32[]{:S(2)}, u32[]{:S(2)}) async-start(f32[32,8,128]{2,1,0:T(8,128)} %bitcast.3), calls=%async_computation.1 | async-start | bytes 262144 | tf_op jit(solution)/shard_map/all_to_all | solution.py:445
  30.9 2.6 %collective-permute-start.4 = (bf16[56,640]{1,0:T(8,128)(2,1)S(1)}, bf16[56,640]{1,0:T(8,128)(2,1)S(1)}, u32[]{:S(2)}, u32[]{:S(2)}) collective-permute-start(bf16[56,640]{1,0:T(8,128)(2,1)S(1)} %get-tuple-element.7.own_ref.elem_ref), channel_id=1, source_target_pairs={{0,3},{1,4},{2,5},{3,6},{4,7},{5,0},{6,1},{7,2},{8,11},{9,12},{10,... | collective-permute-start | bytes 215048 | tf_op jit(solution)/shard_map/ppermute | solution.py:437
  33.5 5.2 %jacobian.1.jac_ref = f32[96,384]{1,0:T(8,128)S(1)} custom-call(bf16[1,48,102400]{2,1,0:T(8,128)(2,1)} %jac_hbm.1, bf16[56,640]{1,0:T(8,128)(2,1)S(1)} %get-tuple-element.7.own_ref.elem_ref, f32[256,128]{1,0:T(8,128)} %spectral.1.after_ref), custom_call_target="tpu_custom_call" | custom-call | flops 943718400 | bytes 9830400 | tf_op jit(solution)/shard_map/jacobian/pallas_call | solution.py:267
  38.8 0.5 %collective-permute-done.4.rest_4_ = bf16[56,640]{1,0:T(8,128)(2,1)S(1)} collective-permute-done((bf16[56,640]{1,0:T(8,128)(2,1)S(1)}, bf16[56,640]{1,0:T(8,128)(2,1)S(1)}, u32[]{:S(2)}, u32[]{:S(2)}) %collective-permute-start.4) | collective-permute-done | bytes 71712 | tf_op jit(solution)/shard_map/ppermute | solution.py:437
  39.3 0.0 collective-permute-done.3.rest_2_
  39.3 0.0 collective-permute-done.2.rest_1_
  39.3 0.0 copy-done
  39.3 0.0 copy-done.1
  39.3 0.0 copy-done.5
  39.3 0.0 copy-done.6
  39.3 0.0 copy-done.7
  39.4 0.0 copy-done.8
  39.4 0.0 copy-done.9
  39.4 0.0 copy-done.10
  39.4 1.5 %space_terms.1.space_ref = f32[96,384]{1,0:T(8,128)S(1)} custom-call(f32[1,16]{1,0:T(1,128)S(1)} %bitcast.13, s32[1,192]{1,0:T(1,128)S(1)} %bitcast.12, s32[1,192]{1,0:T(1,128)S(1)} %copy-done.7, s32[1,192]{1,0:T(1,128)S(1)} %copy-done.8, s32[1,192]{1,0:T(1,128)S(1)} %copy-done.9, f32[96,384]{1,0:T(8,128)S(1)} %jacobian.1.jac_ref, ...), custom_call_target="tpu_custom_call" | custom-call | tf_op jit(solution)/shard_map/space_terms/pallas_call | solution.py:372
  40.9 0.0 all-to-all-done.1
  40.9 0.0 copy-done.4
  40.9 0.7 %finish.1 = (f32[120,128]{1,0:T(8,128)}, f32[120,128]{1,0:T(8,128)}) custom-call(f32[120,128]{1,0:T(8,128)S(1)} %bitcast.11, f32[256,128]{1,0:T(8,128)S(1)} %bitcast.9, f32[96,384]{1,0:T(8,128)S(1)} %space_terms.1.space_ref), custom_call_target="tpu_custom_call" | custom-call | tf_op jit(solution)/shard_map/finish/pallas_call | solution.py:409
  (2 shorter events, 0.0 us)
Async XLA Ops:
  0.6 1.4 %copy-start.3 = (bf16[1,15360]{1,0:T(2,128)(2,1)S(1)}, bf16[1,15360]{1,0:T(2,128)(2,1)}, u32[]{:S(2)}) copy-start(bf16[1,15360]{1,0:T(2,128)(2,1)} %d_ref.1) | copy-start | bytes 92164
  0.6 1.4 %copy-start.2 = (bf16[1,15360]{1,0:T(2,128)(2,1)S(1)}, bf16[1,15360]{1,0:T(2,128)(2,1)}, u32[]{:S(2)}) copy-start(bf16[1,15360]{1,0:T(2,128)(2,1)} %s_ref.1) | copy-start | bytes 92164
  2.7 15.9 %collective-permute-start.1 = (bf16[56,640]{1,0:T(8,128)(2,1)S(1)}, bf16[56,640]{1,0:T(8,128)(2,1)S(1)}, u32[]{:S(2)}, u32[]{:S(2)}) collective-permute-start(bf16[56,640]{1,0:T(8,128)(2,1)S(1)} %get-tuple-element.7.own_ref.elem_ref), channel_id=1, source_target_pairs={{0,7},{1,0},{2,1},{3,2},{4,3},{5,4},{6,5},{7,6},{8,15},{9,8},{10,9... | collective-permute-start | bytes 215048 | tf_op jit(solution)/shard_map/ppermute | solution.py:437
  9.2 9.5 %collective-permute-start = (bf16[56,640]{1,0:T(8,128)(2,1)S(1)}, bf16[56,640]{1,0:T(8,128)(2,1)S(1)}, u32[]{:S(2)}, u32[]{:S(2)}) collective-permute-start(bf16[56,640]{1,0:T(8,128)(2,1)S(1)} %get-tuple-element.7.own_ref.elem_ref), channel_id=1, source_target_pairs={{0,4},{1,5},{2,6},{3,7},{4,0},{5,1},{6,2},{7,3},{8,12},{9,13},{10,... | collective-permute-start | bytes 215048 | tf_op jit(solution)/shard_map/ppermute | solution.py:437
  10.5 15.5 %all-to-all-start = ((bf16[32,8,128]{2,1,0:T(8,128)(2,1)}), bf16[32,8,128]{2,1,0:T(8,128)(2,1)S(1)}, u32[]{:S(2)}, u32[]{:S(2)}) async-start(bf16[32,8,128]{2,1,0:T(8,128)(2,1)} %bitcast.1), calls=%async_computation | async-start | bytes 131072 | tf_op jit(solution)/shard_map/all_to_all | solution.py:441
  18.7 20.6 %collective-permute-start.3 = (bf16[112,640]{1,0:T(8,128)(2,1)S(1)}, bf16[112,640]{1,0:T(8,128)(2,1)S(1)}, u32[]{:S(2)}, u32[]{:S(2)}) collective-permute-start(bf16[112,640]{1,0:T(8,128)(2,1)S(1)} %pair.1.after_ref.rest_0_), channel_id=1, source_target_pairs={{0,2},{1,3},{2,4},{3,5},{4,6},{5,7},{6,0},{7,1},{8,10},{9,11},{10,... | collective-permute-start | bytes 430088 | tf_op jit(solution)/shard_map/ppermute | solution.py:437
  20.9 18.5 %collective-permute-start.2 = (bf16[112,640]{1,0:T(8,128)(2,1)S(1)}, bf16[112,640]{1,0:T(8,128)(2,1)S(1)}, u32[]{:S(2)}, u32[]{:S(2)}) collective-permute-start(bf16[112,640]{1,0:T(8,128)(2,1)S(1)} %pair.1.after_ref.rest_0_), channel_id=1, source_target_pairs={{0,1},{1,2},{2,3},{3,4},{4,5},{5,6},{6,7},{7,0},{8,9},{9,10},{10,1... | collective-permute-start | bytes 430088 | tf_op jit(solution)/shard_map/ppermute | solution.py:437
  26.8 12.5 %copy-start = (bf16[768,384]{1,0:T(8,128)(2,1)S(1)}, bf16[768,384]{1,0:T(8,128)(2,1)}, u32[]{:S(2)}) copy-start(bf16[768,384]{1,0:T(8,128)(2,1)} %constant.7.clone.lift_ref) | copy-start | bytes 1769476
  26.8 12.5 %copy-start.1 = (bf16[384,768]{1,0:T(8,128)(2,1)S(1)}, bf16[384,768]{1,0:T(8,128)(2,1)}, u32[]{:S(2)}) copy-start(bf16[384,768]{1,0:T(8,128)(2,1)} %constant.6.clone.sel_ref) | copy-start | bytes 1769476
  26.8 12.6 %copy-start.5 = (f32[8,384]{1,0:T(8,128)S(1)}, f32[8,384]{1,0:T(8,128)}, u32[]{:S(2)}) copy-start(f32[8,384]{1,0:T(8,128)} %constant.8.clone.inc_ref) | copy-start | bytes 36868
  26.8 12.6 %copy-start.6 = (s32[1,192,1]{1,2,0:T(1,128)S(1)}, s32[1,192,1]{1,2,0:T(1,128)}, u32[]{:S(2)}) copy-start(s32[1,192,1]{1,2,0:T(1,128)} %param.21) | copy-start | bytes 2308
  26.8 12.6 %copy-start.7 = (s32[1,192]{1,0:T(1,128)S(1)}, s32[1,192]{1,0:T(1,128)}, u32[]{:S(2)}) copy-start(s32[1,192]{1,0:T(1,128)} %far_ref.1) | copy-start | bytes 2308
  26.8 12.6 %copy-start.8 = (s32[1,192]{1,0:T(1,128)S(1)}, s32[1,192]{1,0:T(1,128)}, u32[]{:S(2)}) copy-start(s32[1,192]{1,0:T(1,128)} %near_ref.1) | copy-start | bytes 2308
  26.8 12.6 %copy-start.9 = (s32[1,192]{1,0:T(1,128)S(1)}, s32[1,192]{1,0:T(1,128)}, u32[]{:S(2)}) copy-start(s32[1,192]{1,0:T(1,128)} %cls_ref.1) | copy-start | bytes 2308
  26.8 12.6 %copy-start.10 = (f32[16]{0:T(128)S(1)}, f32[16]{0:T(128)}, u32[]{:S(2)}) copy-start(f32[16]{0:T(128)} %param.20) | copy-start | bytes 196
  26.8 14.1 %copy-start.4 = (f32[1,15360]{1,0:T(1,128)S(1)}, f32[1,15360]{1,0:T(1,128)}, u32[]{:S(2)}) copy-start(f32[1,15360]{1,0:T(1,128)} %param.16) | copy-start | bytes 184324
  26.8 14.0 %all-to-all-start.1 = ((f32[32,8,128]{2,1,0:T(8,128)}), f32[32,8,128]{2,1,0:T(8,128)S(1)}, u32[]{:S(2)}, u32[]{:S(2)}) async-start(f32[32,8,128]{2,1,0:T(8,128)} %bitcast.3), calls=%async_computation.1 | async-start | bytes 262144 | tf_op jit(solution)/shard_map/all_to_all | solution.py:445
  30.9 8.4 %collective-permute-start.4 = (bf16[56,640]{1,0:T(8,128)(2,1)S(1)}, bf16[56,640]{1,0:T(8,128)(2,1)S(1)}, u32[]{:S(2)}, u32[]{:S(2)}) collective-permute-start(bf16[56,640]{1,0:T(8,128)(2,1)S(1)} %get-tuple-element.7.own_ref.elem_ref), channel_id=1, source_target_pairs={{0,3},{1,4},{2,5},{3,6},{4,7},{5,0},{6,1},{7,2},{8,11},{9,12},{10,... | collective-permute-start | bytes 215048 | tf_op jit(solution)/shard_map/ppermute | solution.py:437
